TPU v7x, 128 devices: a whole 4x4x4 slice. The times are simulated.
128 devices in a mesh: hullx: 8 (over y, z_lo), hully: 16 (over z_hi, x, core).
Axes of the slice: x: 4, y: 4, z: 4 (z_hi: 2, z_lo: 2; z = z_hi * 2 + z_lo), core: 2. Of those that a mesh axis runs over, the one named last changes fastest.
Arguments:
- velocity: float32 [3, 128, 768, 128], P(None, 'hullx', 'hully'), may hold values from -6 to 6
- pressure: float32 [128, 768, 128], P('hullx', 'hully'), may hold values from -6 to 6
- mom_source: float32 [3, 128, 768, 128], P(None, 'hullx', 'hully'), may hold values from -6 to 6
- mom_diag: float32 [128, 768, 128], P('hullx', 'hully'), may hold values from 0.5 to 8
- press_diag: float32 [128, 768, 128], P('hullx', 'hully'), may hold values from 0.05 to 2
- agglomeration: int32 [128, 768, 128], P('hullx', 'hully'), may hold values from 0 to 32767, as said below
- coarse_blocks: float32 [256, 2, 128, 128], P('hully'), as said below
- coarse_columns: int32 [256, 2], P('hully'), may hold values from 0 to 255, as said below
- wake_cells: int32 [32768], P(('hullx', 'hully')), may hold values from 0 to 98303
- wake_sections: int32 [32768], P(('hullx', 'hully')), may hold values from 0 to 1023
- wake_weights: float32 [32768], P(('hullx', 'hully')), may hold values from 0 to 0.3
- chord: float32 [1024], P(('hullx', 'hully')), may hold values from 0.2 to 1
- radius: float32 [1024], P(('hullx', 'hully')), may hold values from 0.2 to 1
- influence: float32 [1024, 1024], P(('hullx', 'hully')), may hold values from -0.1875 to 0.1875
- resistance: float32 [1], replicated, may hold values from 0.2 to 1.2
- body_cells: int32 [65536], P(('hullx', 'hully')), may hold values from 0 to 98303
- body_sections: int32 [65536], P(('hullx', 'hully')), may hold values from 0 to 1023
- body_weights: float32 [65536], P(('hullx', 'hully')), may hold values from 0.5 to 2
Outputs:
- velocity_new: float32 [3, 128, 768, 128], P(None, 'hullx', 'hully')
- pressure_new: float32 [128, 768, 128], P('hullx', 'hully')
- section_force: float32 [1024], P(('hullx', 'hully'))
Inputs may be any that keep to these rules, and one draw needn't show every extreme that they name: The agglomeration of the cell (i, j, k) differs by at most 3 from ((i * 768 + j) * 128 + k) // 384. coarse_columns[r][0] = r and coarse_columns[r][1] is another block row. coarse_blocks[r][0] holds the diagonal block of block row r.
All inputs are finite; a program needn't handle non-finite values.
Results may differ from a plain program's by a relative error of at most 0.00011.
Values sent between devices are 32-bit elements; how exact they have to be, the bound alone decides.
No kernel may reach another device: no remote copies, remote signals or barrier semaphores. Data moves between devices by JAX's collectives and lax.ppermute only.
A program may use at most 128 MiB of HBM per device.

v0:
```python
import jax
import jax.numpy as jnp
from jax import lax
from jax.sharding import PartitionSpec as P

TRIM = 2


jacobi_weight = 0.8
trim_gain = 0.5
pressure_relax = 0.7


def extended(cells, sides, width):
    for axis, dim in sides:
        count = lax.axis_size(axis)
        ends = count - 1
        head = lax.slice_in_dim(cells, 0, width, axis=dim)
        tail = lax.slice_in_dim(cells, cells.shape[dim] - width, cells.shape[dim], axis=dim)
        cells = jnp.concatenate(
            [
                lax.ppermute(tail, axis, [(i, (i + 1) % count) for i in range(ends)]),
                cells,
                lax.ppermute(head, axis, [((i + 1) % count, i) for i in range(ends)]),
            ],
            axis=dim,
        )
    return cells


def neighbour_sum(padded):
    total = padded[..., 2:, 1:-1, 1:-1] + padded[..., :-2, 1:-1, 1:-1]
    total = total + padded[..., 1:-1, 2:, 1:-1] + padded[..., 1:-1, :-2, 1:-1]
    return total + padded[..., 1:-1, 1:-1, 2:] + padded[..., 1:-1, 1:-1, :-2]


def gradient(padded):
    along_x = 0.5 * (padded[2:, 1:-1, 1:-1] - padded[:-2, 1:-1, 1:-1])
    along_y = 0.5 * (padded[1:-1, 2:, 1:-1] - padded[1:-1, :-2, 1:-1])
    along_z = 0.5 * (padded[1:-1, 1:-1, 2:] - padded[1:-1, 1:-1, :-2])
    return jnp.stack([along_x, along_y, along_z])


def divergence(padded):
    total = 0.5 * (padded[0, 2:, 1:-1, 1:-1] - padded[0, :-2, 1:-1, 1:-1])
    total = total + 0.5 * (padded[1, 1:-1, 2:, 1:-1] - padded[1, 1:-1, :-2, 1:-1])
    return total + 0.5 * (padded[2, 1:-1, 1:-1, 2:] - padded[2, 1:-1, 1:-1, :-2])


def coarse_apply(blocks, columns, vector):
    pieces = vector.reshape(-1, 128)[columns]
    return jnp.einsum("rkij,rkj->ri", blocks, pieces, precision=lax.Precision.HIGHEST).reshape(-1)


def coarse_diagonal(blocks):
    identity = jnp.eye(128, dtype=jnp.float32)
    return jnp.sum(blocks[:, 0] * identity, axis=2).reshape(-1)


def scalar_rim(field):
    haloed = extended(field, (("hullx", 0), ("hully", 1)), 1)
    return jnp.pad(haloed, ((0, 0), (0, 0), (1, 1)))


def vector_rim(field):
    haloed = extended(field, (("hullx", 1), ("hully", 2)), 1)
    return jnp.pad(haloed, ((0, 0), (0, 0), (0, 0), (1, 1)))


def smooth(correction, target, denominator):
    applied = denominator * correction - neighbour_sum(scalar_rim(correction))
    return correction + jacobi_weight * (target - applied) / denominator


def window_tables(agglomeration, coarse_count, group):
    slabs = agglomeration.shape[0]
    run_length = agglomeration.shape[1] * agglomeration.shape[2]
    width = run_length // group + 8
    across = lax.axis_size("hully") * agglomeration.shape[1]
    slab_rows = lax.axis_index("hullx") * slabs + jnp.arange(slabs, dtype=jnp.int32)
    run_first = (
        slab_rows * across + lax.axis_index("hully") * agglomeration.shape[1]
    ) * agglomeration.shape[2]
    starts = jnp.clip(run_first // group - 3, 0, coarse_count - width)
    offsets = agglomeration.reshape(slabs, run_length) - starts[:, None]
    slots = jnp.arange(width, dtype=jnp.int32)
    onehot = (offsets[:, None, :] == slots[None, :, None]).astype(jnp.float32)
    window_index = starts[:, None] + slots[None, :]
    return (onehot, window_index)


def local(
    velocity,
    pressure,
    mom_source,
    mom_diag,
    press_diag,
    agglomeration,
    coarse_blocks,
    coarse_columns,
    wake_cells,
    wake_sections,
    wake_weights,
    chord,
    radius,
    influence,
    resistance,
    body_cells,
    body_sections,
    body_weights,
):
    devices = lax.axis_size("hullx") * lax.axis_size("hully")
    sections = chord.shape[0] * devices
    cell_count = pressure.size
    coarse_count = coarse_blocks.shape[0] * 128 * lax.axis_size("hully")
    group = cell_count * devices // coarse_count
    samples = velocity[0].reshape(-1)[wake_cells] * wake_weights
    partial_wake = jax.ops.segment_sum(samples, wake_sections, num_segments=sections)
    wake = lax.psum_scatter(partial_wake, ("hullx", "hully"), scatter_dimension=0, tiled=True)
    omega = jnp.ones((), jnp.float32)
    induced = jnp.zeros(chord.shape, jnp.float32)
    for step in range(TRIM):
        circulation = chord * (omega * radius - wake - induced)
        all_circulation = lax.all_gather(circulation, ("hullx", "hully"), axis=0, tiled=True)
        thrust = lax.psum(jnp.sum(circulation * radius), ("hullx", "hully")) / sections
        omega = omega + trim_gain * (resistance[0] - thrust)
        induced = jnp.dot(influence, all_circulation, precision=lax.Precision.HIGHEST)
    circulation = chord * (omega * radius - wake - induced)
    section_force = circulation * omega * radius
    all_force = lax.all_gather(section_force, ("hullx", "hully"), axis=0, tiled=True)
    body_force = jax.ops.segment_sum(
        body_weights * all_force[body_sections], body_cells, num_segments=cell_count
    ).reshape(pressure.shape)
    source = mom_source - gradient(scalar_rim(pressure))
    source = source.at[0].add(body_force)
    denominator = 6.0 + mom_diag
    predicted = velocity
    for step in range(2):
        predicted = (source + neighbour_sum(vector_rim(predicted))) / denominator
    target = -divergence(vector_rim(predicted))
    press_denominator = 6.0 + press_diag
    correction = jacobi_weight * target / press_denominator
    correction = smooth(correction, target, press_denominator)
    residual = target - (press_denominator * correction - neighbour_sum(scalar_rim(correction)))
    rescale = (cell_count * devices / coarse_count) ** (-0.5)
    onehot, window_index = window_tables(agglomeration, coarse_count, group)
    slab_sums = jnp.einsum(
        "xwr,xr->xw", onehot, residual.reshape(onehot.shape[0], -1), precision=lax.Precision.HIGHEST
    )
    partial_coarse = (
        jnp.zeros((coarse_count,), jnp.float32)
        .at[window_index.reshape(-1)]
        .add(slab_sums.reshape(-1))
    )
    owned_rows = lax.psum_scatter(partial_coarse, "hully", scatter_dimension=0, tiled=True)
    coarse_residual = lax.psum(owned_rows, "hullx") * rescale
    diagonal = coarse_diagonal(coarse_blocks)
    first = jacobi_weight * coarse_residual / diagonal
    first_whole = lax.all_gather(first, "hully", axis=0, tiled=True)
    second = (
        first
        + jacobi_weight
        * (coarse_residual - coarse_apply(coarse_blocks, coarse_columns, first_whole))
        / diagonal
    )
    second_whole = lax.all_gather(second, "hully", axis=0, tiled=True)
    windows = second_whole[window_index]
    lifted = jnp.einsum("xwr,xw->xr", onehot, windows, precision=lax.Precision.HIGHEST)
    correction = correction + lifted.reshape(correction.shape)
    for step in range(2):
        correction = smooth(correction, target, press_denominator)
    velocity_new = predicted - gradient(scalar_rim(correction))
    pressure_new = pressure + pressure_relax * correction
    return (velocity_new, pressure_new, section_force)


def solution(mesh):
    in_specs = (
        P(None, "hullx", "hully", None),
        P("hullx", "hully", None),
        P(None, "hullx", "hully", None),
        P("hullx", "hully", None),
        P("hullx", "hully", None),
        P("hullx", "hully", None),
        P("hully", None, None, None),
        P("hully", None),
        P(("hullx", "hully")),
        P(("hullx", "hully")),
        P(("hullx", "hully")),
        P(("hullx", "hully")),
        P(("hullx", "hully")),
        P(("hullx", "hully"), None),
        P(),
        P(("hullx", "hully")),
        P(("hullx", "hully")),
        P(("hullx", "hully")),
    )
    out_specs = (P(None, "hullx", "hully", None), P("hullx", "hully", None), P(("hullx", "hully")))
    return jax.shard_map(local, mesh=mesh, in_specs=in_specs, out_specs=out_specs, check_vma=False)
```

profile of v0, /device:TPU:72, one launch (start us, length us, event | category | flops | bytes accessed | tf_op | source)
XLA Modules:
  0.0 688.5 jit_solution(11230297219226235587)
XLA Ops:
  8.2 3.5 collective-permute-start.1
  18.5 4.1 collective-permute-start.4
  26.9 63.0 %all-reduce.12 = f32[1024]{0:T(1024)S(1)} all-reduce(f32[1024]{0:T(1024)S(1)} %scatter_custom_fusion), channel_id=2, replica_groups=mesh['hullx'=8,'hully'=16] {'hullx','hully'}, use_global_device_ids=true, to_apply=%region_1.0.clone | all-reduce | flops 1024 | bytes 8192
  91.4 62.7 %all-reduce.15 = (f32[1024]{0:T(1024)S(1)}, f32[]{:T(128)}) all-reduce(f32[1024]{0:T(1024)S(1)} %fusion.85, f32[]{:T(128)} %get-tuple-element.23), channel_id=1, replica_groups=mesh['hullx'=8,'hully'=16] {'hullx','hully'}, use_global_device_ids=true, to_apply=%add.9 | all-reduce | flops 1025 | bytes 8200
  155.7 63.9 %all-reduce.14 = (f32[1024]{0:T(1024)S(1)}, f32[]{:T(128)}) all-reduce(f32[1024]{0:T(1024)S(1)} %dynamic-update-slice.4, f32[]{:T(128)} %get-tuple-element.65), channel_id=1, replica_groups=mesh['hullx'=8,'hully'=16] {'hullx','hully'}, use_global_device_ids=true, to_apply=%add.10 | all-reduce | flops 1025 | bytes 8200
  220.7 3.6 collective-permute-start.2
  226.6 65.6 %all-reduce.11 = f32[1024]{0:T(1024)S(1)} all-reduce(f32[1024]{0:T(1024)S(1)} %dynamic-update-slice.5), channel_id=1, replica_groups=mesh['hullx'=8,'hully'=16] {'hullx','hully'}, use_global_device_ids=true, to_apply=%add.11 | all-reduce | flops 1024 | bytes 8192
  294.5 4.1 scatter_custom_fusion.1
  301.8 5.1 collective-permute-start.6
  309.1 6.6 collective-permute-done.7
  317.7 4.1 collective-permute-start.8
  324.1 4.9 collective-permute-done.9
  333.5 6.2 collective-permute-done.11
  343.6 3.9 collective-permute-start.13
  355.2 6.3 collective-permute-done.15
  365.0 3.9 collective-permute-start.17
  376.0 6.2 collective-permute-done.19
  385.0 3.9 collective-permute-start.21
  396.4 5.8 collective-permute-done.23
  402.9 4.7 fusion.1
  407.7 4.5 scatter_custom_fusion.2
  413.6 134.7 %all-reduce.18.cloned.1.call-done = f32[32768]{0:T(1024)} async-done(((f32[32768]{0:T(1024)}), f32[32768]{0:T(1024)}) %all-reduce.18.cloned.1.call-update) | async-done | bytes 131088
  549.0 17.5 %psum.23 = f32[2048]{0:T(1024)S(1)} all-reduce(f32[2048]{0:T(1024)S(1)} %dynamic-slice.9), channel_id=1, replica_groups=mesh['hullx'=8,'hully'=16] {'hullx'}, use_global_device_ids=true, to_apply=%region_9.10 | all-reduce | flops 2048 | bytes 16384 | tf_op jit(solution)/shard_map/psum | solution.py:156
  566.5 19.3 %all_gather.18 = f32[32768]{0:T(1024)S(1)} all-gather(f32[2048]{0:T(1024)S(1)} %bitcast_divide_fusion.1), channel_id=1, replica_groups=mesh['hullx'=8,'hully'=16] {'hully'}, dimensions={0}, use_global_device_ids=true | all-gather | bytes 139264 | tf_op jit(solution)/shard_map/all_gather | solution.py:159
  589.8 21.3 %all_gather.19 = f32[32768]{0:T(1024)S(1)} all-gather(f32[2048]{0:T(1024)S(1)} %fusion.81), channel_id=1, replica_groups=mesh['hullx'=8,'hully'=16] {'hully'}, dimensions={0}, use_global_device_ids=true | all-gather | bytes 139264 | tf_op jit(solution)/shard_map/all_gather | solution.py:166
  622.7 4.0 collective-permute-done.25
  631.1 6.2 collective-permute-done.27
  638.0 3.9 collective-permute-start.28
  643.9 4.7 collective-permute-done.29
  653.0 6.2 collective-permute-done.31
  662.6 3.9 collective-permute-start.33
  673.6 6.2 collective-permute-done.35
  (183 shorter events, 106.3 us)
Async XLA Ops:
  7.2 541.0 %all-reduce.18.cloned.1.call-start = ((), (), s32[]{:S(2)}) async-start(), calls=%async_computation | async-start | bytes 262144
  8.2 212.4 %collective-permute-start.1 = (f32[1,48,128]{2,1,0:T(8,128)S(1)}, f32[1,48,128]{2,1,0:T(8,128)S(1)}, u32[]{:S(2)}, u32[]{:S(2)}) collective-permute-start(f32[1,48,128]{2,1,0:T(8,128)S(1)} %get-tuple-element.64), channel_id=1, source_target_pairs={{0,16},{16,32},{32,48},{48,64},{64,80},{80,96},{96,112},{1,17},{17... | collective-permute-start | bytes 73736 | tf_op jit(solution)/shard_map/ppermute | solution.py:22
  11.7 208.9 %collective-permute-start = (f32[1,48,128]{2,1,0:T(8,128)S(1)}, f32[1,48,128]{2,1,0:T(8,128)S(1)}, u32[]{:S(2)}, u32[]{:S(2)}) collective-permute-start(f32[1,48,128]{2,1,0:T(8,128)S(1)} %get-tuple-element.63), channel_id=1, source_target_pairs={{16,0},{32,16},{48,32},{64,48},{80,64},{96,80},{112,96},{17,1},{33... | collective-permute-start | bytes 73736 | tf_op jit(solution)/shard_map/ppermute | solution.py:24
  15.9 284.7 %collective-permute-start.5 = (f32[3,1,48,128]{3,2,1,0:T(8,128)S(1)}, f32[3,1,48,128]{3,2,1,0:T(8,128)S(1)}, u32[]{:S(2)}, u32[]{:S(2)}) collective-permute-start(f32[3,1,48,128]{3,2,1,0:T(8,128)S(1)} %get-tuple-element.36), channel_id=1, source_target_pairs={{0,16},{16,32},{32,48},{48,64},{64,80},{80,96},{96,112},{1,17},{17... | collective-permute-start | bytes 221192 | tf_op jit(solution)/shard_map/ppermute | solution.py:22
  18.5 283.2 %collective-permute-start.4 = (f32[3,1,48,128]{3,2,1,0:T(8,128)S(1)}, f32[3,1,48,128]{3,2,1,0:T(8,128)S(1)}, u32[]{:S(2)}, u32[]{:S(2)}) collective-permute-start(f32[3,1,48,128]{3,2,1,0:T(8,128)S(1)} %get-tuple-element.35), channel_id=1, source_target_pairs={{16,0},{32,16},{48,32},{64,48},{80,64},{96,80},{112,96},{17,1},{33... | collective-permute-start | bytes 221192 | tf_op jit(solution)/shard_map/ppermute | solution.py:24
  220.7 77.9 %collective-permute-start.2 = (f32[18,1,128]{2,1,0:T(1,128)S(1)}, f32[18,1,128]{2,1,0:T(1,128)S(1)}, u32[]{:S(2)}, u32[]{:S(2)}) collective-permute-start(f32[18,1,128]{2,1,0:T(1,128)S(1)} %get-tuple-element.50), channel_id=1, source_target_pairs={{1,0},{2,1},{3,2},{4,3},{5,4},{6,5},{7,6},{8,7},{9,8},{10,9},{11,1... | collective-permute-start | bytes 27656 | tf_op jit(solution)/shard_map/ppermute | solution.py:24
  224.4 74.3 %collective-permute-start.3 = (f32[18,1,128]{2,1,0:T(1,128)S(1)}, f32[18,1,128]{2,1,0:T(1,128)S(1)}, u32[]{:S(2)}, u32[]{:S(2)}) collective-permute-start(f32[18,1,128]{2,1,0:T(1,128)S(1)} %get-tuple-element.49), channel_id=1, source_target_pairs={{0,1},{1,2},{2,3},{3,4},{4,5},{5,6},{6,7},{7,8},{8,9},{9,10},{10,1... | collective-permute-start | bytes 27656 | tf_op jit(solution)/shard_map/ppermute | solution.py:22
  301.8 7.3 %collective-permute-start.6 = (f32[3,18,1,128]{3,2,1,0:T(1,128)S(1)}, f32[3,18,1,128]{3,2,1,0:T(1,128)S(1)}, u32[]{:S(2)}, u32[]{:S(2)}) collective-permute-start(f32[3,18,1,128]{3,2,1,0:T(1,128)S(1)} %get-tuple-element.30), channel_id=1, source_target_pairs={{1,0},{2,1},{3,2},{4,3},{5,4},{6,5},{7,6},{8,7},{9,8},{10,9},{11,1... | collective-permute-start | bytes 82952 | tf_op jit(solution)/shard_map/ppermute | solution.py:24
  306.9 8.8 %collective-permute-start.7 = (f32[3,18,1,128]{3,2,1,0:T(1,128)S(1)}, f32[3,18,1,128]{3,2,1,0:T(1,128)S(1)}, u32[]{:S(2)}, u32[]{:S(2)}) collective-permute-start(f32[3,18,1,128]{3,2,1,0:T(1,128)S(1)} %get-tuple-element.29), channel_id=1, source_target_pairs={{0,1},{1,2},{2,3},{3,4},{4,5},{5,6},{6,7},{7,8},{8,9},{9,10},{10,1... | collective-permute-start | bytes 82952 | tf_op jit(solution)/shard_map/ppermute | solution.py:22
  317.7 6.4 collective-permute-start.8
  321.8 7.1 %collective-permute-start.9 = (f32[3,1,48,128]{3,2,1,0:T(8,128)S(1)}, f32[3,1,48,128]{3,2,1,0:T(8,128)S(1)}, u32[]{:S(2)}, u32[]{:S(2)}) collective-permute-start(f32[3,1,48,128]{3,2,1,0:T(8,128)S(1)} %get-tuple-element.33), channel_id=1, source_target_pairs={{0,16},{16,32},{32,48},{48,64},{64,80},{80,96},{96,112},{1,17},{17... | collective-permute-start | bytes 221192 | tf_op jit(solution)/shard_map/ppermute | solution.py:22
  329.0 4.5 collective-permute-start.10
  330.9 8.8 %collective-permute-start.11 = (f32[3,18,1,128]{3,2,1,0:T(1,128)S(1)}, f32[3,18,1,128]{3,2,1,0:T(1,128)S(1)}, u32[]{:S(2)}, u32[]{:S(2)}) collective-permute-start(f32[3,18,1,128]{3,2,1,0:T(1,128)S(1)} %get-tuple-element.27), channel_id=1, source_target_pairs={{0,1},{1,2},{2,3},{3,4},{4,5},{5,6},{6,7},{7,8},{8,9},{9,10},{10,1... | collective-permute-start | bytes 82952 | tf_op jit(solution)/shard_map/ppermute | solution.py:22
  341.7 6.2 collective-permute-start.12
  343.6 7.1 %collective-permute-start.13 = (f32[3,1,48,128]{3,2,1,0:T(8,128)S(1)}, f32[3,1,48,128]{3,2,1,0:T(8,128)S(1)}, u32[]{:S(2)}, u32[]{:S(2)}) collective-permute-start(f32[3,1,48,128]{3,2,1,0:T(8,128)S(1)} %get-tuple-element.31), channel_id=1, source_target_pairs={{0,16},{16,32},{32,48},{48,64},{64,80},{80,96},{96,112},{1,17},{17... | collective-permute-start | bytes 221192 | tf_op jit(solution)/shard_map/ppermute | solution.py:22
  352.7 8.8 %collective-permute-start.15 = (f32[3,18,1,128]{3,2,1,0:T(1,128)S(1)}, f32[3,18,1,128]{3,2,1,0:T(1,128)S(1)}, u32[]{:S(2)}, u32[]{:S(2)}) collective-permute-start(f32[3,18,1,128]{3,2,1,0:T(1,128)S(1)} %get-tuple-element.25), channel_id=1, source_target_pairs={{0,1},{1,2},{2,3},{3,4},{4,5},{5,6},{6,7},{7,8},{8,9},{9,10},{10,1... | collective-permute-start | bytes 82952 | tf_op jit(solution)/shard_map/ppermute | solution.py:22
  363.1 5.9 collective-permute-start.16
  365.0 6.6 collective-permute-start.17
  373.5 8.6 %collective-permute-start.19 = (f32[18,1,128]{2,1,0:T(1,128)S(1)}, f32[18,1,128]{2,1,0:T(1,128)S(1)}, u32[]{:S(2)}, u32[]{:S(2)}) collective-permute-start(f32[18,1,128]{2,1,0:T(1,128)S(1)} %get-tuple-element.47), channel_id=1, source_target_pairs={{0,1},{1,2},{2,3},{3,4},{4,5},{5,6},{6,7},{7,8},{8,9},{9,10},{10,1... | collective-permute-start | bytes 27656 | tf_op jit(solution)/shard_map/ppermute | solution.py:22
  383.0 6.4 collective-permute-start.20
  385.0 6.6 collective-permute-start.21
  391.7 4.8 collective-permute-start.22
  393.6 8.6 %collective-permute-start.23 = (f32[18,1,128]{2,1,0:T(1,128)S(1)}, f32[18,1,128]{2,1,0:T(1,128)S(1)}, u32[]{:S(2)}, u32[]{:S(2)}) collective-permute-start(f32[18,1,128]{2,1,0:T(1,128)S(1)} %get-tuple-element.45), channel_id=1, source_target_pairs={{0,1},{1,2},{2,3},{3,4},{4,5},{5,6},{6,7},{7,8},{8,9},{9,10},{10,1... | collective-permute-start | bytes 27656 | tf_op jit(solution)/shard_map/ppermute | solution.py:22
  616.9 5.9 collective-permute-start.24
  619.5 7.2 %collective-permute-start.25 = (f32[1,48,128]{2,1,0:T(8,128)S(1)}, f32[1,48,128]{2,1,0:T(8,128)S(1)}, u32[]{:S(2)}, u32[]{:S(2)}) collective-permute-start(f32[1,48,128]{2,1,0:T(8,128)S(1)} %get-tuple-element.55), channel_id=1, source_target_pairs={{0,16},{16,32},{32,48},{48,64},{64,80},{80,96},{96,112},{1,17},{17... | collective-permute-start | bytes 73736 | tf_op jit(solution)/shard_map/ppermute | solution.py:22
  628.7 8.6 %collective-permute-start.27 = (f32[18,1,128]{2,1,0:T(1,128)S(1)}, f32[18,1,128]{2,1,0:T(1,128)S(1)}, u32[]{:S(2)}, u32[]{:S(2)}) collective-permute-start(f32[18,1,128]{2,1,0:T(1,128)S(1)} %get-tuple-element.43), channel_id=1, source_target_pairs={{0,1},{1,2},{2,3},{3,4},{4,5},{5,6},{6,7},{7,8},{8,9},{9,10},{10,1... | collective-permute-start | bytes 27656 | tf_op jit(solution)/shard_map/ppermute | solution.py:22
  638.0 5.9 collective-permute-start.28
  642.0 6.6 collective-permute-start.29
  650.5 8.6 %collective-permute-start.31 = (f32[18,1,128]{2,1,0:T(1,128)S(1)}, f32[18,1,128]{2,1,0:T(1,128)S(1)}, u32[]{:S(2)}, u32[]{:S(2)}) collective-permute-start(f32[18,1,128]{2,1,0:T(1,128)S(1)} %get-tuple-element.41), channel_id=1, source_target_pairs={{0,1},{1,2},{2,3},{3,4},{4,5},{5,6},{6,7},{7,8},{8,9},{9,10},{10,1... | collective-permute-start | bytes 27656 | tf_op jit(solution)/shard_map/ppermute | solution.py:22
  660.7 5.8 collective-permute-start.32
  662.6 6.6 collective-permute-start.33
  671.2 8.6 %collective-permute-start.35 = (f32[18,1,128]{2,1,0:T(1,128)S(1)}, f32[18,1,128]{2,1,0:T(1,128)S(1)}, u32[]{:S(2)}, u32[]{:S(2)}) collective-permute-start(f32[18,1,128]{2,1,0:T(1,128)S(1)} %get-tuple-element.39), channel_id=1, source_target_pairs={{0,1},{1,2},{2,3},{3,4},{4,5},{5,6},{6,7},{7,8},{8,9},{9,10},{10,1... | collective-permute-start | bytes 27656 | tf_op jit(solution)/shard_map/ppermute | solution.py:22
  (24 other events, 1196.1 us)
Sparse Core Ops, SparseCore 0:
  412.4 135.8 all-reduce.17
where the time goes:
time: 690 us; the launch traced here: 689 us
  blocking collectives  313 us (45%)
  waiting for transfers between devices  209 us (30%)
  starting transfers between devices  98 us (14%)
  other arithmetic  24.9 us (4%)
  between operations  17.9 us (3%)
  local copies, waits for them, and re-layouts  13.8 us (2%)
  matrix products  11.9 us (2%)
    unnamed x4, blocking collectives  255 us
    unnamed x2, waiting for transfers between devices  135 us
    ppermute x18, waiting for transfers between devices, extended(): lax.ppermute(tail, axis, [(i, (i + 1) % count) for i in range(ends)])  73.4 us
    ppermute x18, starting transfers between devices, extended(): lax.ppermute(tail, axis, [(i, (i + 1) % count) for i in range(ends)])  49.9 us
    ppermute x18, starting transfers between devices, extended(): lax.ppermute(head, axis, [((i + 1) % count, i) for i in range(ends)])  48 us
    all_gather x1, blocking collectives, local(): second_whole = lax.all_gather(second, 'hully', axis=0, tiled=True)  21.3 us
    all_gather x1, blocking collectives, local(): first_whole = lax.all_gather(first, 'hully', axis=0, tiled=True)  19.3 us
    psum x1, blocking collectives, local(): coarse_residual = lax.psum(owned_rows, 'hullx') * rescale  17.5 us
  transfers between devices with their start and end apart: 37, of which 18 were waited for; matrix products, arithmetic and copies ran while one was open for 2% of the time, Pallas kernels for 0%

commit v1 on v0

v1 whole, which is shorter than its diff:
```python
import numpy as np
import jax
import jax.numpy as jnp
from jax import lax
from jax.experimental import pallas as pl
from jax.experimental.pallas import tpu as pltpu
from jax.sharding import PartitionSpec as P

HX, HY = 8, 16
CX, CY, CZ = 16, 48, 128
NSEC = 1024
BOTH = ("hullx", "hully")
F32, BF16, I32 = jnp.float32, jnp.bfloat16, jnp.int32
HIGH = lax.Precision.HIGHEST
YE = 64
EN = 9 * 512

VM = pl.BlockSpec(memory_space=pltpu.VMEM)
SM = pl.BlockSpec(memory_space=pltpu.SMEM)
PARAMS = pltpu.CompilerParams(vmem_limit_bytes=48 * 1024 * 1024)


def iota(shape, dim):
    return lax.broadcasted_iota(I32, shape, dim)


def split2(x):
    hi = x.astype(BF16)
    lo = (x - hi.astype(F32)).astype(BF16)
    return hi, lo


def split3(x):
    hi = x.astype(BF16)
    rest = x - hi.astype(F32)
    mid = rest.astype(BF16)
    lo = (rest - mid.astype(F32)).astype(BF16)
    return hi, mid, lo


def nt(a, b, precision=None):
    return lax.dot_general(a, b, (((1,), (1,)), ((), ())), precision=precision, preferred_element_type=F32)


def mm(a, b, precision=None):
    return lax.dot_general(a, b, (((1,), (0,)), ((), ())), precision=precision, preferred_element_type=F32)


def lane_row(column, start):
    spot = iota((8, 128), 1) == iota((8, 128), 0) + start
    return jnp.sum(jnp.where(spot, column, 0.0), axis=0, keepdims=True)


def total(x):
    return jnp.sum(jnp.sum(x, axis=1, keepdims=True), axis=0, keepdims=True)


def zdiff_parts(v):
    lane = iota(v.shape, 1)
    before = jnp.where(lane == 0, 0.0, pltpu.roll(v, 1, 1))
    after = jnp.where(lane == CZ - 1, 0.0, pltpu.roll(v, CZ - 1, 1))
    return before, after


def y_parts(v):
    return pltpu.roll(v, 1, 0), pltpu.roll(v, v.shape[0] - 1, 0)


def s_yz(v):
    a, b = y_parts(v)
    c, d = zdiff_parts(v)
    return (a + b) + (c + d)


def wake_kernel(ids, cols, v_ref, wc, ws, ww, chord, radius, ab, out, row):
    hx, hy = ids[0], ids[1]
    cells = wc[...]
    place = cells >> 7
    spot = (iota((768, 256), 0) == place).astype(BF16)
    picked = jnp.zeros((128, 256), F32)
    for part in split3(v_ref[0]):
        picked = picked + lax.dot_general(part, spot, (((0,), (0,)), ((), ())), preferred_element_type=F32)
    samples = jnp.sum(jnp.where(iota((128, 256), 0) == (cells & 127), picked, 0.0), axis=0, keepdims=True) * ww[...]
    sec = ws[...]
    high = jnp.where(iota((8, 256), 0) == (sec >> 7), samples, 0.0)
    low = (iota((128, 256), 0) == (sec & 127)).astype(F32)
    row[0:8, :] = nt(high, low, HIGH)
    crow = lane_row(chord[...], 8 * hy)
    rrow = lane_row(radius[...], 8 * hy)
    lane = iota((1, 128), 1)
    c0 = cols[2 * hx, 1].astype(F32)
    c1 = cols[2 * hx + 1, 1].astype(F32)
    colrow = jnp.where(lane == 0, c0, jnp.where(lane == 1, c1, 0.0))
    eye = iota((128, 128), 0) == iota((128, 128), 1)
    d0 = jnp.sum(jnp.where(eye, ab[0, 0], 0.0), axis=0, keepdims=True)
    d1 = jnp.sum(jnp.where(eye, ab[1, 0], 0.0), axis=0, keepdims=True)
    row[8:16, :] = jnp.concatenate([crow, rrow, colrow, d0, d1, jnp.zeros((3, 128), F32)], axis=0)
    out[...] = jnp.broadcast_to(row[...][None], out.shape)


def trim1_kernel(ids, recv, infl, out, state, cols, grouped):
    hy = ids[1]
    wake = jnp.sum(recv[:, 0:8, :], axis=0)
    rest = recv[:, 8:16, :]
    grouped[...] = jnp.sum(rest.reshape(HX, HY, 8, 128), axis=1)
    chord = grouped[:, 0, :]
    radius = grouped[:, 1, :]
    cols[...] = recv[:, 10, :]
    state[0] = wake
    state[1] = chord
    state[2] = radius
    circ = chord * (radius - wake)
    acc = infl[:, 0:128] * circ[0:1, :]
    for c in range(1, 8):
        acc = acc + infl[:, c * 128 : (c + 1) * 128] * circ[c : c + 1, :]
    row = lane_row(jnp.sum(acc, axis=1, keepdims=True), 8 * hy)
    out[...] = jnp.broadcast_to(row, out.shape)


def trim2_kernel(ids, res, recv, state, infl, out, force):
    hx, hy = ids[0], ids[1]
    induced = jnp.sum(recv[...].reshape(HX, HY, 128), axis=1)
    wake, chord, radius = state[0], state[1], state[2]
    circ = chord * (radius - wake)
    omega = 1.0 + 0.5 * (res[0] - total(circ * radius) * (1.0 / NSEC))
    circ = chord * (omega * radius - wake - induced)
    omega = omega + 0.5 * (res[0] - total(circ * radius) * (1.0 / NSEC))
    acc = infl[:, 0:128] * circ[0:1, :]
    for c in range(1, 8):
        acc = acc + infl[:, c * 128 : (c + 1) * 128] * circ[c : c + 1, :]
    induced2 = lane_row(jnp.sum(acc, axis=1, keepdims=True), 8 * hy)
    mine = (iota((8, 128), 0) == hx) & ((iota((8, 128), 1) >> 3) == hy)
    full = chord * (omega * radius - wake - induced2) * omega * radius
    row = jnp.sum(jnp.where(mine, full, 0.0), axis=0, keepdims=True)
    force[...] = row
    out[...] = jnp.broadcast_to(row, out.shape)


def own_s_yz(v, ylo, yhi):
    r = iota(v.shape, 0)
    up = jnp.where(r == 0, ylo, pltpu.roll(v, 1, 0))
    down = jnp.where(r == CY - 1, yhi, pltpu.roll(v, CY - 1, 0))
    c, d = zdiff_parts(v)
    return (up + down) + (c + d)


def sweep1_kernel(vel, pres, src, mdiag, xlo, xhi, ylo, yhi, pred, source, vext):
    for c in range(3):
        vext[c, 1 : CX + 1] = vel[c]
    vext[3, 1 : CX + 1] = pres[...]
    vext[:, 0:1] = xlo[...][:, None]
    vext[:, CX + 1 : CX + 2] = xhi[...][:, None]

    def body(x, carry):
        inv = 1.0 / (6.0 + mdiag[x])
        p = vext[3, x + 1]
        gx = 0.5 * (vext[3, x + 2] - vext[3, x])
        r = iota(p.shape, 0)
        up = jnp.where(r == 0, ylo[3, pl.ds(x, 1), :], pltpu.roll(p, 1, 0))
        down = jnp.where(r == CY - 1, yhi[3, pl.ds(x, 1), :], pltpu.roll(p, CY - 1, 0))
        before, after = zdiff_parts(p)
        grads = (gx, 0.5 * (down - up), 0.5 * (after - before))
        for c in range(3):
            s = src[c, x] - grads[c]
            source[c, x] = s
            v = vext[c, x + 1]
            around = vext[c, x] + vext[c, x + 2] + own_s_yz(v, ylo[c, pl.ds(x, 1), :], yhi[c, pl.ds(x, 1), :])
            pred[c, x] = (s + around) * inv
        return carry

    lax.fori_loop(0, CX, body, 0)


def sweep2_kernel(pred, source, mdiag, xlo, xhi, ylo, yhi, out, vext):
    for c in range(3):
        vext[c, 1 : CX + 1] = pred[c]
    vext[:, 0:1] = xlo[...][:, None]
    vext[:, CX + 1 : CX + 2] = xhi[...][:, None]

    def body(x, carry):
        inv = 1.0 / (6.0 + mdiag[x])
        for c in range(3):
            v = vext[c, x + 1]
            around = vext[c, x] + vext[c, x + 2] + own_s_yz(v, ylo[c, pl.ds(x, 1), :], yhi[c, pl.ds(x, 1), :])
            out[c, x] = (source[c, x] + around) * inv
        return carry

    lax.fori_loop(0, CX, body, 0)


def body_parts():
    return [(sx, sy) for sy in (0, -1, 1) for sx in (0, -1, 1)]


def body_kernel(
    ids, recv, ecell, esec, ewt, p0, p1, p2, invd, invp, pdiag, acode, cols, gfold,
    pred0, target, corr1, send,
    b, dp, pr0, corr0, acc,
):
    hx, hy = ids[0], ids[1]
    force = jnp.sum(recv[...].reshape(HX, HY, 128), axis=1)
    sec = esec[...].astype(I32)
    low = (iota((128, EN), 0) == (sec & 127)).astype(BF16)
    got = mm(jnp.concatenate(split3(force), axis=0), low)
    got = got[0:8] + got[8:16] + got[16:24]
    val = jnp.sum(jnp.where(iota((8, EN), 0) == (sec >> 7), got, 0.0), axis=0, keepdims=True) * ewt[...]
    cell = ecell[...].astype(I32)
    cz = cell & 127
    place = cell >> 7
    cx = (place * 43691) >> 21
    cy = place - 48 * cx
    zv = jnp.where(iota((128, EN), 0) == cz, val, 0.0)
    zh, zl = split2(zv)
    for k, (sx, sy) in enumerate(body_parts()):
        lanes = slice(k * 512, (k + 1) * 512)
        x, y = cx[:, lanes], cy[:, lanes]
        planes = CX if sx == 0 else 4
        first = {0: 4, -1: 0, 1: 20}[sx]
        x = x - 12 if sx < 0 else x
        inside = (x >= 0) & (x < planes)
        if sy == 0:
            r = jnp.where(inside, x * YE + y + 8, -1)
            rows = planes * YE
        else:
            y = y - 40 if sy < 0 else y
            inside = inside & (y >= 0) & (y < 8)
            r = jnp.where(inside, x * 8 + y, -1)
            rows = planes * 8
        spot = (iota((rows, 512), 0) == r).astype(BF16)
        part = nt(spot, zh[:, lanes]) + nt(spot, zl[:, lanes])
        if sy == 0:
            b[first : first + planes] = part.reshape(planes, YE, 128)
        else:
            at = 0 if sy < 0 else 56
            b[first : first + planes, at : at + 8] = b[first : first + planes, at : at + 8] + part.reshape(planes, 8, 128)

    def s1(p, carry):
        dp[p] = b[p] * invd[p]
        return carry

    lax.fori_loop(0, 24, s1, 0)

    def s2(p, carry):
        d = (b[p] + dp[p - 1] + dp[p + 1] + s_yz(dp[p])) * invd[p]
        pr0[p - 1] = p0[p - 1] + d
        return carry

    lax.fori_loop(1, 23, s2, 0)

    def s3(t, carry):
        ya, yb = y_parts(p1[t])
        za, zb = zdiff_parts(p2[t])
        tg = -0.5 * ((pr0[t + 2] - pr0[t]) + (yb - ya) + (zb - za))
        target[t] = tg
        corr0[t] = 0.8 * tg * invp[t]
        return carry

    lax.fori_loop(0, 20, s3, 0)

    def s4(c, carry):
        t = c + 1
        v = corr0[t]
        corr1[c] = 0.2 * v + 0.8 * (target[t] + corr0[t - 1] + corr0[t + 1] + s_yz(v)) * invp[t]
        return carry

    lax.fori_loop(0, 18, s4, 0)
    acc[...] = jnp.zeros(acc.shape, F32)

    def s5(x, carry):
        pred0[x] = pr0[x + 3, 8:56, :]
        v = corr1[x + 1]
        full = target[x + 2] + corr1[x] + corr1[x + 2] + s_yz(v)
        res = full[8:56] - (6.0 + pdiag[x]) * v[8:56]
        code = acode[x]
        parts = [jnp.where(code == float(d + 1), res, 0.0) for d in range(7)]
        stacked = jnp.concatenate(parts, axis=0)
        hi, lo = split2(stacked)
        both = jnp.concatenate([hi, lo], axis=1)
        pick = (iota((256, 128), 1) == x).astype(BF16)
        acc[...] += mm(both, pick)
        return carry

    lax.fori_loop(0, CX, s5, 0)
    window = mm(gfold[...], acc[...], HIGH) * float(384.0**-0.5)
    blank = jnp.zeros((32, 128), F32)
    spread = jnp.concatenate(
        [jnp.concatenate([window if j == q else blank for j in range(4)], axis=1) for q in range(4)], axis=0
    )
    m = iota((128, 1), 0)
    plane = 8 * (m & 15) + (m >> 4)
    c0 = cols[:, 0:1].astype(I32)
    c1 = cols[:, 1:2].astype(I32)
    lane = iota((128, 128), 1)
    wants = []
    for blk in (2 * plane, 2 * plane + 1, c0, c1):
        half = blk & 1
        pln = blk >> 1
        pln = pln - jnp.where((half == 0) & (hy == HY - 1), 1, 0) + jnp.where((half == 1) & (hy == 0), 1, 0)
        at = pln - CX * hx
        at = jnp.where((at >= 0) & (at < CX), at, -1)
        wants.append((lane == at).astype(F32))
    send[...] = nt(jnp.concatenate(wants, axis=1), spread, HIGH)


def coarse_kernel(ids, half, recv, ab, diag, place, fold, out):
    z = jnp.sum(recv[...].reshape(HX, HY, 128), axis=0)
    y = mm(z, place[...], HIGH)
    lane = iota((HY, 128), 1)
    hys = iota((HY, 128), 0)
    rows = []
    for q in range(4):
        slot = (lane + 4 + 128 * half[q] - 16 * hys) & 255
        a = jnp.where(slot < 16, y[:, (2 * q) * 128 : (2 * q + 1) * 128], 0.0)
        b = jnp.where((slot >= 16) & (slot < 24), y[:, (2 * q + 1) * 128 : (2 * q + 2) * 128], 0.0)
        rows.append(jnp.sum(a + b, axis=0, keepdims=True))
    res = jnp.concatenate(rows + [jnp.zeros((4, 128), F32)], axis=0)
    first = 0.8 * res / diag[...]
    seconds = []
    for i in range(2):
        applied = nt(first, ab[i, 0], HIGH)[i : i + 1] + nt(first, ab[i, 1], HIGH)[2 + i : 3 + i]
        seconds.append(first[i : i + 1] + 0.8 * (res[i : i + 1] - applied) / diag[i : i + 1, :])
    second = jnp.concatenate(seconds, axis=1)
    lane2 = iota((HY, 256), 1)
    slot = (lane2 + 4 - 16 * iota((HY, 256), 0)) & 255
    wide = jnp.broadcast_to(second, (HY, 256))
    d0 = jnp.where(slot < 16, wide, 0.0)
    d1 = jnp.where((slot >= 16) & (slot < 24), wide, 0.0)
    windows = mm(jnp.concatenate([d0, d1], axis=1), fold[...], HIGH)
    for i in range(HX):
        out[i * HY : (i + 1) * HY, :] = windows


def last_kernel(ids, recv, corr1, target, invp, acode, pred0, pred1, pred2, pres, glift, vel_out, pres_out, win, c2, s1, s2):
    hx, hy = ids[0], ids[1]
    for i in range(24):
        p = jnp.clip(CX * hx - 4 + i, 0, 127)
        m = (p & 7) * HY + (p >> 3)
        win[i : i + 1, :] = recv[pl.ds(m, 1), :]
    w = win[0:24, :]
    lane = iota((24, 128), 1)
    w = jnp.where((lane < 4) & (hy == 0), pltpu.roll(w, 1, 0), w)
    w = jnp.where((lane >= 20) & (lane < 24) & (hy == HY - 1), pltpu.roll(w, 23, 0), w)
    win[0:24, :] = w
    win[24:128, :] = jnp.zeros((104, 128), F32)
    wt = win[...].T
    win[...] = wt

    def lift(i, carry):
        column = jnp.sum(jnp.where(iota((32, 128), 1) == i + 1, win[0:32, :], 0.0), axis=1, keepdims=True)
        wide = jnp.broadcast_to(column, (32, 128))
        v = mm(glift[...], jnp.concatenate(split3(wide), axis=0))
        code = acode[i]
        lifted = jnp.zeros((YE, 128), F32)
        for d in range(7):
            lifted = jnp.where(code == float(d + 1), v[d * YE : (d + 1) * YE], lifted)
        c2[i] = corr1[i] + lifted
        return carry

    lax.fori_loop(0, 22, lift, 0)

    def sweep1(t, carry):
        v = c2[t + 1]
        s1[t] = 0.2 * v + 0.8 * (target[t] + c2[t] + c2[t + 2] + s_yz(v)) * invp[t]
        return carry

    lax.fori_loop(0, 20, sweep1, 0)

    def sweep2(c, carry):
        v = s1[c + 1]
        s2[c] = 0.2 * v + 0.8 * (target[c + 1] + s1[c] + s1[c + 2] + s_yz(v)) * invp[c + 1]
        return carry

    lax.fori_loop(0, 18, sweep2, 0)

    def finish(x, carry):
        v = s2[x + 1]
        ya, yb = y_parts(v)
        za, zb = zdiff_parts(v)
        vel_out[0, x] = pred0[x] - 0.5 * (s2[x + 2] - s2[x])[8:56]
        vel_out[1, x] = pred1[x] - 0.5 * (yb - ya)[8:56]
        vel_out[2, x] = pred2[x] - 0.5 * (zb - za)[8:56]
        pres_out[x] = pres[x] + 0.7 * v[8:56]
        return carry

    lax.fori_loop(0, CX, finish, 0)


def tables():
    y = np.arange(CY)
    gfold = np.zeros((32, 7 * CY), np.float32)
    for d in range(7):
        gfold[y // 3 + d + 1, d * CY + y] = 1.0
    glift = np.zeros((7 * YE, 96), np.float32)
    for d in range(7):
        for yy in range(YE):
            slot = (yy - 8) // 3 + d + 1
            if 0 <= slot < 32:
                for part in range(3):
                    glift[d * YE + yy, part * 32 + slot] = 1.0
    place = np.zeros((128, 1024), np.float32)
    lanes = np.arange(128)
    for q in range(4):
        s = (lanes + 4) % 16
        place[q * 32 + s, (2 * q) * 128 + lanes] = 1.0
        ok = s < 8
        place[q * 32 + 16 + s[ok], (2 * q + 1) * 128 + lanes[ok]] = 1.0
    fold = np.zeros((512, 128), np.float32)
    lanes = np.arange(256)
    s = (lanes + 4) % 16
    fold[lanes, s] = 1.0
    ok = s < 8
    fold[256 + lanes[ok], 16 + s[ok]] = 1.0
    return gfold, glift, place, fold


def shift(x, axis, by):
    n = HX if axis == "hullx" else HY
    return lax.ppermute(x, axis, [(i, i + by) for i in range(n) if 0 <= i + by < n])


def to_all(x):
    return lax.all_to_all(x, BOTH, 0, 0, tiled=True)


def shp(*dims, dtype=F32):
    return jax.ShapeDtypeStruct(dims, dtype)


def local(
    velocity, pressure, mom_source, mom_diag, press_diag, agglomeration, coarse_blocks, coarse_columns,
    wake_cells, wake_sections, wake_weights, chord, radius, influence, resistance,
    body_cells, body_sections, body_weights,
):
    hx, hy = lax.axis_index("hullx"), lax.axis_index("hully")
    ids = jnp.stack([hx, hy]).astype(I32)
    gfold, glift, place, fold = (jnp.asarray(t) for t in tables())
    ab = lax.dynamic_slice(coarse_blocks, (2 * hx, 0, 0, 0), (2, 2, 128, 128))

    payload = pl.pallas_call(
        wake_kernel,
        grid=(1,),
        out_shape=shp(128, 16, 128),
        in_specs=[SM, SM, pl.BlockSpec((1, 768, 128), lambda i: (0, 0, 0))] + [VM] * 6,
        out_specs=VM,
        scratch_shapes=[pltpu.VMEM((16, 128), F32)],
        compiler_params=PARAMS,
        name="wake",
    )(
        ids, coarse_columns, velocity.reshape(3, 768, 128), wake_cells[None], wake_sections[None], wake_weights[None],
        chord[:, None], radius[:, None], ab,
    )
    recv1 = to_all(payload)
    out1, state, cols = pl.pallas_call(
        trim1_kernel,
        out_shape=(shp(128, 128), shp(3, 8, 128), shp(128, 128)),
        in_specs=[SM, VM, VM],
        out_specs=(VM, VM, VM),
        scratch_shapes=[pltpu.VMEM((8, 8, 128), F32)],
        compiler_params=PARAMS,
        name="trim1",
    )(ids, recv1, influence)
    recv2 = to_all(out1[:, None, :])[:, 0, :]
    out2, force_row = pl.pallas_call(
        trim2_kernel,
        out_shape=(shp(128, 128), shp(1, 128)),
        in_specs=[SM, SM, VM, VM, VM],
        out_specs=(VM, VM),
        compiler_params=PARAMS,
        name="trim2",
    )(ids, resistance, recv2, state, influence)
    recv3 = to_all(out2[:, None, :])[:, 0, :]
    section_force = lax.dynamic_slice(force_row[0], (8 * hy,), (8,))

    def halo(f):
        return (
            shift(f[:, CX - 1], "hullx", 1), shift(f[:, 0], "hullx", -1),
            shift(f[:, :, CY - 1], "hully", 1), shift(f[:, :, 0], "hully", -1),
        )

    both = jnp.concatenate([velocity, pressure[None]], axis=0)
    pred1, source = pl.pallas_call(
        sweep1_kernel,
        out_shape=(shp(3, CX, CY, CZ), shp(3, CX, CY, CZ)),
        in_specs=[VM] * 8,
        out_specs=(VM, VM),
        scratch_shapes=[pltpu.VMEM((4, CX + 2, CY, CZ), F32)],
        compiler_params=PARAMS,
        name="sweep1",
    )(velocity, pressure, mom_source, mom_diag, *halo(both))
    free = pl.pallas_call(
        sweep2_kernel,
        out_shape=shp(3, CX, CY, CZ),
        in_specs=[VM] * 7,
        out_specs=VM,
        scratch_shapes=[pltpu.VMEM((3, CX + 2, CY, CZ), F32)],
        compiler_params=PARAMS,
        name="sweep2",
    )(pred1, source, mom_diag, *halo(pred1))

    def wide(fields, extra=None):
        tail = jnp.concatenate([f[CX - w :] for f, w in fields], axis=0)
        head = jnp.concatenate([f[:w] for f, w in fields], axis=0)
        rows = tail.shape[0] * CY
        tail, head = tail.reshape(rows, 128), head.reshape(rows, 128)
        if extra is not None:
            tail = jnp.concatenate([tail, extra], axis=0)
            head = jnp.concatenate([head, extra], axis=0)
        lo, hi = shift(tail, "hullx", 1), shift(head, "hullx", -1)
        lists = None if extra is None else [extra, lo[rows:], hi[rows:]]
        lo, hi = lo[:rows].reshape(-1, CY, 128), hi[:rows].reshape(-1, CY, 128)
        grown, at = [], 0
        for f, w in fields:
            grown.append(jnp.concatenate([lo[at : at + w], f, hi[at : at + w]], axis=0))
            at += w
        tail = jnp.concatenate([f[:, CY - 8 :] for f in grown], axis=0)
        head = jnp.concatenate([f[:, :8] for f in grown], axis=0)
        rows = tail.shape[0] * 8
        tail, head = tail.reshape(rows, 128), head.reshape(rows, 128)
        if extra is not None:
            tail = jnp.concatenate([tail] + lists, axis=0)
            head = jnp.concatenate([head] + lists, axis=0)
        lo, hi = shift(tail, "hully", 1), shift(head, "hully", -1)
        if extra is not None:
            n = extra.shape[0]
            for other in (lo, hi):
                lists = lists + [other[rows + i * n : rows + (i + 1) * n] for i in range(3)]
        lo, hi = lo[:rows].reshape(-1, 8, 128), hi[:rows].reshape(-1, 8, 128)
        out, at = [], 0
        for f in grown:
            out.append(jnp.concatenate([lo[at : at + f.shape[0]], f, hi[at : at + f.shape[0]]], axis=1))
            at += f.shape[0]
        return out, lists

    base = (
        (hx * CX + jnp.arange(CX, dtype=I32))[:, None] * 256 + (hy * CY + jnp.arange(CY, dtype=I32))[None, :] // 3
    )[:, :, None]
    code = (agglomeration - base + 4).astype(F32)
    entries = jnp.concatenate(
        [body_cells.astype(F32), body_sections.astype(F32), body_weights, jnp.zeros((512,), F32)]
    ).reshape(16, 128)
    (invd_e, invp_e, code_e), lists = wide(
        [(1.0 / (6.0 + mom_diag), 4), (1.0 / (6.0 + press_diag), 2), (code, 3)], entries
    )
    ecell, esec, ewt = (
        jnp.concatenate([l[4 * j : 4 * j + 4].reshape(1, 512) for l in lists], axis=1) for j in range(3)
    )
    (p0, p1, p2), _ = wide([(free[0], 3), (free[1], 2), (free[2], 2)])

    pred0, target, corr1, send = pl.pallas_call(
        body_kernel,
        out_shape=(shp(CX, CY, CZ), shp(20, YE, CZ), shp(18, YE, CZ), shp(128, 128)),
        in_specs=[SM] + [VM] * 13,
        out_specs=(VM,) * 4,
        scratch_shapes=[
            pltpu.VMEM((24, YE, CZ), F32),
            pltpu.VMEM((24, YE, CZ), F32),
            pltpu.VMEM((22, YE, CZ), F32),
            pltpu.VMEM((20, YE, CZ), F32),
            pltpu.VMEM((7 * CY, 128), F32),
        ],
        compiler_params=PARAMS,
        name="body",
    )(ids, recv3, ecell, esec, ewt, p0, p1, p2, invd_e, invp_e, press_diag, code, cols, gfold)

    recv4 = to_all(send[:, None, :])[:, 0, :]
    (corr1_e,), _ = wide([(corr1[1 : CX + 1, 8:56], 3)])

    mine = lax.dynamic_slice(coarse_columns, (2 * hx, 0), (2, 2))[:, 1]
    half = jnp.concatenate([jnp.array([0, 1], I32), mine & 1])
    diags = [lax.dynamic_slice(recv1, (hx * HY + hy, 11, 0), (1, 2, 128))[0]]
    for i in range(2):
        pln = mine[i] >> 1
        diags.append(lax.dynamic_slice(recv1, ((pln & 7) * HY + (pln >> 3), 11 + (mine[i] & 1), 0), (1, 1, 128))[0])
    diag = jnp.concatenate(diags + [jnp.ones((4, 128), F32)], axis=0)
    out5 = pl.pallas_call(
        coarse_kernel,
        out_shape=shp(128, 128),
        in_specs=[SM, SM] + [VM] * 5,
        out_specs=VM,
        compiler_params=PARAMS,
        name="coarse",
    )(ids, half, recv4, ab, diag, place, fold)
    recv5 = to_all(out5[:, None, :])[:, 0, :]

    vel_new, pres_new = pl.pallas_call(
        last_kernel,
        out_shape=(shp(3, CX, CY, CZ), shp(CX, CY, CZ)),
        in_specs=[SM] + [VM] * 10,
        out_specs=(VM, VM),
        scratch_shapes=[
            pltpu.VMEM((128, 128), F32),
            pltpu.VMEM((22, YE, CZ), F32),
            pltpu.VMEM((20, YE, CZ), F32),
            pltpu.VMEM((18, YE, CZ), F32),
        ],
        compiler_params=PARAMS,
        name="last",
    )(ids, recv5, corr1_e, target, invp_e, code_e, pred0, free[1], free[2], pressure, glift.astype(BF16))
    return vel_new, pres_new, section_force


def solution(mesh):
    fine = P("hullx", "hully", None)
    vector = P(None, "hullx", "hully", None)
    flat = P(BOTH)
    in_specs = (
        vector, fine, vector, fine, fine, fine,
        P("hully", None, None, None), P("hully", None),
        flat, flat, flat, flat, flat, P(BOTH, None), P(), flat, flat, flat,
    )
    return jax.shard_map(local, mesh=mesh, in_specs=in_specs, out_specs=(vector, fine, flat), check_vma=False)
```

time: 690 us -> 278 us (0.40)
  the two profiles are of different devices: /device:TPU:72 before, /device:TPU:1 now
where the time goes in v1:
time: 278 us; the launch traced here: 275 us
  starting transfers between devices  106 us (38%)
  local copies, waits for them, and re-layouts  83.3 us (30%)
  Pallas kernels  35.3 us (13%)
  waiting for transfers between devices  31 us (11%)
  other arithmetic  15.1 us (5%)
  between operations  4.87 us (2%)
    ppermute x20, starting transfers between devices, shift(): lax.ppermute(x, axis, [(i, i + by) for i in range(n) if 0 <= i + by < n])  55.8 us
    all_to_all x5, starting transfers between devices, to_all(): return lax.all_to_all(x, BOTH, 0, 0, tiled=True)  49.9 us
    unnamed x217, local copies, waits for them, and re-layouts  48.7 us
    all_to_all x5, waiting for transfers between devices, to_all(): return lax.all_to_all(x, BOTH, 0, 0, tiled=True)  26.9 us
    pallas_call x1, Pallas kernels, local(): pl.pallas_call(body_kernel, out_shape=(shp(CX, CY, CZ), shp(20, YE, CZ),...  13.3 us
    pallas_call x1, Pallas kernels, local(): pl.pallas_call(last_kernel, out_shape=(shp(3, CX, CY, CZ), shp(CX, CY, CZ...  12.2 us
    concatenate x6, other arithmetic, wide(): jnp.concatenate([lo[at:at + f.shape[0]], f, hi[at:at + f.shape[0]]], axis=1)  7.06 us
    concatenate x1, local copies, waits for them, and re-layouts, wide(): head = jnp.concatenate([head] + lists, axis=0)  6.12 us
  transfers between devices with their start and end apart: 25, of which 6 were waited for; matrix products, arithmetic and copies ran while one was open for 22% of the time, Pallas kernels for 3%

profile of v1, /device:TPU:1, one launch (start us, length us, event | category | flops | bytes accessed | tf_op | source)
XLA Modules:
  0.0 275.2 jit_solution(16656603909341481080)
XLA Ops:
  6.6 5.1 %collective-permute-start = (f32[448,128]{1,0:T(8,128)}, f32[448,128]{1,0:T(8,128)}, u32[]{:S(2)}, u32[]{:S(2)}) collective-permute-start(f32[448,128]{1,0:T(8,128)} %concatenate.113), channel_id=1, source_target_pairs={{0,16},{16,32},{32,48},{48,64},{64,80},{80,96},{96,112},{1,17},{17... | collective-permute-start | bytes 688136 | tf_op jit(solution)/shard_map/ppermute | solution.py:418
  17.8 10.3 %all-to-all-start = ((f32[128,16,128]{2,1,0:T(8,128)}), f32[128,16,128]{2,1,0:T(8,128)}, u32[]{:S(2)}, u32[]{:S(2)}) async-start(f32[128,16,128]{2,1,0:T(8,128)} %copy-done.8), calls=%async_computation | async-start | bytes 2097152 | tf_op jit(solution)/shard_map/all_to_all | solution.py:422
  29.3 3.2 %collective-permute-start.7 = (f32[4,16,128]{2,1,0:T(8,128)S(1)}, f32[4,16,128]{2,1,0:T(8,128)S(1)}, u32[]{:S(2)}, u32[]{:S(2)}) collective-permute-start(f32[4,16,128]{2,1,0:T(8,128)S(1)} %get-tuple-element.31), channel_id=1, source_target_pairs={{1,0},{2,1},{3,2},{4,3},{5,4},{6,5},{7,6},{8,7},{9,8},{10,9},{11,1... | collective-permute-start | bytes 98312 | tf_op jit(solution)/shard_map/ppermute | solution.py:418
  32.5 2.5 collective-permute-start.6
  35.1 3.4 %collective-permute-start.4 = (f32[4,48,128]{2,0,1:T(4,128)S(1)}, f32[4,48,128]{2,0,1:T(4,128)S(1)}, u32[]{:S(2)}, u32[]{:S(2)}) collective-permute-start(f32[4,48,128]{2,0,1:T(4,128)S(1)} %bitcast.208), channel_id=1, source_target_pairs={{0,16},{16,32},{32,48},{48,64},{64,80},{80,96},{96,112},{1,17},{17... | collective-permute-start | bytes 294920 | tf_op jit(solution)/shard_map/ppermute | solution.py:418
  42.3 3.4 %collective-permute-done.4 = f32[4,48,128]{2,0,1:T(4,128)S(1)} collective-permute-done((f32[4,48,128]{2,0,1:T(4,128)S(1)}, f32[4,48,128]{2,0,1:T(4,128)S(1)}, u32[]{:S(2)}, u32[]{:S(2)}) %collective-permute-start.4) | collective-permute-done | bytes 98336 | tf_op jit(solution)/shard_map/ppermute | solution.py:418
  46.4 2.2 sweep1.1
  51.3 4.1 %collective-permute-start.8 = (f32[3,48,128]{2,1,0:T(8,128)S(1)}, f32[3,48,128]{2,1,0:T(8,128)S(1)}, u32[]{:S(2)}, u32[]{:S(2)}) collective-permute-start(f32[3,48,128]{2,1,0:T(8,128)S(1)} %get-tuple-element.49), channel_id=1, source_target_pairs={{0,16},{16,32},{32,48},{48,64},{64,80},{80,96},{96,112},{1,17},{17... | collective-permute-start | bytes 221192 | tf_op jit(solution)/shard_map/ppermute | solution.py:418
  55.4 2.6 collective-permute-start.11
  58.0 3.0 %collective-permute-start.10 = (f32[3,16,128]{2,1,0:T(8,128)S(1)}, f32[3,16,128]{2,1,0:T(8,128)S(1)}, u32[]{:S(2)}, u32[]{:S(2)}) collective-permute-start(f32[3,16,128]{2,1,0:T(8,128)S(1)} %get-tuple-element.47), channel_id=1, source_target_pairs={{0,1},{1,2},{2,3},{3,4},{4,5},{5,6},{6,7},{7,8},{8,9},{9,10},{10,1... | collective-permute-start | bytes 73736 | tf_op jit(solution)/shard_map/ppermute | solution.py:418
  64.1 1.9 concatenate.115
  75.1 6.3 %collective-permute-start.12 = (f32[336,128]{1,0:T(8,128)}, f32[336,128]{1,0:T(8,128)}, u32[]{:S(2)}, u32[]{:S(2)}) collective-permute-start(f32[336,128]{1,0:T(8,128)} %bitcast.67), channel_id=1, source_target_pairs={{0,16},{16,32},{32,48},{48,64},{64,80},{80,96},{96,112},{1,17},{17... | collective-permute-start | bytes 516104 | tf_op jit(solution)/shard_map/ppermute | solution.py:418
  87.8 6.1 %concatenate.122 = f32[576,128]{1,0:T(8,128)} concatenate(f32[528,128]{1,0:T(8,128)} %get-tuple-element.29, f32[4,128]{1,0:T(4,128)} %copy-done.79, f32[4,128]{1,0:T(4,128)} %copy-done.81, f32[4,128]{1,0:T(4,128)S(1)} %bitcast.214, f32[4,128]{1,0:T(4,128)S(1)} %copy-done.78, f32[16,128]{1,0:T(8,128)} %slice.574, f32[16,128]{1,0:T(8,128)} %slice.575), dimensions={0} | concatenate | bytes 589824 | tf_op jit(solution)/shard_map/concatenate | solution.py:521
  93.9 6.1 %concatenate.120 = f32[576,128]{1,0:T(8,128)} concatenate(f32[528,128]{1,0:T(8,128)} %get-tuple-element.30, f32[4,128]{1,0:T(4,128)} %copy-done.79, f32[4,128]{1,0:T(4,128)} %copy-done.81, f32[4,128]{1,0:T(4,128)S(1)} %bitcast.215, f32[4,128]{1,0:T(4,128)S(1)} %copy-done.78, f32[16,128]{1,0:T(8,128)} %slice.574, f32[16,128]{1,0:T(8,128)} %slice.575), dimensions={0} | concatenate | bytes 589824 | tf_op jit(solution)/shard_map/concatenate | solution.py:520
  100.0 2.2 collective-permute-start.2
  102.2 2.1 collective-permute-start.3
  113.8 3.6 %collective-permute-start.14 = (f32[496,128]{1,0:T(8,128)S(1)}, f32[496,128]{1,0:T(8,128)S(1)}, u32[]{:S(2)}, u32[]{:S(2)}) collective-permute-start(f32[496,128]{1,0:T(8,128)S(1)} %get-tuple-element.35), channel_id=1, source_target_pairs={{0,1},{1,2},{2,3},{3,4},{4,5},{5,6},{6,7},{7,8},{8,9},{9,10},{10,1... | collective-permute-start | bytes 761864 | tf_op jit(solution)/shard_map/ppermute | solution.py:418
  117.4 1.9 collective-permute-start.15
  139.1 20.7 %all-to-all-start.1 = ((f32[128,1,128]{2,1,0:T(1,128)}), f32[128,1,128]{2,1,0:T(1,128)}, u32[]{:S(2)}, u32[]{:S(2)}) async-start(f32[128,1,128]{2,1,0:T(1,128)} %bitcast.171), calls=%async_computation.1 | async-start | bytes 131072 | tf_op jit(solution)/shard_map/all_to_all | solution.py:422
  161.1 8.5 %all-to-all-done.1 = f32[128,1,128]{2,1,0:T(1,128)} async-done(((f32[128,1,128]{2,1,0:T(1,128)}), f32[128,1,128]{2,1,0:T(1,128)}, u32[]{:S(2)}, u32[]{:S(2)}) %all-to-all-start.1) | async-done | bytes 65568 | tf_op jit(solution)/shard_map/all_to_all | solution.py:422
  172.7 4.9 %all-to-all-start.2 = ((f32[128,1,128]{2,1,0:T(1,128)}), f32[128,1,128]{2,1,0:T(1,128)}, u32[]{:S(2)}, u32[]{:S(2)}) async-start(f32[128,1,128]{2,1,0:T(1,128)} %bitcast.170), calls=%async_computation.2 | async-start | bytes 131072 | tf_op jit(solution)/shard_map/all_to_all | solution.py:422
  178.8 8.7 %all-to-all-done.2 = f32[128,1,128]{2,1,0:T(1,128)} async-done(((f32[128,1,128]{2,1,0:T(1,128)}), f32[128,1,128]{2,1,0:T(1,128)}, u32[]{:S(2)}, u32[]{:S(2)}) %all-to-all-start.2) | async-done | bytes 65568 | tf_op jit(solution)/shard_map/all_to_all | solution.py:422
  197.8 13.3 %body.1 = (f32[16,48,128]{2,1,0:T(8,128)S(1)}, f32[20,64,128]{2,1,0:T(8,128)S(1)}, f32[18,64,128]{2,1,0:T(8,128)S(1)}, f32[128,128]{1,0:T(8,128)S(1)}) custom-call(s32[2]{0:T(128)S(1)} %pad_add_fusion.ids, f32[128,128]{1,0:T(8,128)} %bitcast.14.recv, f32[1,4608]{1,0:T(1,128)S(1)} %copy-done.45, f32[1,4608]{1,0:T(1,128)S(1)} %copy-done.43, ...), custom_call_target="tpu_custom_call" | custom-call | tf_op jit(solution)/shard_map/body/pallas_call | solution.py:549
  213.2 4.0 %collective-permute-start.16 = (f32[144,128]{1,0:T(8,128)S(1)}, f32[144,128]{1,0:T(8,128)S(1)}, u32[]{:S(2)}, u32[]{:S(2)}) collective-permute-start(f32[144,128]{1,0:T(8,128)S(1)} %bitcast.209), channel_id=1, source_target_pairs={{0,16},{16,32},{32,48},{48,64},{64,80},{80,96},{96,112},{1,17},{17... | collective-permute-start | bytes 221192 | tf_op jit(solution)/shard_map/ppermute | solution.py:418
  218.1 5.1 %all-to-all-start.3 = ((f32[128,1,128]{2,1,0:T(1,128)}), f32[128,1,128]{2,1,0:T(1,128)S(1)}, u32[]{:S(2)}, u32[]{:S(2)}) async-start(f32[128,1,128]{2,1,0:T(1,128)} %bitcast.169), calls=%async_computation.3 | async-start | bytes 131072 | tf_op jit(solution)/shard_map/all_to_all | solution.py:422
  224.8 3.5 %collective-permute-start.18 = (f32[176,128]{1,0:T(8,128)}, f32[176,128]{1,0:T(8,128)}, u32[]{:S(2)}, u32[]{:S(2)}) collective-permute-start(f32[176,128]{1,0:T(8,128)} %get-tuple-element.54), channel_id=1, source_target_pairs={{0,1},{1,2},{2,3},{3,4},{4,5},{5,6},{6,7},{7,8},{8,9},{9,10},{10,1... | collective-permute-start | bytes 270344 | tf_op jit(solution)/shard_map/ppermute | solution.py:418
  228.4 1.9 collective-permute-start.19
  230.9 2.1 all-to-all-done.3
  238.9 9.0 %all-to-all-start.4 = ((f32[128,1,128]{2,1,0:T(1,128)}), f32[128,1,128]{2,1,0:T(1,128)S(1)}, u32[]{:S(2)}, u32[]{:S(2)}) async-start(f32[128,1,128]{2,1,0:T(1,128)} %bitcast.168), calls=%async_computation.4 | async-start | bytes 131072 | tf_op jit(solution)/shard_map/all_to_all | solution.py:422
  247.9 2.0 pad_maximum_fusion.2.corr1
  249.9 7.7 %all-to-all-done.4 = f32[128,1,128]{2,1,0:T(1,128)S(1)} async-done(((f32[128,1,128]{2,1,0:T(1,128)}), f32[128,1,128]{2,1,0:T(1,128)S(1)}, u32[]{:S(2)}, u32[]{:S(2)}) %all-to-all-start.4) | async-done | bytes 65568 | tf_op jit(solution)/shard_map/all_to_all | solution.py:422
  263.0 12.2 %last.1 = (f32[3,16,48,128]{3,2,1,0:T(8,128)}, f32[16,48,128]{2,1,0:T(8,128)}) custom-call(s32[2]{0:T(128)S(1)} %pad_add_fusion.ids, f32[128,128]{1,0:T(8,128)S(1)} %bitcast.166, f32[22,64,128]{2,1,0:T(8,128)S(1)} %copy-done.17, f32[20,64,128]{2,1,0:T(8,128)S(1)} %copy-done.26, f32[20,64,128]{2,1,0:T(8,128)S(1)} %copy-done.5, f32[22,64,128]{2,1,0:T(8,128)S(1)} %copy-done.15, ...), custom_call_target="tpu_custom_call" | custom-call | tf_op jit(solution)/shard_map/last/pallas_call | solution.py:585
  (326 shorter events, 96.9 us)
Async XLA Ops:
  6.6 75.7 %collective-permute-start = (f32[448,128]{1,0:T(8,128)}, f32[448,128]{1,0:T(8,128)}, u32[]{:S(2)}, u32[]{:S(2)}) collective-permute-start(f32[448,128]{1,0:T(8,128)} %concatenate.113), channel_id=1, source_target_pairs={{0,16},{16,32},{32,48},{48,64},{64,80},{80,96},{96,112},{1,17},{17... | collective-permute-start | bytes 688136 | tf_op jit(solution)/shard_map/ppermute | solution.py:418
  17.8 117.2 %all-to-all-start = ((f32[128,16,128]{2,1,0:T(8,128)}), f32[128,16,128]{2,1,0:T(8,128)}, u32[]{:S(2)}, u32[]{:S(2)}) async-start(f32[128,16,128]{2,1,0:T(8,128)} %copy-done.8), calls=%async_computation | async-start | bytes 2097152 | tf_op jit(solution)/shard_map/all_to_all | solution.py:422
  29.3 17.1 %collective-permute-start.7 = (f32[4,16,128]{2,1,0:T(8,128)S(1)}, f32[4,16,128]{2,1,0:T(8,128)S(1)}, u32[]{:S(2)}, u32[]{:S(2)}) collective-permute-start(f32[4,16,128]{2,1,0:T(8,128)S(1)} %get-tuple-element.31), channel_id=1, source_target_pairs={{1,0},{2,1},{3,2},{4,3},{5,4},{6,5},{7,6},{8,7},{9,8},{10,9},{11,1... | collective-permute-start | bytes 98312 | tf_op jit(solution)/shard_map/ppermute | solution.py:418
  32.5 13.9 %collective-permute-start.6 = (f32[4,16,128]{2,1,0:T(8,128)S(1)}, f32[4,16,128]{2,1,0:T(8,128)S(1)}, u32[]{:S(2)}, u32[]{:S(2)}) collective-permute-start(f32[4,16,128]{2,1,0:T(8,128)S(1)} %get-tuple-element.32), channel_id=1, source_target_pairs={{0,1},{1,2},{2,3},{3,4},{4,5},{5,6},{6,7},{7,8},{8,9},{9,10},{10,1... | collective-permute-start | bytes 98312 | tf_op jit(solution)/shard_map/ppermute | solution.py:418
  35.1 10.6 %collective-permute-start.4 = (f32[4,48,128]{2,0,1:T(4,128)S(1)}, f32[4,48,128]{2,0,1:T(4,128)S(1)}, u32[]{:S(2)}, u32[]{:S(2)}) collective-permute-start(f32[4,48,128]{2,0,1:T(4,128)S(1)} %bitcast.208), channel_id=1, source_target_pairs={{0,16},{16,32},{32,48},{48,64},{64,80},{80,96},{96,112},{1,17},{17... | collective-permute-start | bytes 294920 | tf_op jit(solution)/shard_map/ppermute | solution.py:418
  38.6 7.8 %collective-permute-start.5 = (f32[4,48,128]{2,0,1:T(4,128)S(1)}, f32[4,48,128]{2,0,1:T(4,128)S(1)}, u32[]{:S(2)}, u32[]{:S(2)}) collective-permute-start(f32[4,48,128]{2,0,1:T(4,128)S(1)} %bitcast.207), channel_id=1, source_target_pairs={{16,0},{32,16},{48,32},{64,48},{80,64},{96,80},{112,96},{17,1},{33... | collective-permute-start | bytes 294920 | tf_op jit(solution)/shard_map/ppermute | solution.py:418
  48.6 19.3 %copy-start.13 = (f32[16,48,128]{2,1,0:T(8,128)S(1)}, f32[16,48,128]{2,1,0:T(8,128)}, u32[]{:S(2)}) copy-start(f32[16,48,128]{2,1,0:T(8,128)} %mdiag.3) | copy-start | bytes 1179652
  50.0 17.9 %collective-permute-start.9 = (f32[3,48,128]{2,1,0:T(8,128)S(1)}, f32[3,48,128]{2,1,0:T(8,128)S(1)}, u32[]{:S(2)}, u32[]{:S(2)}) collective-permute-start(f32[3,48,128]{2,1,0:T(8,128)S(1)} %get-tuple-element.48), channel_id=1, source_target_pairs={{16,0},{32,16},{48,32},{64,48},{80,64},{96,80},{112,96},{17,1},{33... | collective-permute-start | bytes 221192 | tf_op jit(solution)/shard_map/ppermute | solution.py:418
  51.3 16.6 %collective-permute-start.8 = (f32[3,48,128]{2,1,0:T(8,128)S(1)}, f32[3,48,128]{2,1,0:T(8,128)S(1)}, u32[]{:S(2)}, u32[]{:S(2)}) collective-permute-start(f32[3,48,128]{2,1,0:T(8,128)S(1)} %get-tuple-element.49), channel_id=1, source_target_pairs={{0,16},{16,32},{32,48},{48,64},{64,80},{80,96},{96,112},{1,17},{17... | collective-permute-start | bytes 221192 | tf_op jit(solution)/shard_map/ppermute | solution.py:418
  55.4 11.2 %collective-permute-start.11 = (f32[3,16,128]{2,1,0:T(8,128)S(1)}, f32[3,16,128]{2,1,0:T(8,128)S(1)}, u32[]{:S(2)}, u32[]{:S(2)}) collective-permute-start(f32[3,16,128]{2,1,0:T(8,128)S(1)} %get-tuple-element.46), channel_id=1, source_target_pairs={{1,0},{2,1},{3,2},{4,3},{5,4},{6,5},{7,6},{8,7},{9,8},{10,9},{11,1... | collective-permute-start | bytes 73736 | tf_op jit(solution)/shard_map/ppermute | solution.py:418
  58.0 9.9 %collective-permute-start.10 = (f32[3,16,128]{2,1,0:T(8,128)S(1)}, f32[3,16,128]{2,1,0:T(8,128)S(1)}, u32[]{:S(2)}, u32[]{:S(2)}) collective-permute-start(f32[3,16,128]{2,1,0:T(8,128)S(1)} %get-tuple-element.47), channel_id=1, source_target_pairs={{0,1},{1,2},{2,3},{3,4},{4,5},{5,6},{6,7},{7,8},{8,9},{9,10},{10,1... | collective-permute-start | bytes 73736 | tf_op jit(solution)/shard_map/ppermute | solution.py:418
  66.6 18.3 %collective-permute-start.1 = (f32[448,128]{1,0:T(8,128)}, f32[448,128]{1,0:T(8,128)S(1)}, u32[]{:S(2)}, u32[]{:S(2)}) collective-permute-start(f32[448,128]{1,0:T(8,128)} %concatenate.115), channel_id=1, source_target_pairs={{16,0},{32,16},{48,32},{64,48},{80,64},{96,80},{112,96},{17,1},{33... | collective-permute-start | bytes 688136 | tf_op jit(solution)/shard_map/ppermute | solution.py:418
  73.1 36.3 %collective-permute-start.13 = (f32[336,128]{1,0:T(8,128)}, f32[336,128]{1,0:T(8,128)}, u32[]{:S(2)}, u32[]{:S(2)}) collective-permute-start(f32[336,128]{1,0:T(8,128)} %bitcast.73), channel_id=1, source_target_pairs={{16,0},{32,16},{48,32},{64,48},{80,64},{96,80},{112,96},{17,1},{33... | collective-permute-start | bytes 516104 | tf_op jit(solution)/shard_map/ppermute | solution.py:418
  75.1 36.0 %collective-permute-start.12 = (f32[336,128]{1,0:T(8,128)}, f32[336,128]{1,0:T(8,128)}, u32[]{:S(2)}, u32[]{:S(2)}) collective-permute-start(f32[336,128]{1,0:T(8,128)} %bitcast.67), channel_id=1, source_target_pairs={{0,16},{16,32},{32,48},{48,64},{64,80},{80,96},{96,112},{1,17},{17... | collective-permute-start | bytes 516104 | tf_op jit(solution)/shard_map/ppermute | solution.py:418
  100.0 19.3 %collective-permute-start.2 = (f32[576,128]{1,0:T(8,128)}, f32[576,128]{1,0:T(8,128)S(1)}, u32[]{:S(2)}, u32[]{:S(2)}) collective-permute-start(f32[576,128]{1,0:T(8,128)} %concatenate.120), channel_id=1, source_target_pairs={{0,1},{1,2},{2,3},{3,4},{4,5},{5,6},{6,7},{7,8},{8,9},{9,10},{10,1... | collective-permute-start | bytes 884744 | tf_op jit(solution)/shard_map/ppermute | solution.py:418
  102.2 22.3 %collective-permute-start.3 = (f32[576,128]{1,0:T(8,128)}, f32[576,128]{1,0:T(8,128)S(1)}, u32[]{:S(2)}, u32[]{:S(2)}) collective-permute-start(f32[576,128]{1,0:T(8,128)} %concatenate.122), channel_id=1, source_target_pairs={{1,0},{2,1},{3,2},{4,3},{5,4},{6,5},{7,6},{8,7},{9,8},{10,9},{11,1... | collective-permute-start | bytes 884744 | tf_op jit(solution)/shard_map/ppermute | solution.py:418
  113.8 18.9 %collective-permute-start.14 = (f32[496,128]{1,0:T(8,128)S(1)}, f32[496,128]{1,0:T(8,128)S(1)}, u32[]{:S(2)}, u32[]{:S(2)}) collective-permute-start(f32[496,128]{1,0:T(8,128)S(1)} %get-tuple-element.35), channel_id=1, source_target_pairs={{0,1},{1,2},{2,3},{3,4},{4,5},{5,6},{6,7},{7,8},{8,9},{9,10},{10,1... | collective-permute-start | bytes 761864 | tf_op jit(solution)/shard_map/ppermute | solution.py:418
  117.4 15.4 %collective-permute-start.15 = (f32[496,128]{1,0:T(8,128)S(1)}, f32[496,128]{1,0:T(8,128)S(1)}, u32[]{:S(2)}, u32[]{:S(2)}) collective-permute-start(f32[496,128]{1,0:T(8,128)S(1)} %get-tuple-element.36), channel_id=1, source_target_pairs={{1,0},{2,1},{3,2},{4,3},{5,4},{6,5},{7,6},{8,7},{9,8},{10,9},{11,1... | collective-permute-start | bytes 761864 | tf_op jit(solution)/shard_map/ppermute | solution.py:418
  139.1 30.5 %all-to-all-start.1 = ((f32[128,1,128]{2,1,0:T(1,128)}), f32[128,1,128]{2,1,0:T(1,128)}, u32[]{:S(2)}, u32[]{:S(2)}) async-start(f32[128,1,128]{2,1,0:T(1,128)} %bitcast.171), calls=%async_computation.1 | async-start | bytes 131072 | tf_op jit(solution)/shard_map/all_to_all | solution.py:422
  172.7 14.8 %all-to-all-start.2 = ((f32[128,1,128]{2,1,0:T(1,128)}), f32[128,1,128]{2,1,0:T(1,128)}, u32[]{:S(2)}, u32[]{:S(2)}) async-start(f32[128,1,128]{2,1,0:T(1,128)} %bitcast.170), calls=%async_computation.2 | async-start | bytes 131072 | tf_op jit(solution)/shard_map/all_to_all | solution.py:422
  197.8 19.4 %copy-start.87 = (f32[2,128]{1,0:T(2,128)S(1)}, f32[2,128]{1,0:T(2,128)}, u32[]{:S(2)}) copy-start(f32[2,128]{1,0:T(2,128)} %fusion.14) | copy-start | bytes 3076
  197.8 19.4 %copy-start.90 = (f32[1,128]{1,0:T(1,128)S(1)}, f32[1,128]{1,0:T(1,128)}, u32[]{:S(2)}) copy-start(f32[1,128]{1,0:T(1,128)} %get-tuple-element.50) | copy-start | bytes 1540
  197.8 19.4 %copy-start.91 = (f32[1,128]{1,0:T(1,128)S(1)}, f32[1,128]{1,0:T(1,128)}, u32[]{:S(2)}) copy-start(f32[1,128]{1,0:T(1,128)} %get-tuple-element.51) | copy-start | bytes 1540
  197.8 19.5 %copy-start.94 = (f32[8]{0:T(128)S(1)}, f32[8]{0:T(128)}, u32[]{:S(2)}) copy-start(f32[8]{0:T(128)} %pad.16.clone) | copy-start | bytes 100
  211.9 11.3 %collective-permute-start.17 = (f32[144,128]{1,0:T(8,128)S(1)}, f32[144,128]{1,0:T(8,128)S(1)}, u32[]{:S(2)}, u32[]{:S(2)}) collective-permute-start(f32[144,128]{1,0:T(8,128)S(1)} %bitcast.210), channel_id=1, source_target_pairs={{16,0},{32,16},{48,32},{64,48},{80,64},{96,80},{112,96},{17,1},{33... | collective-permute-start | bytes 221192 | tf_op jit(solution)/shard_map/ppermute | solution.py:418
  213.2 10.0 %collective-permute-start.16 = (f32[144,128]{1,0:T(8,128)S(1)}, f32[144,128]{1,0:T(8,128)S(1)}, u32[]{:S(2)}, u32[]{:S(2)}) collective-permute-start(f32[144,128]{1,0:T(8,128)S(1)} %bitcast.209), channel_id=1, source_target_pairs={{0,16},{16,32},{32,48},{48,64},{64,80},{80,96},{96,112},{1,17},{17... | collective-permute-start | bytes 221192 | tf_op jit(solution)/shard_map/ppermute | solution.py:418
  218.1 14.8 %all-to-all-start.3 = ((f32[128,1,128]{2,1,0:T(1,128)}), f32[128,1,128]{2,1,0:T(1,128)S(1)}, u32[]{:S(2)}, u32[]{:S(2)}) async-start(f32[128,1,128]{2,1,0:T(1,128)} %bitcast.169), calls=%async_computation.3 | async-start | bytes 131072 | tf_op jit(solution)/shard_map/all_to_all | solution.py:422
  224.8 23.0 %collective-permute-start.18 = (f32[176,128]{1,0:T(8,128)}, f32[176,128]{1,0:T(8,128)}, u32[]{:S(2)}, u32[]{:S(2)}) collective-permute-start(f32[176,128]{1,0:T(8,128)} %get-tuple-element.54), channel_id=1, source_target_pairs={{0,1},{1,2},{2,3},{3,4},{4,5},{5,6},{6,7},{7,8},{8,9},{9,10},{10,1... | collective-permute-start | bytes 270344 | tf_op jit(solution)/shard_map/ppermute | solution.py:418
  228.4 19.5 %collective-permute-start.19 = (f32[176,128]{1,0:T(8,128)}, f32[176,128]{1,0:T(8,128)}, u32[]{:S(2)}, u32[]{:S(2)}) collective-permute-start(f32[176,128]{1,0:T(8,128)} %get-tuple-element.55), channel_id=1, source_target_pairs={{1,0},{2,1},{3,2},{4,3},{5,4},{6,5},{7,6},{8,7},{9,8},{10,9},{11,1... | collective-permute-start | bytes 270344 | tf_op jit(solution)/shard_map/ppermute | solution.py:418
  236.4 21.2 %copy-start.10 = (f32[16,48,128]{2,1,0:T(8,128)S(1)}, f32[16,48,128]{2,1,0:T(8,128)}, u32[]{:S(2)}) copy-start(f32[16,48,128]{2,1,0:T(8,128)} %pres.3) | copy-start | bytes 1179652
  238.9 18.8 %copy-start.36 = (bf16[448,96]{1,0:T(8,128)(2,1)S(1)}, bf16[448,96]{1,0:T(8,128)(2,1)}, u32[]{:S(2)}) copy-start(bf16[448,96]{1,0:T(8,128)(2,1)} %constant.87.glift) | copy-start | bytes 258052
  238.9 18.8 %all-to-all-start.4 = ((f32[128,1,128]{2,1,0:T(1,128)}), f32[128,1,128]{2,1,0:T(1,128)S(1)}, u32[]{:S(2)}, u32[]{:S(2)}) async-start(f32[128,1,128]{2,1,0:T(1,128)} %bitcast.168), calls=%async_computation.4 | async-start | bytes 131072 | tf_op jit(solution)/shard_map/all_to_all | solution.py:422
  (88 other events, 420.3 us)

commit v2 on v1

v2 whole, which is shorter than its diff:
```python
import numpy as np
import jax
import jax.numpy as jnp
from jax import lax
from jax.experimental import pallas as pl
from jax.experimental.pallas import tpu as pltpu
from jax.sharding import PartitionSpec as P

HX, HY = 8, 16
CX, CY, CZ = 16, 48, 128
NSEC = 1024
BOTH = ("hullx", "hully")
ROWS = (2, 4, 4)
F32, BF16, I32 = jnp.float32, jnp.bfloat16, jnp.int32
HIGH = lax.Precision.HIGHEST
YE = 64
EN = 9 * 512

VM = pl.BlockSpec(memory_space=pltpu.VMEM)
SM = pl.BlockSpec(memory_space=pltpu.SMEM)
AN = pl.BlockSpec(memory_space=pl.ANY)
PARAMS = pltpu.CompilerParams(vmem_limit_bytes=67000000)


def here():
    return lax.axis_index("hullx"), lax.axis_index("hully")


def iota(shape, dim):
    return lax.broadcasted_iota(I32, shape, dim)


def split2(x):
    hi = x.astype(BF16)
    lo = (x - hi.astype(F32)).astype(BF16)
    return hi, lo


def split3(x):
    hi = x.astype(BF16)
    rest = x - hi.astype(F32)
    mid = rest.astype(BF16)
    lo = (rest - mid.astype(F32)).astype(BF16)
    return hi, mid, lo


def nt(a, b, precision=None):
    return lax.dot_general(a, b, (((1,), (1,)), ((), ())), precision=precision, preferred_element_type=F32)


def mm(a, b, precision=None):
    return lax.dot_general(a, b, (((1,), (0,)), ((), ())), precision=precision, preferred_element_type=F32)


def lane_row(column, start):
    spot = iota((8, 128), 1) == iota((8, 128), 0) + start
    return jnp.sum(jnp.where(spot, column, 0.0), axis=0, keepdims=True)


def total(x):
    return jnp.sum(jnp.sum(x, axis=1, keepdims=True), axis=0, keepdims=True)


def zdiff_parts(v):
    lane = iota(v.shape, 1)
    before = jnp.where(lane == 0, 0.0, pltpu.roll(v, 1, 1))
    after = jnp.where(lane == CZ - 1, 0.0, pltpu.roll(v, CZ - 1, 1))
    return before, after


def y_parts(v):
    return pltpu.roll(v, 1, 0), pltpu.roll(v, v.shape[0] - 1, 0)


def s_yz(v):
    a, b = y_parts(v)
    c, d = zdiff_parts(v)
    return (a + b) + (c + d)


def wake_kernel(cols, chord, radius, vel, wc, ws, ww, blocks, keep, give, row, ab, sem):
    hx, hy = here()
    copies = [pltpu.make_async_copy(blocks.at[2 * hx + i, 0], ab.at[i], sem.at[i]) for i in range(2)]
    for c in copies:
        c.start()
    cells = wc[...]
    place = cells >> 7
    spot = (iota((768, 256), 0) == place).astype(BF16)
    picked = jnp.zeros((128, 256), F32)
    for part in split3(vel[0].reshape(768, 128)):
        picked = picked + lax.dot_general(part, spot, (((0,), (0,)), ((), ())), preferred_element_type=F32)
    samples = jnp.sum(jnp.where(iota((128, 256), 0) == (cells & 127), picked, 0.0), axis=0, keepdims=True) * ww[...]
    sec = ws[...]
    high = jnp.where(iota((8, 256), 0) == (sec >> 7), samples, 0.0)
    low = (iota((128, 256), 0) == (sec & 127)).astype(F32)
    row[...] = nt(high, low, HIGH)
    lane = iota((1, 128), 1)
    crow = rrow = jnp.zeros((1, 128), F32)
    for k in range(8):
        crow = jnp.where(lane == 8 * hy + k, chord[k], crow)
        rrow = jnp.where(lane == 8 * hy + k, radius[k], rrow)
    c0 = cols[1, 2 * hx].astype(F32)
    c1 = cols[1, 2 * hx + 1].astype(F32)
    colrow = jnp.where(lane == 0, c0, jnp.where(lane == 1, c1, 0.0))
    eye = iota((128, 128), 0) == iota((128, 128), 1)
    even = (hy & 1) == 0
    first, second = row[0:4, :], row[4:8, :]
    for c in copies:
        c.wait()
    d0 = jnp.sum(jnp.where(eye, ab[0], 0.0), axis=0, keepdims=True)
    d1 = jnp.sum(jnp.where(eye, ab[1], 0.0), axis=0, keepdims=True)
    keep[...] = jnp.concatenate([jnp.where(even, first, second), jnp.where(even, crow, rrow), d0, d1, colrow], axis=0)
    give[...] = jnp.concatenate(
        [jnp.where(even, second, first), jnp.where(even, rrow, crow), jnp.zeros((3, 128), F32)], axis=0
    )


def join_kernel(keep, got, out):
    out[...] = jnp.broadcast_to((keep[...] + got[...])[None], out.shape)


def trim1_kernel(recv, infl, out, state, table, grouped):
    hx, hy = here()
    by_core = recv[...].reshape(HX, HY // 2, 2, 8, 128)
    for core in range(2):
        grouped[core] = jnp.sum(by_core[:, :, core], axis=1)
    wake = jnp.concatenate([jnp.sum(grouped[0], axis=0)[0:4], jnp.sum(grouped[1], axis=0)[0:4]], axis=0)
    chord = grouped[0, :, 4, :]
    radius = grouped[1, :, 4, :]
    table[0] = recv[:, 7, :]
    table[1] = recv[:, 5, :]
    table[2] = recv[:, 6, :]
    state[0] = wake
    state[1] = chord
    state[2] = radius
    circ = chord * (radius - wake)
    acc = infl[:, 0:128] * circ[0:1, :]
    for c in range(1, 8):
        acc = acc + infl[:, c * 128 : (c + 1) * 128] * circ[c : c + 1, :]
    row = lane_row(jnp.sum(acc, axis=1, keepdims=True), 8 * hy)
    out[...] = jnp.broadcast_to(row[None], out.shape)


def trim2_kernel(res, recv, state, infl, out, force):
    hx, hy = here()
    induced = jnp.sum(recv[:, 0, :].reshape(HX, HY, 128), axis=1)
    wake, chord, radius = state[0], state[1], state[2]
    circ = chord * (radius - wake)
    omega = 1.0 + 0.5 * (res[0] - total(circ * radius) * (1.0 / NSEC))
    circ = chord * (omega * radius - wake - induced)
    omega = omega + 0.5 * (res[0] - total(circ * radius) * (1.0 / NSEC))
    acc = infl[:, 0:128] * circ[0:1, :]
    for c in range(1, 8):
        acc = acc + infl[:, c * 128 : (c + 1) * 128] * circ[c : c + 1, :]
    induced2 = lane_row(jnp.sum(acc, axis=1, keepdims=True), 8 * hy)
    mine = (iota((8, 128), 0) == hx) & ((iota((8, 128), 1) >> 3) == hy)
    full = chord * (omega * radius - wake - induced2) * omega * radius
    row = jnp.sum(jnp.where(mine, full, 0.0), axis=0, keepdims=True)
    force[...] = pltpu.roll(row, lax.rem(128 - 8 * hy, 128), 1)[:, 0:8]
    out[...] = jnp.broadcast_to(row[None], out.shape)


MID = slice(8, 8 + CY)


def run(pairs, sems):
    copies = [pltpu.make_async_copy(src, dst, sems.at[i]) for i, (src, dst) in enumerate(pairs)]
    for c in copies:
        c.start()
    return copies


def finish_all(copies):
    for c in copies:
        c.wait()


def codes_of(agg, hx, hy, y0):
    rows = agg.shape[1]
    plane = iota(agg.shape, 0) + CX * hx
    group = lax.div(iota((1, rows, 128), 1) + y0, 3) + 16 * hy
    return (agg - plane * 256 - group + 4).astype(F32)


def widen(low, middle, high):
    return jnp.concatenate([low, middle, high], axis=0)


def load_kernel(
    vel, src, pres, mdiag, pdiag, agg, bc, bs, bw,
    v, s, pr, invd, invp, codes, lists, tail, head,
    ag, ints, sems,
):
    hx, hy = here()
    copies = run(
        [(mdiag, invd), (pdiag, invp), (bc, ints.at[0]), (bs, ints.at[1]), (bw, lists.at[8:12]), (pres, pr), (vel, v), (agg, ag), (src, s)],
        sems,
    )
    lists[12:16, :] = jnp.zeros((4, 128), F32)
    finish_all(copies[:5])
    lists[0:4, :] = ints[0].astype(F32)
    lists[4:8, :] = ints[1].astype(F32)
    invd[...] = 1.0 / (6.0 + invd[...])
    invp[...] = 1.0 / (6.0 + invp[...])
    tail[4:8] = invd[CX - 4 : CX]
    head[4:8] = invd[0:4]
    tail[8:10] = invp[CX - 2 : CX]
    head[8:10] = invp[0:2]
    for out in (tail, head):
        out[10, 0:16] = lists[...]
        out[10, 16:48] = jnp.zeros((32, 128), F32)
    finish_all(copies[5:8])
    for x, out in ((CX - 1, tail), (0, head)):
        out[0:3] = v[:, x]
        out[3] = pr[x]
    codes[...] = codes_of(ag[...], hx, hy, 0)
    finish_all(copies[8:])


def packy_kernel(v, s, pr, invd, invp, codes, lists, xlo, xhi, token, tail_a, head_a, tail_b, head_b):
    for row, a, out in ((CY - 8, tail_a, tail_b), (0, head_a, head_b)):
        rows = slice(row, row + 8)
        for c in range(3):
            a[CX * c : CX * c + CX] = v[c, :, rows, :]
            a[48 + CX * c : 64 + CX * c] = s[c, :, rows, :]
        for k, f in enumerate((pr, invd, invp, codes)):
            out[CX * k : CX * k + CX] = f[:, rows, :]
        out[64:74] = xlo[0:10, rows, :]
        out[74:84] = xhi[0:10, rows, :]
        for j in range(2):
            part = slice(8 * j, 8 * j + 8)
            out[84 + j] = lists[part, :]
            out[86 + j] = xlo[10, part, :]
            out[88 + j] = xhi[10, part, :]


def sweep1_kernel(
    vel, src, pres, invd_own, invp_own, codes_own, yalo, yahi, ylo, yhi, xlo, xhi, token,
    pred, source, invd, invp, codes, tail, head,
    v,
):
    for n, (side, at) in enumerate(((xlo, 64), (xhi, 74))):
        for k in range(4):
            v[k, (CX + 1) * n] = widen(ylo[at + k], side[k], yhi[at + k])
        for k in range(4):
            invd[20 * n + k] = widen(ylo[at + 4 + k], side[4 + k], yhi[at + 4 + k])
        for k in range(2):
            invp[18 * n + k] = widen(ylo[at + 8 + k], side[8 + k], yhi[at + 8 + k])

    def grow(x, carry):
        for k in range(3):
            v[k, x + 1] = widen(yalo[CX * k + x], vel[k, x], yahi[CX * k + x])
        v[3, x + 1] = widen(ylo[x], pres[x], yhi[x])
        invd[x + 4] = widen(ylo[16 + x], invd_own[x], yhi[16 + x])
        invp[x + 2] = widen(ylo[32 + x], invp_own[x], yhi[32 + x])
        codes[x] = widen(ylo[48 + x], codes_own[x], yhi[48 + x])
        return carry

    lax.fori_loop(0, CX, grow, 0, unroll=2)

    def body(x, carry):
        inv = invd[x + 4]
        p = v[3, x + 1]
        ya, yb = y_parts(p)
        za, zb = zdiff_parts(p)
        for c, grad in enumerate((v[3, x + 2] - v[3, x], yb - ya, zb - za)):
            sc = widen(yalo[48 + CX * c + x], src[c, x], yahi[48 + CX * c + x]) - 0.5 * grad
            source[c, x] = sc
            pred[c, x] = (sc + v[c, x] + v[c, x + 2] + s_yz(v[c, x + 1])) * inv
        return carry

    lax.fori_loop(0, CX, body, 0, unroll=2)
    tail[0:3] = pred[:, CX - 1]
    head[0:3] = pred[:, 0]


def sweep2_kernel(pred, source, invd, xlo, xhi, token, out, tail, head):
    def at(x, before, here_, after):
        inv = invd[x + 4]
        for c in range(3):
            out[c, x] = (source[c, x] + before(c) + after(c) + s_yz(here_(c))) * inv

    def body(x, carry):
        at(x, lambda c: pred[c, x - 1], lambda c: pred[c, x], lambda c: pred[c, x + 1])
        return carry

    at(0, lambda c: xlo[c], lambda c: pred[c, 0], lambda c: pred[c, 1])
    lax.fori_loop(1, CX - 1, body, 0, unroll=2)
    at(CX - 1, lambda c: pred[c, CX - 2], lambda c: pred[c, CX - 1], lambda c: xhi[c])
    to = 0
    for c, w in enumerate((3, 2, 2)):
        tail[to : to + w] = out[c, CX - w : CX]
        head[to : to + w] = out[c, 0:w]
        to += w


def body_parts():
    return [(sx, sy) for sy in (0, -1, 1) for sx in (0, -1, 1)]


def force_kernel(recv, lists, ylo, yhi, x1lo, x1hi, b, listed, sems):
    listed[0:16, :] = lists[...]
    early = [(x1lo.at[10, 0:16], listed.at[16:32]), (x1hi.at[10, 0:16], listed.at[32:48])]
    for n, buf in enumerate((ylo, yhi)):
        for j in range(6):
            at = 48 + 48 * n + 8 * j
            early.append((buf.at[84 + j], listed.at[at : at + 8]))
    finish_all(run(early, sems))
    force = jnp.sum(recv[:, 0, :].reshape(HX, HY, 128), axis=1)

    def entries(j):
        rows = [listed[16 * k + 4 * j + i : 16 * k + 4 * j + i + 1, :] for k in range(9) for i in range(4)]
        return jnp.concatenate(rows, axis=1)

    ecell, esec, ewt = entries(0), entries(1), entries(2)
    sec = esec.astype(I32)
    low = (iota((128, EN), 0) == (sec & 127)).astype(BF16)
    got = mm(jnp.concatenate(split3(force), axis=0), low)
    got = got[0:8] + got[8:16] + got[16:24]
    val = jnp.sum(jnp.where(iota((8, EN), 0) == (sec >> 7), got, 0.0), axis=0, keepdims=True) * ewt
    cell = ecell.astype(I32)
    cz = cell & 127
    place = cell >> 7
    cx = (place * 43691) >> 21
    cy = place - 48 * cx
    zv = jnp.where(iota((128, EN), 0) == cz, val, 0.0)
    zh, zl = split2(zv)
    for k, (sx, sy) in enumerate(body_parts()):
        lanes = slice(k * 512, (k + 1) * 512)
        x, y = cx[:, lanes], cy[:, lanes]
        planes = CX if sx == 0 else 4
        first = {0: 4, -1: 0, 1: 20}[sx]
        x = x - 12 if sx < 0 else x
        inside = (x >= 0) & (x < planes)
        if sy == 0:
            r = jnp.where(inside, x * YE + y + 8, -1)
            rows = planes * YE
        else:
            y = y - 40 if sy < 0 else y
            inside = inside & (y >= 0) & (y < 8)
            r = jnp.where(inside, x * 8 + y, -1)
            rows = planes * 8
        spot = (iota((rows, 512), 0) == r).astype(BF16)
        part = nt(spot, zh[:, lanes]) + nt(spot, zl[:, lanes])
        if sy == 0:
            b[first : first + planes] = part.reshape(planes, YE, 128)
        else:
            at = 0 if sy < 0 else 56
            b[first : first + planes, at : at + 8] = b[first : first + planes, at : at + 8] + part.reshape(planes, 8, 128)


def three(n, w, fn):
    for i in range(w):
        fn(i, 0, i)

    def own(j, carry):
        fn(j + w, 1, j)
        return carry

    lax.fori_loop(0, CX, own, 0, unroll=4)
    for i in range(n - CX - w):
        fn(CX + w + i, 2, i)


def body_kernel(
    b, x3lo, x3hi, free, invd, invp, codes, table, gfold,
    pr0, target, corr1, tail, head, send,
    dp, corr0, acc,
):
    hx, hy = here()
    u = lambda c, at, part, j: (x3lo[at + j] if part == 0 else x3hi[at + j]) if part != 1 else free[c, j]

    def s1(p, part, j):
        dp[p] = b[p] * invd[p]

    def s2(i, part, j):
        p = i + 1
        pr0[i] = u(0, 0, part, j) + (b[p] + dp[p - 1] + dp[p + 1] + s_yz(dp[p])) * invd[p]

    def s3(t, part, j):
        ya, yb = y_parts(u(1, 3, part, j))
        za, zb = zdiff_parts(u(2, 5, part, j))
        tg = -0.5 * ((pr0[t + 2] - pr0[t]) + (yb - ya) + (zb - za))
        target[t] = tg
        corr0[t] = 0.8 * tg * invp[t]

    def s4(c, part, j):
        t = c + 1
        v = corr0[t]
        corr1[c] = 0.2 * v + 0.8 * (target[t] + corr0[t - 1] + corr0[t + 1] + s_yz(v)) * invp[t]

    three(24, 4, s1)
    three(22, 3, s2)
    three(20, 2, s3)
    three(18, 1, s4)

    def s5(g, carry):
        halves, picks = [], []
        for k in range(4):
            x = 4 * g + k
            v = corr1[x + 1]
            full = target[x + 2] + corr1[x] + corr1[x + 2] + s_yz(v)
            res = full[8:56] - v[8:56] / invp[x + 2, MID, :]
            code = codes[x, MID, :]
            hi, lo = split2(jnp.concatenate([jnp.where(code == float(n + 1), res, 0.0) for n in range(7)], axis=0))
            halves += [hi, lo]
            picks += [(iota((256, 128), 1) == x).astype(BF16)]
        part = mm(jnp.concatenate(halves, axis=1), jnp.concatenate(picks, axis=0))
        acc[...] = jnp.where(g == 0, part, acc[...] + part)
        return carry

    acc[...] = jnp.zeros(acc.shape, F32)
    lax.fori_loop(0, CX // 4, s5, 0)
    tail[0:3] = corr1[CX - 2 : CX + 1]
    tail[3:6] = codes[CX - 3 : CX]
    head[0:3] = corr1[1:4]
    head[3:6] = codes[0:3]
    window = mm(gfold[...], acc[...], HIGH) * float(384.0**-0.5)
    blank = jnp.zeros((32, 128), F32)
    spread = jnp.concatenate(
        [jnp.concatenate([window if j == q else blank for j in range(4)], axis=1) for q in range(4)], axis=0
    )
    m = iota((128, 1), 0)
    plane = 8 * (m & 15) + (m >> 4)
    c0 = table[0, :, 0:1].astype(I32)
    c1 = table[0, :, 1:2].astype(I32)
    lane = iota((128, 128), 1)
    wants = []
    for blk in (2 * plane, 2 * plane + 1, c0, c1):
        half = blk & 1
        pln = blk >> 1
        pln = pln - jnp.where((half == 0) & (hy == HY - 1), 1, 0) + jnp.where((half == 1) & (hy == 0), 1, 0)
        at = pln - CX * hx
        at = jnp.where((at >= 0) & (at < CX), at, -1)
        wants.append((lane == at).astype(F32))
    send[...] = jnp.broadcast_to(nt(jnp.concatenate(wants, axis=1), spread, HIGH)[:, None, :], send.shape)


def coarse_kernel(cols, recv, blocks, table, out, ab, diag, sem):
    hx, hy = here()
    copy = pltpu.make_async_copy(blocks.at[pl.ds(2 * hx, 2)], ab, sem)
    copy.start()
    c0, c1 = cols[1, 2 * hx], cols[1, 2 * hx + 1]
    half = (0, 1, c0 & 1, c1 & 1)
    m = hx * HY + hy
    diag[...] = jnp.ones((8, 128), F32)
    diag[0:1, :] = table[1, pl.ds(m, 1), :]
    diag[1:2, :] = table[2, pl.ds(m, 1), :]
    for i, c in enumerate((c0, c1)):
        pln = c >> 1
        diag[2 + i : 3 + i, :] = table[1 + (c & 1), pl.ds((pln & 7) * HY + (pln >> 3), 1), :]
    z = jnp.sum(recv[:, 0, :].reshape(HX, HY, 128), axis=0)
    r, c = iota((128, 1024), 0), iota((128, 1024), 1)
    later = (c >> 7) & 1
    m16 = (c + 4) & 15
    place = ((r >> 5) == (c >> 8)) & ((r & 31) == m16 + 16 * later) & ((later == 0) | (m16 < 8))
    y3 = mm(jnp.concatenate(split3(z), axis=0), place.astype(BF16))
    y = y3[0:16] + y3[16:32] + y3[32:48]
    lane = iota((HY, 128), 1)
    hys = iota((HY, 128), 0)
    rows = []
    for q in range(4):
        slot = (lane + 4 + 128 * half[q] - 16 * hys) & 255
        a = jnp.where(slot < 16, y[:, (2 * q) * 128 : (2 * q + 1) * 128], 0.0)
        b = jnp.where((slot >= 16) & (slot < 24), y[:, (2 * q + 1) * 128 : (2 * q + 2) * 128], 0.0)
        rows.append(jnp.sum(a + b, axis=0, keepdims=True))
    res = jnp.concatenate(rows + [jnp.zeros((4, 128), F32)], axis=0)
    first = 0.8 * res / diag[...]
    seconds = []
    copy.wait()
    for i in range(2):
        applied = nt(first, ab[i, 0], HIGH)[i : i + 1] + nt(first, ab[i, 1], HIGH)[2 + i : 3 + i]
        seconds.append(first[i : i + 1] + 0.8 * (res[i : i + 1] - applied) / diag[i : i + 1, :])
    second = jnp.concatenate(seconds, axis=1)
    lane2 = iota((HY, 256), 1)
    slot = (lane2 + 4 - 16 * iota((HY, 256), 0)) & 255
    wide = jnp.broadcast_to(second, (HY, 256))
    d0 = jnp.where(slot < 16, wide, 0.0)
    d1 = jnp.where((slot >= 16) & (slot < 24), wide, 0.0)
    r, c = iota((512, 128), 0), iota((512, 128), 1)
    later = r >> 8
    m16 = (r + 4) & 15
    fold = (c == m16 + 16 * later) & ((later == 0) | (m16 < 8))
    w3 = mm(jnp.concatenate(split3(jnp.concatenate([d0, d1], axis=1)), axis=0), fold.astype(BF16))
    windows = w3[0:16] + w3[16:32] + w3[32:48]
    for i in range(HX):
        out[i * HY : (i + 1) * HY, :] = windows


def last_kernel(
    recv, corr1, codes, xlo, xhi, target, invp, pr0, free, pres, glift,
    vel_out, pres_out,
    win, c2, s1, s2,
):
    hx, hy = here()
    for i in range(24):
        p = jnp.clip(CX * hx - 4 + i, 0, 127)
        m = (p & 7) * HY + (p >> 3)
        win[i : i + 1, :] = recv[pl.ds(m, 1), :]
    w = win[0:24, :]
    lane = iota((24, 128), 1)
    w = jnp.where((lane < 4) & (hy == 0), pltpu.roll(w, 1, 0), w)
    w = jnp.where((lane >= 20) & (lane < 24) & (hy == HY - 1), pltpu.roll(w, 23, 0), w)
    win[0:24, :] = w
    win[24:128, :] = jnp.zeros((104, 128), F32)
    wt = win[...].T
    win[...] = wt

    def lift(i, part, j):
        column = jnp.sum(jnp.where(iota((32, 128), 1) == i + 1, win[0:32, :], 0.0), axis=1, keepdims=True)
        wide = jnp.broadcast_to(column, (32, 128))
        v = mm(glift[...], jnp.concatenate(split3(wide), axis=0))
        side = (xlo, None, xhi)[part]
        code = codes[j] if part == 1 else side[3 + j]
        lifted = corr1[j + 1] if part == 1 else side[j]
        for n in range(7):
            lifted = jnp.where(code == float(n + 1), lifted + v[n * YE : (n + 1) * YE], lifted)
        c2[i] = lifted

    three(22, 3, lift)

    def sweep1(t, part, j):
        v = c2[t + 1]
        s1[t] = 0.2 * v + 0.8 * (target[t] + c2[t] + c2[t + 2] + s_yz(v)) * invp[t]

    def sweep2(c, part, j):
        v = s1[c + 1]
        s2[c] = 0.2 * v + 0.8 * (target[c + 1] + s1[c] + s1[c + 2] + s_yz(v)) * invp[c + 1]

    three(20, 2, sweep1)
    three(18, 1, sweep2)

    def finish(x, carry):
        v = s2[x + 1]
        ya, yb = y_parts(v)
        za, zb = zdiff_parts(v)
        vel_out[0, x] = pr0[x + 3, MID, :] - 0.5 * (s2[x + 2] - s2[x])[8:56]
        vel_out[1, x] = free[1, x, MID, :] - 0.5 * (yb - ya)[8:56]
        vel_out[2, x] = free[2, x, MID, :] - 0.5 * (zb - za)[8:56]
        pres_out[x] = pres[x] + 0.7 * v[8:56]
        return carry

    lax.fori_loop(0, CX, finish, 0, unroll=2)


def tables():
    y = np.arange(CY)
    gfold = np.zeros((32, 7 * CY), np.float32)
    for d in range(7):
        gfold[y // 3 + d + 1, d * CY + y] = 1.0
    glift = np.zeros((7 * YE, 96), np.float32)
    for d in range(7):
        for yy in range(YE):
            slot = (yy - 8) // 3 + d + 1
            if 0 <= slot < 32:
                for part in range(3):
                    glift[d * YE + yy, part * 32 + slot] = 1.0
    return gfold, glift


def shift(x, axis, by):
    n = HX if axis == "hullx" else HY
    return lax.ppermute(x, axis, [(i, i + by) for i in range(n) if 0 <= i + by < n])


def to_all(x):
    return lax.all_to_all(x, BOTH, 0, 0, tiled=True)


def pair(x):
    return lax.ppermute(x, "hully", [(i, i ^ 1) for i in range(HY)])


def fast(*dims, dtype=F32):
    return jax.ShapeDtypeStruct(dims, dtype)


def send(*dims, dtype=F32):
    return jax.ShapeDtypeStruct(dims, dtype)


def shp(*dims, dtype=F32):
    return jax.ShapeDtypeStruct(dims, dtype)


def local(
    velocity, pressure, mom_source, mom_diag, press_diag, agglomeration, coarse_blocks, coarse_columns,
    wake_cells, wake_sections, wake_weights, chord, radius, influence, resistance,
    body_cells, body_sections, body_weights,
):
    gfold, glift = (jnp.asarray(t) for t in tables())
    cols = coarse_columns.T
    block = lambda *n: pltpu.VMEM((*n, YE, CZ), F32)
    sems = lambda n: pltpu.SemaphoreType.DMA((n,))

    def call(kernel, name, outs, ins, scratch, args):
        many = isinstance(outs, tuple)
        return pl.pallas_call(
            kernel, out_shape=outs, in_specs=ins, out_specs=(VM,) * len(outs) if many else VM,
            scratch_shapes=scratch, compiler_params=PARAMS, name=name,
        )(*args)

    def slow(*arrays):
        return arrays

    v, src, pres, invd_own, invp_own, codes_own, lists, xt, xh = call(
        load_kernel, "load",
        (fast(3, CX, CY, CZ),) * 2 + (fast(CX, CY, CZ),) * 4 + (fast(16, 128),) + (send(11, CY, CZ),) * 2,
        [AN] * 9, [pltpu.VMEM((CX, CY, CZ), I32), pltpu.VMEM((2, 4, 128), I32), sems(9)],
        slow(velocity, mom_source, pressure, mom_diag, press_diag, agglomeration)
        + slow(*(a.reshape(4, 128) for a in (body_cells, body_sections, body_weights))),
    )
    x1lo, x1hi = shift(xt, "hullx", 1), shift(xh, "hullx", -1)

    keep, give = call(
        wake_kernel, "wake", (fast(8, 128), send(8, 128)), [SM, SM, SM, VM, VM, VM, VM, AN],
        [pltpu.VMEM((8, 128), F32), pltpu.VMEM((2, 128, 128), F32), sems(2)],
        (cols, chord, radius, v, wake_cells[None], wake_sections[None], wake_weights[None]) + slow(coarse_blocks),
    )
    payload = call(join_kernel, "join", send(128, 8, 128), [VM, VM], [], (keep, pair(give)))
    recv1 = to_all(payload)
    out1, state, table = call(
        trim1_kernel, "trim1", (send(128, ROWS[0], 128), fast(3, 8, 128), fast(3, 128, 128)), [VM, VM],
        [pltpu.VMEM((2, 8, 8, 128), F32)], (recv1,) + slow(influence),
    )
    recv2 = to_all(out1)

    yat, yah, yt, yh = call(
        packy_kernel, "packy", (send(96, 8, CZ),) * 2 + (send(90, 8, CZ),) * 2, [VM] * 9 + [AN], [],
        (v, src, pres, invd_own, invp_own, codes_own, lists, x1lo, x1hi, payload),
    )
    yalo, yahi = shift(yat, "hully", 1), shift(yah, "hully", -1)
    ylo, yhi = shift(yt, "hully", 1), shift(yh, "hully", -1)
    pred1, source, invd, invp, codes, xt, xh = call(
        sweep1_kernel, "sweep1",
        (fast(3, CX, YE, CZ),) * 2 + (fast(24, YE, CZ), fast(20, YE, CZ), fast(CX, YE, CZ)) + (send(3, YE, CZ),) * 2,
        [VM] * 13, [block(4, CX + 2)],
        (v, src, pres, invd_own, invp_own, codes_own, yalo, yahi, ylo, yhi, x1lo, x1hi, state),
    )
    x2lo, x2hi = shift(xt, "hullx", 1), shift(xh, "hullx", -1)

    out2, force = call(
        trim2_kernel, "trim2", (send(128, ROWS[1], 128), fast(1, 8)), [SM, VM, VM, VM], [],
        (resistance, recv2, state) + slow(influence),
    )
    recv3 = to_all(out2)
    free, xt, xh = call(
        sweep2_kernel, "sweep2", (fast(3, CX, YE, CZ),) + (send(7, YE, CZ),) * 2, [VM] * 6, [],
        (pred1, source, invd, x2lo, x2hi, force),
    )
    x3lo, x3hi = shift(xt, "hullx", 1), shift(xh, "hullx", -1)

    b = call(
        force_kernel, "force", fast(24, YE, CZ), [VM, VM] + [AN] * 4, [pltpu.VMEM((144, 128), F32), sems(14)],
        (recv3, lists, ylo, yhi, x1lo, x1hi),
    )
    pr0, target, corr1, ct, ch, out4 = call(
        body_kernel, "body",
        (fast(22, YE, CZ), fast(20, YE, CZ), fast(18, YE, CZ), send(6, YE, CZ), send(6, YE, CZ), send(128, ROWS[2], 128)),
        [VM] * 9, [block(24), block(20), pltpu.VMEM((7 * CY, 128), F32)],
        (b, x3lo, x3hi, free, invd, invp, codes, table) + slow(gfold),
    )
    recv4 = to_all(out4)
    cxlo, cxhi = shift(ct, "hullx", 1), shift(ch, "hullx", -1)
    out5 = call(
        coarse_kernel, "coarse", send(128, 128), [SM, VM, AN, VM],
        [pltpu.VMEM((2, 2, 128, 128), F32), pltpu.VMEM((8, 128), F32), pltpu.SemaphoreType.DMA],
        (cols, recv4) + slow(coarse_blocks) + (table,),
    )
    recv5 = to_all(out5[:, None, :])[:, 0, :]
    vel_new, pres_new = call(
        last_kernel, "last", (shp(3, CX, CY, CZ), shp(CX, CY, CZ)), [VM] * 11,
        [pltpu.VMEM((128, 128), F32), block(22), block(20), block(18)],
        (recv5, corr1, codes, cxlo, cxhi, target, invp, pr0, free, pres) + slow(glift.astype(BF16)),
    )
    section_force = force.reshape(8)
    return vel_new, pres_new, section_force


def solution(mesh):
    fine = P("hullx", "hully", None)
    vector = P(None, "hullx", "hully", None)
    flat = P(BOTH)
    in_specs = (
        vector, fine, vector, fine, fine, fine,
        P("hully", None, None, None), P("hully", None),
        flat, flat, flat, flat, flat, P(BOTH, None), P(), flat, flat, flat,
    )
    return jax.shard_map(local, mesh=mesh, in_specs=in_specs, out_specs=(vector, fine, flat), check_vma=False)
```

time: 278 us -> 166 us (0.60)
  local copies, waits for them, and re-layouts: 83.3 us -> 0.59 us
  Pallas kernels: 35.3 us -> 52.1 us
  starting transfers between devices: 106 us -> 90.5 us
  other arithmetic: 15.1 us -> 0 us
  waiting for transfers between devices: 31 us -> 20.3 us
  between operations: 4.87 us -> 1.53 us
    unnamed x217 -> x2, local copies, waits for them, and re-layouts: 48.7 us -> 0.59 us
    ppermute x20 -> x12, starting transfers between devices: 55.8 us -> 34.1 us  [shift(): lax.ppermute(x, axis, [(i, i + by) for i in range(n) if 0 <= i + by < n])]
    concatenate x8 -> x0, local copies, waits for them, and re-layouts: 18.4 us -> none  [the longest x1 6.12 us: wide(): head = jnp.concatenate([head] + lists, axis=0)]
    pallas_call x8 -> x12, Pallas kernels: 35.3 us -> 52.1 us  [call(): pl.pallas_call(kernel, out_shape=outs, in_specs=ins, out_specs=(VM,) * le...]
    all_to_all x5, waiting for transfers between devices: 26.9 us -> 15.3 us  [to_all(): return lax.all_to_all(x, BOTH, 0, 0, tiled=True)]
    slice x34 -> x0, local copies, waits for them, and re-layouts: 11 us -> none  [the longest x10 6.1 us: wide(): grown.append(jnp.concatenate([lo[at:at + w], f, hi[at:at + w]], axis=0))]
    concatenate x12 -> x0, other arithmetic: 9.93 us -> none  [the longest x6 7.06 us: wide(): jnp.concatenate([lo[at:at + f.shape[0]], f, hi[at:at + f.shape[0]]], axis=1)]
    all_to_all x5, starting transfers between devices: 49.9 us -> 55.4 us  [to_all(): return lax.all_to_all(x, BOTH, 0, 0, tiled=True)]
  transfers between devices with their start and end apart: 25 -> 18, of which waited for: 6 -> 5; matrix products, arithmetic and copies ran while one was open for 22% -> 0% of each run, Pallas kernels for 3% -> 19%
where the time goes in v2:
time: 166 us; the launch traced here: 165 us
  starting transfers between devices  90.5 us (55%)
  Pallas kernels  52.1 us (31%)
  waiting for transfers between devices  20.3 us (12%)
    all_to_all x5, starting transfers between devices, to_all(): return lax.all_to_all(x, BOTH, 0, 0, tiled=True)  55.4 us
    pallas_call x12, Pallas kernels, call(): pl.pallas_call(kernel, out_shape=outs, in_specs=ins, out_specs=(VM,) * le...  52.1 us
    ppermute x12, starting transfers between devices, shift(): lax.ppermute(x, axis, [(i, i + by) for i in range(n) if 0 <= i + by < n])  34.1 us
    all_to_all x5, waiting for transfers between devices, to_all(): return lax.all_to_all(x, BOTH, 0, 0, tiled=True)  15.3 us
    ppermute x12, waiting for transfers between devices, shift(): lax.ppermute(x, axis, [(i, i + by) for i in range(n) if 0 <= i + by < n])  3.98 us
  transfers between devices with their start and end apart: 18, of which 5 were waited for; matrix products, arithmetic and copies ran while one was open for 0% of the time, Pallas kernels for 19%

profile of v2, /device:TPU:1, one launch (start us, length us, event | category | flops | bytes accessed | tf_op | source)
XLA Modules:
  0.0 164.9 jit_solution(17276691009408485024)
XLA Ops:
  0.6 4.3 %load.1 = (f32[3,16,48,128]{3,2,1,0:T(8,128)}, f32[3,16,48,128]{3,2,1,0:T(8,128)}, f32[16,48,128]{2,1,0:T(8,128)}, f32[16,48,128]{2,1,0:T(8,128)}, f32[16,48,128...) custom-call(f32[3,16,48,128]{3,2,1,0:T(8,128)} %vel.1, ...), custom_call_target="tpu_custom_call" | custom-call | tf_op jit(solution)/shard_map/load/pallas_call | solution.py:598
  5.0 5.1 %collective-permute-start.1 = (f32[11,48,128]{2,1,0:T(8,128)}, f32[11,48,128]{2,1,0:T(8,128)}, u32[]{:S(2)}, u32[]{:S(2)}) collective-permute-start(f32[11,48,128]{2,1,0:T(8,128)} %get-tuple-element.53), channel_id=1, source_target_pairs={{0,16},{16,32},{32,48},{48,64},{64,80},{80,96},{96,112},{1,17},{17... | collective-permute-start | bytes 811016 | tf_op jit(solution)/shard_map/ppermute | solution.py:563
  10.1 1.3 collective-permute-start.2
  11.4 3.3 %wake.1 = (f32[8,128]{1,0:T(8,128)}, f32[8,128]{1,0:T(8,128)}) custom-call(s32[2,16]{1,0:T(2,128)} %bitcast.13, f32[8]{0:T(128)} %chord.1, f32[8]{0:T(128)} %radius.1, f32[3,16,48,128]{3,2,1,0:T(8,128)} %get-tuple-element.41.vel.v, s32[1,256]{1,0:T(1,128)} %bitcast.18, s32[1,256]{1,0:T(1,128)} %bitcast.19, f32[1,256]{1,0:T(1,128)} %bitcast.20, ...), custom_call_target="tpu_custom_call" | custom-call | tf_op jit(solution)/shard_map/wake/pallas_call | solution.py:598
  17.3 1.5 join.1.token
  18.9 11.6 %all-to-all-start = ((f32[128,8,128]{2,1,0:T(8,128)}), f32[128,8,128]{2,1,0:T(8,128)}, u32[]{:S(2)}, u32[]{:S(2)}) async-start(f32[128,8,128]{2,1,0:T(8,128)} %join.1.token), calls=%async_computation | async-start | bytes 1048576 | tf_op jit(solution)/shard_map/all_to_all | solution.py:567
  30.5 3.5 %packy.1 = (f32[96,8,128]{2,1,0:T(8,128)}, f32[96,8,128]{2,1,0:T(8,128)}, f32[90,8,128]{2,1,0:T(8,128)}, f32[90,8,128]{2,1,0:T(8,128)}) custom-call(f32[3,16,48,128]{3,2,1,0:T(8,128)} %get-tuple-element.41.vel.v, f32[3,16,48,128]{3,2,1,0:T(8,128)} %get-tuple-element.48.s.src, f32[16,48,128]{2,1,0:T(8,128)} %get-tuple-element.49.pr.pres, ...), custom_call_target="tpu_custom_call" | custom-call | tf_op jit(solution)/shard_map/packy/pallas_call | solution.py:598
  33.9 3.5 %collective-permute-start.5 = (f32[96,8,128]{2,1,0:T(8,128)}, f32[96,8,128]{2,1,0:T(8,128)}, u32[]{:S(2)}, u32[]{:S(2)}) collective-permute-start(f32[96,8,128]{2,1,0:T(8,128)} %get-tuple-element.57), channel_id=1, source_target_pairs={{0,1},{1,2},{2,3},{3,4},{4,5},{5,6},{6,7},{7,8},{8,9},{9,10},{10,1... | collective-permute-start | bytes 1179656 | tf_op jit(solution)/shard_map/ppermute | solution.py:563
  37.5 1.9 %collective-permute-start.6 = (f32[96,8,128]{2,1,0:T(8,128)}, f32[96,8,128]{2,1,0:T(8,128)}, u32[]{:S(2)}, u32[]{:S(2)}) collective-permute-start(f32[96,8,128]{2,1,0:T(8,128)} %get-tuple-element.58), channel_id=1, source_target_pairs={{1,0},{2,1},{3,2},{4,3},{5,4},{6,5},{7,6},{8,7},{9,8},{10,9},{11,1... | collective-permute-start | bytes 1179656 | tf_op jit(solution)/shard_map/ppermute | solution.py:563
  39.4 3.6 %collective-permute-start.3 = (f32[90,8,128]{2,1,0:T(8,128)}, f32[90,8,128]{2,1,0:T(8,128)}, u32[]{:S(2)}, u32[]{:S(2)}) collective-permute-start(f32[90,8,128]{2,1,0:T(8,128)} %get-tuple-element.55), channel_id=1, source_target_pairs={{0,1},{1,2},{2,3},{3,4},{4,5},{5,6},{6,7},{7,8},{8,9},{9,10},{10,1... | collective-permute-start | bytes 1105928 | tf_op jit(solution)/shard_map/ppermute | solution.py:563
  43.0 1.9 %collective-permute-start.4 = (f32[90,8,128]{2,1,0:T(8,128)}, f32[90,8,128]{2,1,0:T(8,128)}, u32[]{:S(2)}, u32[]{:S(2)}) collective-permute-start(f32[90,8,128]{2,1,0:T(8,128)} %get-tuple-element.56), channel_id=1, source_target_pairs={{1,0},{2,1},{3,2},{4,3},{5,4},{6,5},{7,6},{8,7},{9,8},{10,9},{11,1... | collective-permute-start | bytes 1105928 | tf_op jit(solution)/shard_map/ppermute | solution.py:563
  45.0 2.0 %trim1.1 = (f32[128,2,128]{2,1,0:T(2,128)}, f32[3,8,128]{2,1,0:T(8,128)}, f32[3,128,128]{2,1,0:T(8,128)}) custom-call(f32[128,8,128]{2,1,0:T(8,128)} %all-to-all-done.recv, f32[8,1024]{1,0:T(8,128)} %infl.3), custom_call_target="tpu_custom_call" | custom-call | tf_op jit(solution)/shard_map/trim1/pallas_call | solution.py:598
  47.0 15.1 %all-to-all-start.1 = ((f32[128,2,128]{2,1,0:T(2,128)}), f32[128,2,128]{2,1,0:T(2,128)}, u32[]{:S(2)}, u32[]{:S(2)}) async-start(f32[128,2,128]{2,1,0:T(2,128)} %get-tuple-element.44), calls=%async_computation.1 | async-start | bytes 262144 | tf_op jit(solution)/shard_map/all_to_all | solution.py:567
  62.1 6.9 %sweep1.1 = (f32[3,16,64,128]{3,2,1,0:T(8,128)}, f32[3,16,64,128]{3,2,1,0:T(8,128)}, f32[24,64,128]{2,1,0:T(8,128)}, f32[20,64,128]{2,1,0:T(8,128)}, f32[16,64,1...) custom-call(f32[3,16,48,128]{3,2,1,0:T(8,128)} %get-tuple-element.41.vel.v, ...), custom_call_target="tpu_custom_call" | custom-call | tf_op jit(solution)/shard_map/sweep1/pallas_call | solution.py:598
  69.0 4.0 %collective-permute-start.7 = (f32[3,64,128]{2,1,0:T(8,128)}, f32[3,64,128]{2,1,0:T(8,128)}, u32[]{:S(2)}, u32[]{:S(2)}) collective-permute-start(f32[3,64,128]{2,1,0:T(8,128)} %get-tuple-element.62), channel_id=1, source_target_pairs={{0,16},{16,32},{32,48},{48,64},{64,80},{80,96},{96,112},{1,17},{17... | collective-permute-start | bytes 294920 | tf_op jit(solution)/shard_map/ppermute | solution.py:563
  73.0 1.3 collective-permute-start.8
  75.0 1.9 %trim2.1 = (f32[128,4,128]{2,1,0:T(4,128)}, f32[1,8]{1,0:T(1,128)}) custom-call(f32[1]{0:T(128)S(6)} %copy.24.res, f32[128,2,128]{2,1,0:T(2,128)} %all-to-all-done.1.recv, f32[3,8,128]{2,1,0:T(8,128)} %get-tuple-element.45.state.token, f32[8,1024]{1,0:T(8,128)} %infl.3), custom_call_target="tpu_custom_call" | custom-call | tf_op jit(solution)/shard_map/trim2/pallas_call | solution.py:598
  76.9 11.6 %all-to-all-start.2 = ((f32[128,4,128]{2,1,0:T(4,128)}), f32[128,4,128]{2,1,0:T(4,128)}, u32[]{:S(2)}, u32[]{:S(2)}) async-start(f32[128,4,128]{2,1,0:T(4,128)} %get-tuple-element.46), calls=%async_computation.2 | async-start | bytes 524288 | tf_op jit(solution)/shard_map/all_to_all | solution.py:567
  88.5 4.8 %sweep2.1 = (f32[3,16,64,128]{3,2,1,0:T(8,128)}, f32[7,64,128]{2,1,0:T(8,128)}, f32[7,64,128]{2,1,0:T(8,128)}) custom-call(f32[3,16,64,128]{3,2,1,0:T(8,128)} %get-tuple-element.59.pred, f32[3,16,64,128]{3,2,1,0:T(8,128)} %get-tuple-element.60.source, f32[24,64,128]{2,1,0:T(8,128)} %get-tuple-element.61.invd, f32[3,64,128]{2,1,0:T(8,128)} %collective-permute-done.7.xlo, ...), custom_call_target="tpu_custom_call" | custom-call | tf_op jit(solution)/shard_map/sweep2/pallas_call | solution.py:598
  93.3 1.3 collective-permute-start.10
  94.6 4.7 %collective-permute-start.9 = (f32[7,64,128]{2,1,0:T(8,128)}, f32[7,64,128]{2,1,0:T(8,128)}, u32[]{:S(2)}, u32[]{:S(2)}) collective-permute-start(f32[7,64,128]{2,1,0:T(8,128)} %get-tuple-element.65), channel_id=1, source_target_pairs={{0,16},{16,32},{32,48},{48,64},{64,80},{80,96},{96,112},{1,17},{17... | collective-permute-start | bytes 688136 | tf_op jit(solution)/shard_map/ppermute | solution.py:563
  99.5 4.7 %force.1.b = f32[24,64,128]{2,1,0:T(8,128)} custom-call(f32[128,4,128]{2,1,0:T(4,128)} %all-to-all-done.2.recv, f32[16,128]{1,0:T(8,128)} %get-tuple-element.47.lists, f32[90,8,128]{2,1,0:T(8,128)} %collective-permute-done.3.ylo, f32[90,8,128]{2,1,0:T(8,128)} %collective-permute-done.4.yhi, f32[11,48,128]{2,1,0:T(8,128)} %collective-permute-done.1.xlo.x1lo, ...), custom_call_target="tpu_custom_call" | custom-call | tf_op jit(solution)/shard_map/force/pallas_call | solution.py:598
  104.2 3.9 %collective-permute-done.9.x3lo = f32[7,64,128]{2,1,0:T(8,128)} collective-permute-done((f32[7,64,128]{2,1,0:T(8,128)}, f32[7,64,128]{2,1,0:T(8,128)}, u32[]{:S(2)}, u32[]{:S(2)}) %collective-permute-start.9) | collective-permute-done | bytes 229408 | tf_op jit(solution)/shard_map/ppermute | solution.py:563
  108.2 7.8 %body.1 = (f32[22,64,128]{2,1,0:T(8,128)}, f32[20,64,128]{2,1,0:T(8,128)}, f32[18,64,128]{2,1,0:T(8,128)}, f32[6,64,128]{2,1,0:T(8,128)}, f32[6,64,128]{2,1,0:T(8,128)}, /*index=5*/f32[128,4,128]{2,1,0:T(4,128)}) custom-call(f32[24,64,128]{2,1,0:T(8,128)} %force.1.b, f32[7,64,128]{2,1,0:T(8,128)} %collective-permute-done.9.x3lo, ...), custom_call_target="tpu_custom_call" | custom-call | tf_op jit(solution)/shard_map/body/pallas_call | solution.py:598
  116.0 11.0 %all-to-all-start.3 = ((f32[128,4,128]{2,1,0:T(4,128)}), f32[128,4,128]{2,1,0:T(4,128)}, u32[]{:S(2)}, u32[]{:S(2)}) async-start(f32[128,4,128]{2,1,0:T(4,128)} %get-tuple-element.71), calls=%async_computation.3 | async-start | bytes 524288 | tf_op jit(solution)/shard_map/all_to_all | solution.py:567
  127.0 4.1 %collective-permute-start.11 = (f32[6,64,128]{2,1,0:T(8,128)}, f32[6,64,128]{2,1,0:T(8,128)}, u32[]{:S(2)}, u32[]{:S(2)}) collective-permute-start(f32[6,64,128]{2,1,0:T(8,128)} %get-tuple-element.73), channel_id=1, source_target_pairs={{0,16},{16,32},{32,48},{48,64},{64,80},{80,96},{96,112},{1,17},{17... | collective-permute-start | bytes 589832 | tf_op jit(solution)/shard_map/ppermute | solution.py:563
  131.1 1.3 collective-permute-start.12
  132.4 5.6 %all-to-all-done.3.recv = f32[128,4,128]{2,1,0:T(4,128)} async-done(((f32[128,4,128]{2,1,0:T(4,128)}), f32[128,4,128]{2,1,0:T(4,128)}, u32[]{:S(2)}, u32[]{:S(2)}) %all-to-all-start.3) | async-done | bytes 262176 | tf_op jit(solution)/shard_map/all_to_all | solution.py:567
  138.0 3.3 %coarse.1 = f32[128,128]{1,0:T(8,128)} custom-call(s32[2,16]{1,0:T(2,128)} %bitcast.14, f32[128,4,128]{2,1,0:T(4,128)} %all-to-all-done.3.recv, f32[16,2,128,128]{3,2,1,0:T(8,128)} %blocks.3, f32[3,128,128]{2,1,0:T(8,128)} %get-tuple-element.70.table), custom_call_target="tpu_custom_call" | custom-call | tf_op jit(solution)/shard_map/coarse/pallas_call | solution.py:598
  141.4 6.0 %all-to-all-start.4 = ((f32[128,1,128]{2,1,0:T(1,128)}), f32[128,1,128]{2,1,0:T(1,128)}, u32[]{:S(2)}, u32[]{:S(2)}) async-start(f32[128,1,128]{2,1,0:T(1,128)} %bitcast.12), calls=%async_computation.4 | async-start | bytes 131072 | tf_op jit(solution)/shard_map/all_to_all | solution.py:567
  147.4 9.6 %all-to-all-done.4 = f32[128,1,128]{2,1,0:T(1,128)} async-done(((f32[128,1,128]{2,1,0:T(1,128)}), f32[128,1,128]{2,1,0:T(1,128)}, u32[]{:S(2)}, u32[]{:S(2)}) %all-to-all-start.4) | async-done | bytes 65568 | tf_op jit(solution)/shard_map/all_to_all | solution.py:567
  157.0 8.0 %last.1 = (f32[3,16,48,128]{3,2,1,0:T(8,128)}, f32[16,48,128]{2,1,0:T(8,128)}) custom-call(f32[128,128]{1,0:T(8,128)} %bitcast.9.recv, f32[18,64,128]{2,1,0:T(8,128)} %get-tuple-element.72.corr1, f32[16,64,128]{2,1,0:T(8,128)} %get-tuple-element.69.codes, f32[6,64,128]{2,1,0:T(8,128)} %collective-permute-done.11.xlo, ...), custom_call_target="tpu_custom_call" | custom-call | tf_op jit(solution)/shard_map/last/pallas_call | solution.py:598
  (18 shorter events, 2.8 us)
Async XLA Ops:
  5.0 25.5 %collective-permute-start.1 = (f32[11,48,128]{2,1,0:T(8,128)}, f32[11,48,128]{2,1,0:T(8,128)}, u32[]{:S(2)}, u32[]{:S(2)}) collective-permute-start(f32[11,48,128]{2,1,0:T(8,128)} %get-tuple-element.53), channel_id=1, source_target_pairs={{0,16},{16,32},{32,48},{48,64},{64,80},{80,96},{96,112},{1,17},{17... | collective-permute-start | bytes 811016 | tf_op jit(solution)/shard_map/ppermute | solution.py:563
  10.1 20.4 %collective-permute-start.2 = (f32[11,48,128]{2,1,0:T(8,128)}, f32[11,48,128]{2,1,0:T(8,128)}, u32[]{:S(2)}, u32[]{:S(2)}) collective-permute-start(f32[11,48,128]{2,1,0:T(8,128)} %get-tuple-element.54), channel_id=1, source_target_pairs={{16,0},{32,16},{48,32},{64,48},{80,64},{96,80},{112,96},{17,1},{33... | collective-permute-start | bytes 811016 | tf_op jit(solution)/shard_map/ppermute | solution.py:563
  14.7 2.1 %collective-permute-start = (f32[8,128]{1,0:T(8,128)}, f32[8,128]{1,0:T(8,128)S(1)}, u32[]{:S(2)}, u32[]{:S(2)}) collective-permute-start(f32[8,128]{1,0:T(8,128)} %get-tuple-element.43), channel_id=1, source_target_pairs={{0,1},{1,0},{2,3},{3,2},{4,5},{5,4},{6,7},{7,6},{8,9},{9,8},{10,11... | collective-permute-start | bytes 12296 | tf_op jit(solution)/shard_map/ppermute | solution.py:571
  16.8 0.6 copy-start
  18.9 26.1 %all-to-all-start = ((f32[128,8,128]{2,1,0:T(8,128)}), f32[128,8,128]{2,1,0:T(8,128)}, u32[]{:S(2)}, u32[]{:S(2)}) async-start(f32[128,8,128]{2,1,0:T(8,128)} %join.1.token), calls=%async_computation | async-start | bytes 1048576 | tf_op jit(solution)/shard_map/all_to_all | solution.py:567
  33.9 28.2 %collective-permute-start.5 = (f32[96,8,128]{2,1,0:T(8,128)}, f32[96,8,128]{2,1,0:T(8,128)}, u32[]{:S(2)}, u32[]{:S(2)}) collective-permute-start(f32[96,8,128]{2,1,0:T(8,128)} %get-tuple-element.57), channel_id=1, source_target_pairs={{0,1},{1,2},{2,3},{3,4},{4,5},{5,6},{6,7},{7,8},{8,9},{9,10},{10,1... | collective-permute-start | bytes 1179656 | tf_op jit(solution)/shard_map/ppermute | solution.py:563
  37.5 24.6 %collective-permute-start.6 = (f32[96,8,128]{2,1,0:T(8,128)}, f32[96,8,128]{2,1,0:T(8,128)}, u32[]{:S(2)}, u32[]{:S(2)}) collective-permute-start(f32[96,8,128]{2,1,0:T(8,128)} %get-tuple-element.58), channel_id=1, source_target_pairs={{1,0},{2,1},{3,2},{4,3},{5,4},{6,5},{7,6},{8,7},{9,8},{10,9},{11,1... | collective-permute-start | bytes 1179656 | tf_op jit(solution)/shard_map/ppermute | solution.py:563
  39.4 22.7 %collective-permute-start.3 = (f32[90,8,128]{2,1,0:T(8,128)}, f32[90,8,128]{2,1,0:T(8,128)}, u32[]{:S(2)}, u32[]{:S(2)}) collective-permute-start(f32[90,8,128]{2,1,0:T(8,128)} %get-tuple-element.55), channel_id=1, source_target_pairs={{0,1},{1,2},{2,3},{3,4},{4,5},{5,6},{6,7},{7,8},{8,9},{9,10},{10,1... | collective-permute-start | bytes 1105928 | tf_op jit(solution)/shard_map/ppermute | solution.py:563
  43.0 19.0 %collective-permute-start.4 = (f32[90,8,128]{2,1,0:T(8,128)}, f32[90,8,128]{2,1,0:T(8,128)}, u32[]{:S(2)}, u32[]{:S(2)}) collective-permute-start(f32[90,8,128]{2,1,0:T(8,128)} %get-tuple-element.56), channel_id=1, source_target_pairs={{1,0},{2,1},{3,2},{4,3},{5,4},{6,5},{7,6},{8,7},{9,8},{10,9},{11,1... | collective-permute-start | bytes 1105928 | tf_op jit(solution)/shard_map/ppermute | solution.py:563
  47.0 28.0 %all-to-all-start.1 = ((f32[128,2,128]{2,1,0:T(2,128)}), f32[128,2,128]{2,1,0:T(2,128)}, u32[]{:S(2)}, u32[]{:S(2)}) async-start(f32[128,2,128]{2,1,0:T(2,128)} %get-tuple-element.44), calls=%async_computation.1 | async-start | bytes 262144 | tf_op jit(solution)/shard_map/all_to_all | solution.py:567
  69.0 19.5 %collective-permute-start.7 = (f32[3,64,128]{2,1,0:T(8,128)}, f32[3,64,128]{2,1,0:T(8,128)}, u32[]{:S(2)}, u32[]{:S(2)}) collective-permute-start(f32[3,64,128]{2,1,0:T(8,128)} %get-tuple-element.62), channel_id=1, source_target_pairs={{0,16},{16,32},{32,48},{48,64},{64,80},{80,96},{96,112},{1,17},{17... | collective-permute-start | bytes 294920 | tf_op jit(solution)/shard_map/ppermute | solution.py:563
  73.0 15.5 %collective-permute-start.8 = (f32[3,64,128]{2,1,0:T(8,128)}, f32[3,64,128]{2,1,0:T(8,128)}, u32[]{:S(2)}, u32[]{:S(2)}) collective-permute-start(f32[3,64,128]{2,1,0:T(8,128)} %get-tuple-element.63), channel_id=1, source_target_pairs={{16,0},{32,16},{48,32},{64,48},{80,64},{96,80},{112,96},{17,1},{33... | collective-permute-start | bytes 294920 | tf_op jit(solution)/shard_map/ppermute | solution.py:563
  76.9 22.6 %all-to-all-start.2 = ((f32[128,4,128]{2,1,0:T(4,128)}), f32[128,4,128]{2,1,0:T(4,128)}, u32[]{:S(2)}, u32[]{:S(2)}) async-start(f32[128,4,128]{2,1,0:T(4,128)} %get-tuple-element.46), calls=%async_computation.2 | async-start | bytes 524288 | tf_op jit(solution)/shard_map/all_to_all | solution.py:567
  93.3 10.9 %collective-permute-start.10 = (f32[7,64,128]{2,1,0:T(8,128)}, f32[7,64,128]{2,1,0:T(8,128)}, u32[]{:S(2)}, u32[]{:S(2)}) collective-permute-start(f32[7,64,128]{2,1,0:T(8,128)} %get-tuple-element.66), channel_id=1, source_target_pairs={{16,0},{32,16},{48,32},{64,48},{80,64},{96,80},{112,96},{17,1},{33... | collective-permute-start | bytes 688136 | tf_op jit(solution)/shard_map/ppermute | solution.py:563
  94.6 13.6 %collective-permute-start.9 = (f32[7,64,128]{2,1,0:T(8,128)}, f32[7,64,128]{2,1,0:T(8,128)}, u32[]{:S(2)}, u32[]{:S(2)}) collective-permute-start(f32[7,64,128]{2,1,0:T(8,128)} %get-tuple-element.65), channel_id=1, source_target_pairs={{0,16},{16,32},{32,48},{48,64},{64,80},{80,96},{96,112},{1,17},{17... | collective-permute-start | bytes 688136 | tf_op jit(solution)/shard_map/ppermute | solution.py:563
  116.0 22.0 %all-to-all-start.3 = ((f32[128,4,128]{2,1,0:T(4,128)}), f32[128,4,128]{2,1,0:T(4,128)}, u32[]{:S(2)}, u32[]{:S(2)}) async-start(f32[128,4,128]{2,1,0:T(4,128)} %get-tuple-element.71), calls=%async_computation.3 | async-start | bytes 524288 | tf_op jit(solution)/shard_map/all_to_all | solution.py:567
  127.0 20.4 %collective-permute-start.11 = (f32[6,64,128]{2,1,0:T(8,128)}, f32[6,64,128]{2,1,0:T(8,128)}, u32[]{:S(2)}, u32[]{:S(2)}) collective-permute-start(f32[6,64,128]{2,1,0:T(8,128)} %get-tuple-element.73), channel_id=1, source_target_pairs={{0,16},{16,32},{32,48},{48,64},{64,80},{80,96},{96,112},{1,17},{17... | collective-permute-start | bytes 589832 | tf_op jit(solution)/shard_map/ppermute | solution.py:563
  131.1 16.3 %collective-permute-start.12 = (f32[6,64,128]{2,1,0:T(8,128)}, f32[6,64,128]{2,1,0:T(8,128)}, u32[]{:S(2)}, u32[]{:S(2)}) collective-permute-start(f32[6,64,128]{2,1,0:T(8,128)} %get-tuple-element.74), channel_id=1, source_target_pairs={{16,0},{32,16},{48,32},{64,48},{80,64},{96,80},{112,96},{17,1},{33... | collective-permute-start | bytes 589832 | tf_op jit(solution)/shard_map/ppermute | solution.py:563
  141.4 15.6 %all-to-all-start.4 = ((f32[128,1,128]{2,1,0:T(1,128)}), f32[128,1,128]{2,1,0:T(1,128)}, u32[]{:S(2)}, u32[]{:S(2)}) async-start(f32[128,1,128]{2,1,0:T(1,128)} %bitcast.12), calls=%async_computation.4 | async-start | bytes 131072 | tf_op jit(solution)/shard_map/all_to_all | solution.py:567

commit v3 on v2

--- a/solution.py
+++ b/solution.py
@@ -10,7 +10,7 @@
 CX, CY, CZ = 16, 48, 128
 NSEC = 1024
 BOTH = ("hullx", "hully")
-ROWS = (2, 4, 4)
+ROWS = (4, 1, 4)
 F32, BF16, I32 = jnp.float32, jnp.bfloat16, jnp.int32
 HIGH = lax.Precision.HIGHEST
 YE = 64
@@ -78,16 +78,15 @@
     return (a + b) + (c + d)
 
 
-def wake_kernel(cols, chord, radius, vel, wc, ws, ww, blocks, keep, give, row, ab, sem):
-    hx, hy = here()
-    copies = [pltpu.make_async_copy(blocks.at[2 * hx + i, 0], ab.at[i], sem.at[i]) for i in range(2)]
-    for c in copies:
-        c.start()
+def wake_kernel(cols, chord, radius, vel, wc, ws, ww, blocks, keep, give, row, ab, v, sem):
+    hx, hy = here()
+    copies = run([(vel.at[0], v)] + [(blocks.at[2 * hx + i, 0], ab.at[i]) for i in range(2)], sem)
     cells = wc[...]
     place = cells >> 7
     spot = (iota((768, 256), 0) == place).astype(BF16)
     picked = jnp.zeros((128, 256), F32)
-    for part in split3(vel[0].reshape(768, 128)):
+    copies[0].wait()
+    for part in split2(v[...].reshape(768, 128)):
         picked = picked + lax.dot_general(part, spot, (((0,), (0,)), ((), ())), preferred_element_type=F32)
     samples = jnp.sum(jnp.where(iota((128, 256), 0) == (cells & 127), picked, 0.0), axis=0, keepdims=True) * ww[...]
     sec = ws[...]
@@ -105,8 +104,7 @@
     eye = iota((128, 128), 0) == iota((128, 128), 1)
     even = (hy & 1) == 0
     first, second = row[0:4, :], row[4:8, :]
-    for c in copies:
-        c.wait()
+    finish_all(copies[1:])
     d0 = jnp.sum(jnp.where(eye, ab[0], 0.0), axis=0, keepdims=True)
     d1 = jnp.sum(jnp.where(eye, ab[1], 0.0), axis=0, keepdims=True)
     keep[...] = jnp.concatenate([jnp.where(even, first, second), jnp.where(even, crow, rrow), d0, d1, colrow], axis=0)
@@ -186,126 +184,174 @@
     return jnp.concatenate([low, middle, high], axis=0)
 
 
-def load_kernel(
-    vel, src, pres, mdiag, pdiag, agg, bc, bs, bw,
-    v, s, pr, invd, invp, codes, lists, tail, head,
-    ag, ints, sems,
+HALO = 17
+
+
+def packx_kernel(vel, src, pres, mdiag, pdiag, bc, bs, bw, tail, head, ints, sems):
+    ends = ((1, tail), (0, head))
+    pairs = []
+    for last, out in ends:
+        end = lambda w: pl.ds(last * (CX - w), w)
+        pairs += [(mdiag.at[end(4)], out.at[11:15]), (pdiag.at[end(2)], out.at[15:17])]
+    pairs += [(bc, ints.at[0]), (bs, ints.at[1])]
+    first = len(pairs)
+    for last, out in ends:
+        end = lambda w: pl.ds(last * (CX - w), w)
+        pairs.append((bw, out.at[HALO, 8:12]))
+        pairs.append((pres.at[end(2)], out.at[9:11]))
+        for c in range(3):
+            pairs.append((vel.at[c, end(2)], out.at[2 * c : 2 * c + 2]))
+            pairs.append((src.at[c, end(1)], out.at[6 + c : 7 + c]))
+    copies = run(pairs, sems)
+    finish_all(copies[:first])
+    for out in (tail, head):
+        out[11:17] = 1.0 / (6.0 + out[11:17])
+        out[HALO, 0:4] = ints[0].astype(F32)
+        out[HALO, 4:8] = ints[1].astype(F32)
+        out[HALO, 12:16] = jnp.zeros((4, 128), F32)
+        out[HALO, 16:48] = jnp.zeros((32, 128), F32)
+    finish_all(copies[first:])
+
+
+def packy_kernel(
+    vel, src, pres, mdiag, pdiag, agg, lists, xlo, xhi, token,
+    near_a, far_a, near_b, far_b,
+    edge, aedge, sems,
 ):
     hx, hy = here()
-    copies = run(
-        [(mdiag, invd), (pdiag, invp), (bc, ints.at[0]), (bs, ints.at[1]), (bw, lists.at[8:12]), (pres, pr), (vel, v), (agg, ag), (src, s)],
-        sems,
-    )
-    lists[12:16, :] = jnp.zeros((4, 128), F32)
-    finish_all(copies[:5])
-    lists[0:4, :] = ints[0].astype(F32)
-    lists[4:8, :] = ints[1].astype(F32)
-    invd[...] = 1.0 / (6.0 + invd[...])
-    invp[...] = 1.0 / (6.0 + invp[...])
-    tail[4:8] = invd[CX - 4 : CX]
-    head[4:8] = invd[0:4]
-    tail[8:10] = invp[CX - 2 : CX]
-    head[8:10] = invp[0:2]
-    for out in (tail, head):
-        out[10, 0:16] = lists[...]
-        out[10, 16:48] = jnp.zeros((32, 128), F32)
-    finish_all(copies[5:8])
-    for x, out in ((CX - 1, tail), (0, head)):
-        out[0:3] = v[:, x]
-        out[3] = pr[x]
-    codes[...] = codes_of(ag[...], hx, hy, 0)
-    finish_all(copies[8:])
-
-
-def packy_kernel(v, s, pr, invd, invp, codes, lists, xlo, xhi, token, tail_a, head_a, tail_b, head_b):
-    for row, a, out in ((CY - 8, tail_a, tail_b), (0, head_a, head_b)):
-        rows = slice(row, row + 8)
+    odd = hy & 1
+    ends = []
+    for at, a, out in ((1 - odd, near_a, near_b), (odd, far_a, far_b)):
+        row = pl.multiple_of((CY - 8) * at, 8)
+        ends.append((pl.ds(row, 8), row, a, out))
+    pairs = []
+    for n, (rows, _, a, out) in enumerate(ends):
+        pairs += [(mdiag.at[:, rows], edge.at[n, 0]), (pdiag.at[:, rows], edge.at[n, 1]), (agg.at[:, rows], aedge.at[n])]
+    for rows, _, a, out in ends:
         for c in range(3):
-            a[CX * c : CX * c + CX] = v[c, :, rows, :]
-            a[48 + CX * c : 64 + CX * c] = s[c, :, rows, :]
-        for k, f in enumerate((pr, invd, invp, codes)):
-            out[CX * k : CX * k + CX] = f[:, rows, :]
-        out[64:74] = xlo[0:10, rows, :]
-        out[74:84] = xhi[0:10, rows, :]
+            pairs.append((vel.at[c, :, rows], a.at[CX * c : CX * c + CX]))
+            pairs.append((src.at[c, :, rows], a.at[48 + CX * c : 64 + CX * c]))
+        pairs.append((pres.at[:, rows], out.at[0:CX]))
+        for k, side in ((0, xlo), (1, xhi)):
+            pairs.append((side.at[0:HALO, rows], out.at[pl.ds(64 + HALO * k, HALO)]))
+            for j in range(2):
+                pairs.append((side.at[HALO, slice(8 * j, 8 * j + 8)], out.at[100 + 2 * k + j]))
         for j in range(2):
-            part = slice(8 * j, 8 * j + 8)
-            out[84 + j] = lists[part, :]
-            out[86 + j] = xlo[10, part, :]
-            out[88 + j] = xhi[10, part, :]
-
-
-def sweep1_kernel(
-    vel, src, pres, invd_own, invp_own, codes_own, yalo, yahi, ylo, yhi, xlo, xhi, token,
-    pred, source, invd, invp, codes, tail, head,
-    v,
+            pairs.append((lists.at[HALO, slice(8 * j, 8 * j + 8)], out.at[98 + j]))
+    copies = run(pairs, sems)
+    finish_all(copies[:6])
+    for n, (_, row, a, out) in enumerate(ends):
+        out[16:32] = 1.0 / (6.0 + edge[n, 0])
+        out[32:48] = 1.0 / (6.0 + edge[n, 1])
+        out[48:64] = codes_of(aedge[n], hx, hy, row)
+    finish_all(copies[6:])
+
+
+def sweeps_kernel(
+    vel, src, pres, mdiag, pdiag, agg, near_a, far_a, near_b, far_b, xlo, xhi, token,
+    free, invd_out, invp_out, codes_out, near, far,
+    v, s, q, invd, invp, codes, ya, yb, xb, sems,
 ):
-    for n, (side, at) in enumerate(((xlo, 64), (xhi, 74))):
+    hx, hy = here()
+    odd = hy & 1
+    finish_all(
+        run(
+            [(near_a, ya.at[1 - odd]), (far_a, ya.at[odd]), (near_b, yb.at[1 - odd]), (far_b, yb.at[odd])]
+            + [(xlo.at[0:HALO], xb.at[0]), (xhi.at[0:HALO], xb.at[1])],
+            sems,
+        )
+    )
+    yalo, yahi, ylo, yhi = ya.at[0], ya.at[1], yb.at[0], yb.at[1]
+    for n in range(2):
+        grown = lambda k: widen(ylo[64 + HALO * n + k], xb[n, k], yhi[64 + HALO * n + k])
+        for k in range(2):
+            for c in range(3):
+                v[c, 18 * n + k] = grown(2 * c + k)
+            v[3, 18 * n + k] = grown(9 + k)
+            invp[18 * n + k] = grown(15 + k)
+        for c in range(3):
+            s[c, 17 * n] = grown(6 + c)
         for k in range(4):
-            v[k, (CX + 1) * n] = widen(ylo[at + k], side[k], yhi[at + k])
-        for k in range(4):
-            invd[20 * n + k] = widen(ylo[at + 4 + k], side[4 + k], yhi[at + 4 + k])
-        for k in range(2):
-            invp[18 * n + k] = widen(ylo[at + 8 + k], side[8 + k], yhi[at + 8 + k])
+            invd[20 * n + k] = grown(11 + k)
 
     def grow(x, carry):
-        for k in range(3):
-            v[k, x + 1] = widen(yalo[CX * k + x], vel[k, x], yahi[CX * k + x])
-        v[3, x + 1] = widen(ylo[x], pres[x], yhi[x])
-        invd[x + 4] = widen(ylo[16 + x], invd_own[x], yhi[16 + x])
-        invp[x + 2] = widen(ylo[32 + x], invp_own[x], yhi[32 + x])
-        codes[x] = widen(ylo[48 + x], codes_own[x], yhi[48 + x])
+        for c in range(3):
+            v[c, x + 2] = widen(yalo[CX * c + x], vel[c, x], yahi[CX * c + x])
+            s[c, x + 1] = widen(yalo[48 + CX * c + x], src[c, x], yahi[48 + CX * c + x])
+        v[3, x + 2] = widen(ylo[x], pres[x], yhi[x])
+        invd[x + 4] = widen(ylo[16 + x], 1.0 / (6.0 + mdiag[x]), yhi[16 + x])
+        invp[x + 2] = widen(ylo[32 + x], 1.0 / (6.0 + pdiag[x]), yhi[32 + x])
+        base = (CX * hx + x) * 256 + 16 * hy + lax.div(iota((CY, 128), 0), 3)
+        codes[x] = widen(ylo[48 + x], (agg[x] - base + 4).astype(F32), yhi[48 + x])
         return carry
 
     lax.fori_loop(0, CX, grow, 0, unroll=2)
 
-    def body(x, carry):
-        inv = invd[x + 4]
-        p = v[3, x + 1]
+    copies = run([(invd, invd_out), (invp, invp_out), (codes, codes_out)], sems)
+
+    def first(i, carry):
+        inv = invd[i + 3]
+        p = v[3, i + 1]
         ya, yb = y_parts(p)
         za, zb = zdiff_parts(p)
-        for c, grad in enumerate((v[3, x + 2] - v[3, x], yb - ya, zb - za)):
-            sc = widen(yalo[48 + CX * c + x], src[c, x], yahi[48 + CX * c + x]) - 0.5 * grad
-            source[c, x] = sc
-            pred[c, x] = (sc + v[c, x] + v[c, x + 2] + s_yz(v[c, x + 1])) * inv
+        for c, grad in enumerate((v[3, i + 2] - v[3, i], yb - ya, zb - za)):
+            sc = s[c, i] - 0.5 * grad
+            s[c, i] = sc
+            q[c, i] = (sc + v[c, i] + v[c, i + 2] + s_yz(v[c, i + 1])) * inv
         return carry
 
-    lax.fori_loop(0, CX, body, 0, unroll=2)
-    tail[0:3] = pred[:, CX - 1]
-    head[0:3] = pred[:, 0]
-
-
-def sweep2_kernel(pred, source, invd, xlo, xhi, token, out, tail, head):
-    def at(x, before, here_, after):
+    lax.fori_loop(0, CX + 2, first, 0, unroll=2)
+
+    def second(x, carry):
         inv = invd[x + 4]
         for c in range(3):
-            out[c, x] = (source[c, x] + before(c) + after(c) + s_yz(here_(c))) * inv
-
-    def body(x, carry):
-        at(x, lambda c: pred[c, x - 1], lambda c: pred[c, x], lambda c: pred[c, x + 1])
+            free[c, x] = (s[c, x + 1] + q[c, x] + q[c, x + 2] + s_yz(q[c, x + 1])) * inv
         return carry
 
-    at(0, lambda c: xlo[c], lambda c: pred[c, 0], lambda c: pred[c, 1])
-    lax.fori_loop(1, CX - 1, body, 0, unroll=2)
-    at(CX - 1, lambda c: pred[c, CX - 2], lambda c: pred[c, CX - 1], lambda c: xhi[c])
+    lax.fori_loop(0, CX, second, 0, unroll=2)
     to = 0
     for c, w in enumerate((3, 2, 2)):
-        tail[to : to + w] = out[c, CX - w : CX]
-        head[to : to + w] = out[c, 0:w]
+        near[to : to + w] = free[c, pl.ds((1 - (hx & 1)) * (CX - w), w)]
+        far[to : to + w] = free[c, pl.ds((hx & 1) * (CX - w), w)]
         to += w
+    finish_all(copies)
 
 
 def body_parts():
     return [(sx, sy) for sy in (0, -1, 1) for sx in (0, -1, 1)]
 
 
-def force_kernel(recv, lists, ylo, yhi, x1lo, x1hi, b, listed, sems):
-    listed[0:16, :] = lists[...]
-    early = [(x1lo.at[10, 0:16], listed.at[16:32]), (x1hi.at[10, 0:16], listed.at[32:48])]
-    for n, buf in enumerate((ylo, yhi)):
+def three(n, w, fn):
+    for i in range(w):
+        fn(i, 0, i)
+
+    def own(j, carry):
+        fn(j + w, 1, j)
+        return carry
+
+    lax.fori_loop(0, CX, own, 0, unroll=4)
+    for i in range(n - CX - w):
+        fn(CX + w + i, 2, i)
+
+
+def body_kernel(
+    recv, lists, ynear, yfar, xlo, xhi, unear, ufar, free_in, invd_in, invp_in, codes_in, table_in, gfold,
+    pr0, target, corr1, near, far, send,
+    b, listed, dp, corr0, acc, x3, free, invd, invp, codes, table, early_sems, sems,
+):
+    hx, hy = here()
+    early = [(lists.at[HALO, 0:16], listed.at[0:16])]
+    early += [(xlo.at[HALO, 0:16], listed.at[16:32]), (xhi.at[HALO, 0:16], listed.at[32:48])]
+    for n, buf in ((1 - (hy & 1), ynear), (hy & 1, yfar)):
         for j in range(6):
-            at = 48 + 48 * n + 8 * j
-            early.append((buf.at[84 + j], listed.at[at : at + 8]))
-    finish_all(run(early, sems))
+            at = pl.multiple_of(48 + 48 * n + 8 * j, 8)
+            early.append((buf.at[98 + j], listed.at[pl.ds(at, 8)]))
+    early = run(early, early_sems)
+    copies = run(
+        [(invd_in, invd), (unear, x3.at[1 - (hx & 1)]), (ufar, x3.at[hx & 1]), (free_in, free), (invp_in, invp), (codes_in, codes), (table_in, table)],
+        sems,
+    )
+    finish_all(early)
     force = jnp.sum(recv[:, 0, :].reshape(HX, HY, 128), axis=1)
 
     def entries(j):
@@ -348,27 +394,8 @@
             at = 0 if sy < 0 else 56
             b[first : first + planes, at : at + 8] = b[first : first + planes, at : at + 8] + part.reshape(planes, 8, 128)
 
-
-def three(n, w, fn):
-    for i in range(w):
-        fn(i, 0, i)
-
-    def own(j, carry):
-        fn(j + w, 1, j)
-        return carry
-
-    lax.fori_loop(0, CX, own, 0, unroll=4)
-    for i in range(n - CX - w):
-        fn(CX + w + i, 2, i)
-
-
-def body_kernel(
-    b, x3lo, x3hi, free, invd, invp, codes, table, gfold,
-    pr0, target, corr1, tail, head, send,
-    dp, corr0, acc,
-):
-    hx, hy = here()
-    u = lambda c, at, part, j: (x3lo[at + j] if part == 0 else x3hi[at + j]) if part != 1 else free[c, j]
+    finish_all(copies[:4])
+    u = lambda c, at, part, j: x3[part // 2, at + j] if part != 1 else free[c, j]
 
     def s1(p, part, j):
         dp[p] = b[p] * invd[p]
@@ -391,6 +418,7 @@
 
     three(24, 4, s1)
     three(22, 3, s2)
+    finish_all(copies[4:])
     three(20, 2, s3)
     three(18, 1, s4)
 
@@ -411,10 +439,9 @@
 
     acc[...] = jnp.zeros(acc.shape, F32)
     lax.fori_loop(0, CX // 4, s5, 0)
-    tail[0:3] = corr1[CX - 2 : CX + 1]
-    tail[3:6] = codes[CX - 3 : CX]
-    head[0:3] = corr1[1:4]
-    head[3:6] = codes[0:3]
+    for last, out in ((1 - (hx & 1), near), (hx & 1, far)):
+        out[0:3] = corr1[pl.ds(1 + last * (CX - 3), 3)]
+        out[3:6] = codes[pl.ds(last * (CX - 3), 3)]
     window = mm(gfold[...], acc[...], HIGH) * float(384.0**-0.5)
     blank = jnp.zeros((32, 128), F32)
     spread = jnp.concatenate(
@@ -468,8 +495,15 @@
     first = 0.8 * res / diag[...]
     seconds = []
     copy.wait()
+    parts = jnp.concatenate(split3(first), axis=0)
+
+    def product(block, row):
+        hi, lo = split2(block)
+        both = nt(parts, hi) + nt(parts, lo)
+        return both[row : row + 1] + both[8 + row : 9 + row] + both[16 + row : 17 + row]
+
     for i in range(2):
-        applied = nt(first, ab[i, 0], HIGH)[i : i + 1] + nt(first, ab[i, 1], HIGH)[2 + i : 3 + i]
+        applied = product(ab[i, 0], i) + product(ab[i, 1], 2 + i)
         seconds.append(first[i : i + 1] + 0.8 * (res[i : i + 1] - applied) / diag[i : i + 1, :])
     second = jnp.concatenate(seconds, axis=1)
     lane2 = iota((HY, 256), 1)
@@ -488,10 +522,18 @@
 
 
 def last_kernel(
-    recv, corr1, codes, xlo, xhi, target, invp, pr0, free, pres, glift,
+    recv, corr1_in, codes_in, xnear, xfar, target_in, invp_in, pr0_in, free_in, pres_in, glift,
     vel_out, pres_out,
-    win, c2, s1, s2,
+    win, c2, s1, s2, corr1, codes, target, invp, pr0, free, pres, xb, sems,
 ):
+    hx, hy = here()
+    mid = slice(1, CX + 1)
+    copies = run(
+        [(corr1_in.at[mid], corr1.at[mid]), (codes_in, codes), (xnear, xb.at[1 - (hx & 1)]), (xfar, xb.at[hx & 1])]
+        + [(target_in, target), (invp_in, invp)]
+        + [(pr0_in.at[3 : 3 + CX, MID], pr0), (free_in.at[1:3, :, MID], free), (pres_in, pres)],
+        sems,
+    )
     hx, hy = here()
     for i in range(24):
         p = jnp.clip(CX * hx - 4 + i, 0, 127)
@@ -509,15 +551,17 @@
     def lift(i, part, j):
         column = jnp.sum(jnp.where(iota((32, 128), 1) == i + 1, win[0:32, :], 0.0), axis=1, keepdims=True)
         wide = jnp.broadcast_to(column, (32, 128))
-        v = mm(glift[...], jnp.concatenate(split3(wide), axis=0))
-        side = (xlo, None, xhi)[part]
+        v = mm(glift[...], jnp.concatenate(split2(wide), axis=0))
+        side = xb.at[part // 2]
         code = codes[j] if part == 1 else side[3 + j]
         lifted = corr1[j + 1] if part == 1 else side[j]
         for n in range(7):
             lifted = jnp.where(code == float(n + 1), lifted + v[n * YE : (n + 1) * YE], lifted)
         c2[i] = lifted
 
+    finish_all(copies[:4])
     three(22, 3, lift)
+    finish_all(copies[4:6])
 
     def sweep1(t, part, j):
         v = c2[t + 1]
@@ -529,14 +573,16 @@
 
     three(20, 2, sweep1)
     three(18, 1, sweep2)
+
+    finish_all(copies[6:])
 
     def finish(x, carry):
         v = s2[x + 1]
         ya, yb = y_parts(v)
         za, zb = zdiff_parts(v)
-        vel_out[0, x] = pr0[x + 3, MID, :] - 0.5 * (s2[x + 2] - s2[x])[8:56]
-        vel_out[1, x] = free[1, x, MID, :] - 0.5 * (yb - ya)[8:56]
-        vel_out[2, x] = free[2, x, MID, :] - 0.5 * (zb - za)[8:56]
+        vel_out[0, x] = pr0[x] - 0.5 * (s2[x + 2] - s2[x])[8:56]
+        vel_out[1, x] = free[0, x] - 0.5 * (yb - ya)[8:56]
+        vel_out[2, x] = free[1, x] - 0.5 * (zb - za)[8:56]
         pres_out[x] = pres[x] + 0.7 * v[8:56]
         return carry
 
@@ -548,35 +594,31 @@
     gfold = np.zeros((32, 7 * CY), np.float32)
     for d in range(7):
         gfold[y // 3 + d + 1, d * CY + y] = 1.0
-    glift = np.zeros((7 * YE, 96), np.float32)
+    glift = np.zeros((7 * YE, 64), np.float32)
     for d in range(7):
         for yy in range(YE):
             slot = (yy - 8) // 3 + d + 1
             if 0 <= slot < 32:
-                for part in range(3):
+                for part in range(2):
                     glift[d * YE + yy, part * 32 + slot] = 1.0
     return gfold, glift
 
 
-def shift(x, axis, by):
-    n = HX if axis == "hullx" else HY
-    return lax.ppermute(x, axis, [(i, i + by) for i in range(n) if 0 <= i + by < n])
-
-
 def to_all(x):
     return lax.all_to_all(x, BOTH, 0, 0, tiled=True)
 
 
-def pair(x):
-    return lax.ppermute(x, "hully", [(i, i ^ 1) for i in range(HY)])
-
-
-def fast(*dims, dtype=F32):
-    return jax.ShapeDtypeStruct(dims, dtype)
-
-
-def send(*dims, dtype=F32):
-    return jax.ShapeDtypeStruct(dims, dtype)
+def pair(x, axis="hully"):
+    return lax.ppermute(x, axis, [(i, i ^ 1) for i in range(HX if axis == "hullx" else HY)])
+
+
+def across(x, axis="hully"):
+    n = HX if axis == "hullx" else HY
+    return lax.ppermute(x, axis, [(i, j) for k in range(1, n - 1, 2) for i, j in ((k, k + 1), (k + 1, k))])
+
+
+def shift(x, by):
+    return lax.ppermute(x, "hullx", [(i, i + by) for i in range(HX) if 0 <= i + by < HX])
 
 
 def shp(*dims, dtype=F32):
@@ -593,85 +635,80 @@
     block = lambda *n: pltpu.VMEM((*n, YE, CZ), F32)
     sems = lambda n: pltpu.SemaphoreType.DMA((n,))
 
-    def call(kernel, name, outs, ins, scratch, args):
-        many = isinstance(outs, tuple)
+    def call(kernel, name, outs, ins, scratch, args, out_specs=None):
+        if out_specs is None:
+            out_specs = (VM,) * len(outs) if isinstance(outs, tuple) else VM
         return pl.pallas_call(
-            kernel, out_shape=outs, in_specs=ins, out_specs=(VM,) * len(outs) if many else VM,
+            kernel, out_shape=outs, in_specs=ins, out_specs=out_specs,
             scratch_shapes=scratch, compiler_params=PARAMS, name=name,
         )(*args)
 
-    def slow(*arrays):
-        return arrays
-
-    v, src, pres, invd_own, invp_own, codes_own, lists, xt, xh = call(
-        load_kernel, "load",
-        (fast(3, CX, CY, CZ),) * 2 + (fast(CX, CY, CZ),) * 4 + (fast(16, 128),) + (send(11, CY, CZ),) * 2,
-        [AN] * 9, [pltpu.VMEM((CX, CY, CZ), I32), pltpu.VMEM((2, 4, 128), I32), sems(9)],
-        slow(velocity, mom_source, pressure, mom_diag, press_diag, agglomeration)
-        + slow(*(a.reshape(4, 128) for a in (body_cells, body_sections, body_weights))),
-    )
-    x1lo, x1hi = shift(xt, "hullx", 1), shift(xh, "hullx", -1)
+    xt, xh = call(
+        packx_kernel, "packx", (shp(HALO + 1, CY, CZ),) * 2, [AN] * 8, [pltpu.VMEM((2, 4, 128), I32), sems(22)],
+        (velocity, mom_source, pressure, mom_diag, press_diag)
+        + tuple(a.reshape(4, 128) for a in (body_cells, body_sections, body_weights)),
+    )
+    x1lo, x1hi = shift(xt, 1), shift(xh, -1)
 
     keep, give = call(
-        wake_kernel, "wake", (fast(8, 128), send(8, 128)), [SM, SM, SM, VM, VM, VM, VM, AN],
-        [pltpu.VMEM((8, 128), F32), pltpu.VMEM((2, 128, 128), F32), sems(2)],
-        (cols, chord, radius, v, wake_cells[None], wake_sections[None], wake_weights[None]) + slow(coarse_blocks),
-    )
-    payload = call(join_kernel, "join", send(128, 8, 128), [VM, VM], [], (keep, pair(give)))
+        wake_kernel, "wake", (shp(8, 128),) * 2, [SM, SM, SM, AN, VM, VM, VM, AN],
+        [pltpu.VMEM((8, 128), F32), pltpu.VMEM((2, 128, 128), F32), pltpu.VMEM((CX, CY, CZ), F32), sems(3)],
+        (cols, chord, radius, velocity, wake_cells[None], wake_sections[None], wake_weights[None]) + (coarse_blocks,),
+    )
+    payload = call(join_kernel, "join", shp(128, 8, 128), [VM, VM], [], (keep, pair(give)))
     recv1 = to_all(payload)
     out1, state, table = call(
-        trim1_kernel, "trim1", (send(128, ROWS[0], 128), fast(3, 8, 128), fast(3, 128, 128)), [VM, VM],
-        [pltpu.VMEM((2, 8, 8, 128), F32)], (recv1,) + slow(influence),
+        trim1_kernel, "trim1", (shp(128, ROWS[0], 128), shp(3, 8, 128), shp(3, 128, 128)), [VM, VM],
+        [pltpu.VMEM((2, 8, 8, 128), F32)], (recv1,) + (influence,),
     )
     recv2 = to_all(out1)
 
-    yat, yah, yt, yh = call(
-        packy_kernel, "packy", (send(96, 8, CZ),) * 2 + (send(90, 8, CZ),) * 2, [VM] * 9 + [AN], [],
-        (v, src, pres, invd_own, invp_own, codes_own, lists, x1lo, x1hi, payload),
-    )
-    yalo, yahi = shift(yat, "hully", 1), shift(yah, "hully", -1)
-    ylo, yhi = shift(yt, "hully", 1), shift(yh, "hully", -1)
-    pred1, source, invd, invp, codes, xt, xh = call(
-        sweep1_kernel, "sweep1",
-        (fast(3, CX, YE, CZ),) * 2 + (fast(24, YE, CZ), fast(20, YE, CZ), fast(CX, YE, CZ)) + (send(3, YE, CZ),) * 2,
-        [VM] * 13, [block(4, CX + 2)],
-        (v, src, pres, invd_own, invp_own, codes_own, yalo, yahi, ylo, yhi, x1lo, x1hi, state),
-    )
-    x2lo, x2hi = shift(xt, "hullx", 1), shift(xh, "hullx", -1)
+    ya_near, ya_far, yb_near, yb_far = call(
+        packy_kernel, "packy", (shp(96, 8, CZ),) * 2 + (shp(104, 8, CZ),) * 2, [AN] * 10,
+        [pltpu.VMEM((2, 2, CX, 8, CZ), F32), pltpu.VMEM((2, CX, 8, CZ), I32), sems(36)],
+        (velocity, mom_source, pressure, mom_diag, press_diag, agglomeration, xt, x1lo, x1hi, payload),
+    )
+    ya_near, yb_near = pair(ya_near), pair(yb_near)
+    ya_far, yb_far = across(ya_far), across(yb_far)
+    free, invd, invp, codes, fxt, fxh = call(
+        sweeps_kernel, "sweeps",
+        (shp(3, CX, YE, CZ), shp(24, YE, CZ), shp(20, YE, CZ), shp(CX, YE, CZ)) + (shp(7, YE, CZ),) * 2,
+        [VM] * 6 + [AN] * 7,
+        [block(4, CX + 4), block(3, CX + 2), block(3, CX + 2), block(24), block(20), block(CX)]
+        + [pltpu.VMEM((2, 96, 8, CZ), F32), pltpu.VMEM((2, 104, 8, CZ), F32), pltpu.VMEM((2, HALO, CY, CZ), F32), sems(6)],
+        (velocity, mom_source, pressure, mom_diag, press_diag, agglomeration, ya_near, ya_far, yb_near, yb_far, x1lo, x1hi, state),
+        (VM, AN, AN, AN, VM, VM),
+    )
+    x3near, x3far = pair(fxt, "hullx"), across(fxh, "hullx")
 
     out2, force = call(
-        trim2_kernel, "trim2", (send(128, ROWS[1], 128), fast(1, 8)), [SM, VM, VM, VM], [],
-        (resistance, recv2, state) + slow(influence),
+        trim2_kernel, "trim2", (shp(128, ROWS[1], 128), shp(1, 8)), [SM, VM, VM, VM], [],
+        (resistance, recv2, state, influence),
     )
     recv3 = to_all(out2)
-    free, xt, xh = call(
-        sweep2_kernel, "sweep2", (fast(3, CX, YE, CZ),) + (send(7, YE, CZ),) * 2, [VM] * 6, [],
-        (pred1, source, invd, x2lo, x2hi, force),
-    )
-    x3lo, x3hi = shift(xt, "hullx", 1), shift(xh, "hullx", -1)
-
-    b = call(
-        force_kernel, "force", fast(24, YE, CZ), [VM, VM] + [AN] * 4, [pltpu.VMEM((144, 128), F32), sems(14)],
-        (recv3, lists, ylo, yhi, x1lo, x1hi),
-    )
+
     pr0, target, corr1, ct, ch, out4 = call(
         body_kernel, "body",
-        (fast(22, YE, CZ), fast(20, YE, CZ), fast(18, YE, CZ), send(6, YE, CZ), send(6, YE, CZ), send(128, ROWS[2], 128)),
-        [VM] * 9, [block(24), block(20), pltpu.VMEM((7 * CY, 128), F32)],
-        (b, x3lo, x3hi, free, invd, invp, codes, table) + slow(gfold),
+        (shp(22, YE, CZ), shp(20, YE, CZ), shp(18, YE, CZ), shp(6, YE, CZ), shp(6, YE, CZ), shp(128, ROWS[2], 128)),
+        [VM] + [AN] * 12 + [VM],
+        [block(24), pltpu.VMEM((144, 128), F32), block(24), block(20), pltpu.VMEM((7 * CY, 128), F32)]
+        + [block(2, 7), block(3, CX), block(24), block(20), block(CX), pltpu.VMEM((3, 128, 128), F32), sems(15), sems(7)],
+        (recv3, xt, yb_near, yb_far, x1lo, x1hi, x3near, x3far, free, invd, invp, codes, table, gfold),
     )
     recv4 = to_all(out4)
-    cxlo, cxhi = shift(ct, "hullx", 1), shift(ch, "hullx", -1)
+    cxnear, cxfar = pair(ct, "hullx"), across(ch, "hullx")
     out5 = call(
-        coarse_kernel, "coarse", send(128, 128), [SM, VM, AN, VM],
+        coarse_kernel, "coarse", shp(128, 128), [SM, VM, AN, VM],
         [pltpu.VMEM((2, 2, 128, 128), F32), pltpu.VMEM((8, 128), F32), pltpu.SemaphoreType.DMA],
-        (cols, recv4) + slow(coarse_blocks) + (table,),
+        (cols, recv4) + (coarse_blocks,) + (table,),
     )
     recv5 = to_all(out5[:, None, :])[:, 0, :]
     vel_new, pres_new = call(
-        last_kernel, "last", (shp(3, CX, CY, CZ), shp(CX, CY, CZ)), [VM] * 11,
-        [pltpu.VMEM((128, 128), F32), block(22), block(20), block(18)],
-        (recv5, corr1, codes, cxlo, cxhi, target, invp, pr0, free, pres) + slow(glift.astype(BF16)),
+        last_kernel, "last", (shp(3, CX, CY, CZ), shp(CX, CY, CZ)),
+        [VM] + [AN] * 9 + [VM],
+        [pltpu.VMEM((128, 128), F32), block(22), block(20), block(18), block(CX + 2), block(CX), block(20), block(20)]
+        + [pltpu.VMEM((CX, CY, CZ), F32), pltpu.VMEM((2, CX, CY, CZ), F32), pltpu.VMEM((CX, CY, CZ), F32), block(2, 6), sems(9)],
+        (recv5, corr1, codes, cxnear, cxfar, target, invp, pr0, free, pressure, glift.astype(BF16)),
     )
     section_force = force.reshape(8)
     return vel_new, pres_new, section_force

time: 166 us -> 142 us (0.86)
  starting transfers between devices: 90.5 us -> 50.9 us
  blocking collectives: 0 us -> 21.8 us
  Pallas kernels: 52.1 us -> 43.9 us
  waiting for transfers between devices: 20.3 us -> 22.1 us
    all_to_all x5 -> x4, starting transfers between devices: 55.4 us -> 29.5 us  [to_all(): return lax.all_to_all(x, BOTH, 0, 0, tiled=True)]
    all_to_all x0 -> x1, blocking collectives: none -> 21.8 us  [to_all(): return lax.all_to_all(x, BOTH, 0, 0, tiled=True)]
    ppermute x13 -> x11, starting transfers between devices: 35.1 us -> 21.4 us  [the longest x4 8.68 us: across(): lax.ppermute(x, axis, [(i, j) for k in range(1, n - 1, 2) for i, j in ((k...]
    pallas_call x12 -> x10, Pallas kernels: 52.1 us -> 43.9 us  [call(): pl.pallas_call(kernel, out_shape=outs, in_specs=ins, out_specs=out_specs,...]
    all_to_all x5 -> x4, waiting for transfers between devices: 15.3 us -> 21 us  [to_all(): return lax.all_to_all(x, BOTH, 0, 0, tiled=True)]
    ppermute x13 -> x11, waiting for transfers between devices: 5.01 us -> 1.06 us  [the longest x5 1.04 us: pair(): lax.ppermute(x, axis, [(i, i ^ 1) for i in range(HX if axis == 'hullx' el...]
  transfers between devices with their start and end apart: 18 -> 15, of which waited for: 5 -> 4; matrix products, arithmetic and copies ran while one was open for 0% -> 0% of each run, Pallas kernels for 19% -> 17%
where the time goes in v3:
time: 142 us; the launch traced here: 141 us
  starting transfers between devices  50.9 us (36%)
  Pallas kernels  43.9 us (31%)
  waiting for transfers between devices  22.1 us (16%)
  blocking collectives  21.8 us (15%)
  between operations  1.47 us (1%)
    pallas_call x10, Pallas kernels, call(): pl.pallas_call(kernel, out_shape=outs, in_specs=ins, out_specs=out_specs,...  43.9 us
    all_to_all x4, starting transfers between devices, to_all(): return lax.all_to_all(x, BOTH, 0, 0, tiled=True)  29.5 us
    all_to_all x1, blocking collectives, to_all(): return lax.all_to_all(x, BOTH, 0, 0, tiled=True)  21.8 us
    all_to_all x4, waiting for transfers between devices, to_all(): return lax.all_to_all(x, BOTH, 0, 0, tiled=True)  21 us
    ppermute x4, starting transfers between devices, across(): lax.ppermute(x, axis, [(i, j) for k in range(1, n - 1, 2) for i, j in ((k...  8.68 us
    ppermute x2, starting transfers between devices, shift(): lax.ppermute(x, 'hullx', [(i, i + by) for i in range(HX) if 0 <= i + by <...  7.08 us
    ppermute x5, starting transfers between devices, pair(): lax.ppermute(x, axis, [(i, i ^ 1) for i in range(HX if axis == 'hullx' el...  5.67 us
  transfers between devices with their start and end apart: 15, of which 4 were waited for; matrix products, arithmetic and copies ran while one was open for 0% of the time, Pallas kernels for 17%

profile of v3, /device:TPU:1, one launch (start us, length us, event | category | flops | bytes accessed | tf_op | source)
XLA Modules:
  0.0 140.7 jit_solution(1615150209546824325)
XLA Ops:
  0.6 2.3 %packx.1 = (f32[18,48,128]{2,1,0:T(8,128)}, f32[18,48,128]{2,1,0:T(8,128)}) custom-call(f32[3,16,48,128]{3,2,1,0:T(8,128)} %vel.7, f32[3,16,48,128]{3,2,1,0:T(8,128)} %src.5, f32[16,48,128]{2,1,0:T(8,128)} %pres_in.1, f32[16,48,128]{2,1,0:T(8,128)} %mdiag.5, f32[16,48,128]{2,1,0:T(8,128)} %pdiag.5, s32[4,128]{1,0:T(4,128)} %bitcast.15, s32[4,128]{1,0:T(4,128)} %bitcast.16, ...), custom_call_target="tpu_custom_call" | custom-call | tf_op jit(solution)/shard_map/packx/pallas_call | solution.py:641
  2.9 1.3 collective-permute-start.2
  4.2 5.8 %collective-permute-start.1 = (f32[18,48,128]{2,1,0:T(8,128)}, f32[18,48,128]{2,1,0:T(8,128)}, u32[]{:S(2)}, u32[]{:S(2)}) collective-permute-start(f32[18,48,128]{2,1,0:T(8,128)} %get-tuple-element.35.lists), channel_id=1, source_target_pairs={{0,16},{16,32},{32,48},{48,64},{64,80},{80,96},{96,112},{1,17},{17... | collective-permute-start | bytes 1327112 | tf_op jit(solution)/shard_map/ppermute | solution.py:621
  10.0 3.2 %wake.1 = (f32[8,128]{1,0:T(8,128)}, f32[8,128]{1,0:T(8,128)}) custom-call(s32[2,16]{1,0:T(2,128)} %bitcast.13, f32[8]{0:T(128)} %chord.1, f32[8]{0:T(128)} %radius.1, f32[3,16,48,128]{3,2,1,0:T(8,128)} %vel.7, s32[1,256]{1,0:T(1,128)} %bitcast.18, s32[1,256]{1,0:T(1,128)} %bitcast.19, f32[1,256]{1,0:T(1,128)} %bitcast.20, f32[16,2,128,128]{3,2,1,0:T(8,128)} %blocks.3), custom_call_target="tpu_custom_call" | custom-call | tf_op jit(solution)/shard_map/wake/pallas_call | solution.py:641
  13.2 1.0 collective-permute-start
  14.2 1.0 collective-permute-done.got
  15.3 0.6 copy-done
  15.9 1.5 %join.1.token = f32[128,8,128]{2,1,0:T(8,128)} custom-call(f32[8,128]{1,0:T(8,128)} %get-tuple-element.30.keep, f32[8,128]{1,0:T(8,128)} %copy-done), custom_call_target="tpu_custom_call" | custom-call | tf_op jit(solution)/shard_map/join/pallas_call | solution.py:641
  17.4 11.0 %all-to-all-start = ((f32[128,8,128]{2,1,0:T(8,128)}), f32[128,8,128]{2,1,0:T(8,128)}, u32[]{:S(2)}, u32[]{:S(2)}) async-start(f32[128,8,128]{2,1,0:T(8,128)} %join.1.token), calls=%async_computation | async-start | bytes 1048576 | tf_op jit(solution)/shard_map/all_to_all | solution.py:608
  28.4 0.0 collective-permute-done.2.xhi
  28.4 3.0 %packy.1 = (f32[96,8,128]{2,1,0:T(8,128)}, f32[96,8,128]{2,1,0:T(8,128)}, f32[104,8,128]{2,1,0:T(8,128)}, f32[104,8,128]{2,1,0:T(8,128)}) custom-call(f32[3,16,48,128]{3,2,1,0:T(8,128)} %vel.7, f32[3,16,48,128]{3,2,1,0:T(8,128)} %src.5, f32[16,48,128]{2,1,0:T(8,128)} %pres_in.1, f32[16,48,128]{2,1,0:T(8,128)} %mdiag.5, f32[16,48,128]{2,1,0:T(8,128)} %pdiag.5, ...), custom_call_target="tpu_custom_call" | custom-call | tf_op jit(solution)/shard_map/packy/pallas_call | solution.py:641
  31.5 1.2 collective-permute-start.3
  32.7 2.5 %collective-permute-start.4 = (f32[104,8,128]{2,1,0:T(8,128)}, f32[104,8,128]{2,1,0:T(8,128)}, u32[]{:S(2)}, u32[]{:S(2)}) collective-permute-start(f32[104,8,128]{2,1,0:T(8,128)} %get-tuple-element.38), channel_id=1, source_target_pairs={{1,2},{2,1},{3,4},{4,3},{5,6},{6,5},{7,8},{8,7},{9,10},{10,9},{11,... | collective-permute-start | bytes 1277960 | tf_op jit(solution)/shard_map/ppermute | solution.py:617
  35.2 0.1 collective-permute-start.5
  35.3 3.5 %collective-permute-start.6 = (f32[96,8,128]{2,1,0:T(8,128)}, f32[96,8,128]{2,1,0:T(8,128)}, u32[]{:S(2)}, u32[]{:S(2)}) collective-permute-start(f32[96,8,128]{2,1,0:T(8,128)} %get-tuple-element.40), channel_id=1, source_target_pairs={{1,2},{2,1},{3,4},{4,3},{5,6},{6,5},{7,8},{8,7},{9,10},{10,9},{11,... | collective-permute-start | bytes 1179656 | tf_op jit(solution)/shard_map/ppermute | solution.py:617
  38.8 3.0 %all-to-all-done.recv = f32[128,8,128]{2,1,0:T(8,128)} async-done(((f32[128,8,128]{2,1,0:T(8,128)}), f32[128,8,128]{2,1,0:T(8,128)}, u32[]{:S(2)}, u32[]{:S(2)}) %all-to-all-start) | async-done | bytes 524320 | tf_op jit(solution)/shard_map/all_to_all | solution.py:608
  41.8 2.0 %trim1.1 = (f32[128,4,128]{2,1,0:T(4,128)}, f32[3,8,128]{2,1,0:T(8,128)}, f32[3,128,128]{2,1,0:T(8,128)}) custom-call(f32[128,8,128]{2,1,0:T(8,128)} %all-to-all-done.recv, f32[8,1024]{1,0:T(8,128)} %infl.3), custom_call_target="tpu_custom_call" | custom-call | tf_op jit(solution)/shard_map/trim1/pallas_call | solution.py:641
  43.8 8.5 %all-to-all-start.1 = ((f32[128,4,128]{2,1,0:T(4,128)}), f32[128,4,128]{2,1,0:T(4,128)}, u32[]{:S(2)}, u32[]{:S(2)}) async-start(f32[128,4,128]{2,1,0:T(4,128)} %get-tuple-element.32), calls=%async_computation.1 | async-start | bytes 524288 | tf_op jit(solution)/shard_map/all_to_all | solution.py:608
  52.4 8.8 %sweeps.1 = (f32[3,16,64,128]{3,2,1,0:T(8,128)}, f32[24,64,128]{2,1,0:T(8,128)}, f32[20,64,128]{2,1,0:T(8,128)}, f32[16,64,128]{2,1,0:T(8,128)}, f32[7,64,128]{2,1,0:T(8,128)}, /*index=5*/f32[7,64,128]{2,1,0:T(8,128)}) custom-call(f32[3,16,48,128]{3,2,1,0:T(8,128)} %vel.7, f32[3,16,48,128]{3,2,1,0:T(8,128)} %src.5, f32[16,48,128]{2,1,0:T(8,128)} %pres_in.1, ...), custom_call_target="tpu_custom_call" | custom-call | tf_op jit(solution)/shard_map/sweeps/pallas_call | solution.py:641
  61.2 1.6 %collective-permute-start.7 = (f32[7,64,128]{2,1,0:T(8,128)}, f32[7,64,128]{2,1,0:T(8,128)}, u32[]{:S(2)}, u32[]{:S(2)}) collective-permute-start(f32[7,64,128]{2,1,0:T(8,128)} %get-tuple-element.41), channel_id=1, source_target_pairs={{0,16},{16,0},{32,48},{48,32},{64,80},{80,64},{96,112},{112,96},{1... | collective-permute-start | bytes 688136 | tf_op jit(solution)/shard_map/ppermute | solution.py:612
  62.8 1.3 collective-permute-start.8
  64.8 1.8 %trim2.1 = (f32[128,1,128]{2,1,0:T(1,128)}, f32[1,8]{1,0:T(1,128)}) custom-call(f32[1]{0:T(128)S(6)} %copy.24.res, f32[128,4,128]{2,1,0:T(4,128)} %all-to-all-done.1.recv, f32[3,8,128]{2,1,0:T(8,128)} %get-tuple-element.33.state.token, f32[8,1024]{1,0:T(8,128)} %infl.3), custom_call_target="tpu_custom_call" | custom-call | tf_op jit(solution)/shard_map/trim2/pallas_call | solution.py:641
  66.6 21.8 %all_to_all.25.recv = f32[128,1,128]{2,1,0:T(1,128)} all-to-all(f32[128,1,128]{2,1,0:T(1,128)} %get-tuple-element.34), channel_id=1, replica_groups=mesh['hullx'=8,'hully'=16] {'hullx','hully'}, dimensions={0} | all-to-all | bytes 131072 | tf_op jit(solution)/shard_map/all_to_all | solution.py:608
  88.4 10.5 %body.1 = (f32[22,64,128]{2,1,0:T(8,128)}, f32[20,64,128]{2,1,0:T(8,128)}, f32[18,64,128]{2,1,0:T(8,128)}, f32[6,64,128]{2,1,0:T(8,128)}, f32[6,64,128]{2,1,0:T(8,128)}, /*index=5*/f32[128,4,128]{2,1,0:T(4,128)}) custom-call(f32[128,1,128]{2,1,0:T(1,128)} %all_to_all.25.recv, f32[18,48,128]{2,1,0:T(8,128)} %get-tuple-element.35.lists, ...), custom_call_target="tpu_custom_call" | custom-call | tf_op jit(solution)/shard_map/body/pallas_call | solution.py:641
  98.9 5.0 %all-to-all-start.3 = ((f32[128,4,128]{2,1,0:T(4,128)}), f32[128,4,128]{2,1,0:T(4,128)}, u32[]{:S(2)}, u32[]{:S(2)}) async-start(f32[128,4,128]{2,1,0:T(4,128)} %get-tuple-element.48), calls=%async_computation.3 | async-start | bytes 524288 | tf_op jit(solution)/shard_map/all_to_all | solution.py:608
  103.9 1.7 %collective-permute-start.9 = (f32[6,64,128]{2,1,0:T(8,128)}, f32[6,64,128]{2,1,0:T(8,128)}, u32[]{:S(2)}, u32[]{:S(2)}) collective-permute-start(f32[6,64,128]{2,1,0:T(8,128)} %get-tuple-element.50), channel_id=1, source_target_pairs={{0,16},{16,0},{32,48},{48,32},{64,80},{80,64},{96,112},{112,96},{1... | collective-permute-start | bytes 589832 | tf_op jit(solution)/shard_map/ppermute | solution.py:612
  105.7 1.3 collective-permute-start.10
  107.0 8.1 %all-to-all-done.3.recv = f32[128,4,128]{2,1,0:T(4,128)} async-done(((f32[128,4,128]{2,1,0:T(4,128)}), f32[128,4,128]{2,1,0:T(4,128)}, u32[]{:S(2)}, u32[]{:S(2)}) %all-to-all-start.3) | async-done | bytes 262176 | tf_op jit(solution)/shard_map/all_to_all | solution.py:608
  115.1 3.0 %coarse.1 = f32[128,128]{1,0:T(8,128)} custom-call(s32[2,16]{1,0:T(2,128)} %bitcast.14, f32[128,4,128]{2,1,0:T(4,128)} %all-to-all-done.3.recv, f32[16,2,128,128]{3,2,1,0:T(8,128)} %blocks.3, f32[3,128,128]{2,1,0:T(8,128)} %get-tuple-element.47.table_in.table), custom_call_target="tpu_custom_call" | custom-call | tf_op jit(solution)/shard_map/coarse/pallas_call | solution.py:641
  118.2 5.0 %all-to-all-start.4 = ((f32[128,1,128]{2,1,0:T(1,128)}), f32[128,1,128]{2,1,0:T(1,128)}, u32[]{:S(2)}, u32[]{:S(2)}) async-start(f32[128,1,128]{2,1,0:T(1,128)} %bitcast.12), calls=%async_computation.4 | async-start | bytes 131072 | tf_op jit(solution)/shard_map/all_to_all | solution.py:608
  123.2 9.9 %all-to-all-done.4 = f32[128,1,128]{2,1,0:T(1,128)} async-done(((f32[128,1,128]{2,1,0:T(1,128)}), f32[128,1,128]{2,1,0:T(1,128)}, u32[]{:S(2)}, u32[]{:S(2)}) %all-to-all-start.4) | async-done | bytes 65568 | tf_op jit(solution)/shard_map/all_to_all | solution.py:608
  133.0 7.7 %last.1 = (f32[3,16,48,128]{3,2,1,0:T(8,128)}, f32[16,48,128]{2,1,0:T(8,128)}) custom-call(f32[128,128]{1,0:T(8,128)} %bitcast.9.recv, f32[18,64,128]{2,1,0:T(8,128)} %get-tuple-element.49.corr1_in, f32[16,64,128]{2,1,0:T(8,128)} %get-tuple-element.46.codes_in, f32[6,64,128]{2,1,0:T(8,128)} %collective-permute-done.9.xnear, ...), custom_call_target="tpu_custom_call" | custom-call | tf_op jit(solution)/shard_map/last/pallas_call | solution.py:641
  (11 shorter events, 0.0 us)
Async XLA Ops:
  2.9 25.5 %collective-permute-start.2 = (f32[18,48,128]{2,1,0:T(8,128)}, f32[18,48,128]{2,1,0:T(8,128)}, u32[]{:S(2)}, u32[]{:S(2)}) collective-permute-start(f32[18,48,128]{2,1,0:T(8,128)} %get-tuple-element.36), channel_id=1, source_target_pairs={{16,0},{32,16},{48,32},{64,48},{80,64},{96,80},{112,96},{17,1},{33... | collective-permute-start | bytes 1327112 | tf_op jit(solution)/shard_map/ppermute | solution.py:621
  4.2 24.2 %collective-permute-start.1 = (f32[18,48,128]{2,1,0:T(8,128)}, f32[18,48,128]{2,1,0:T(8,128)}, u32[]{:S(2)}, u32[]{:S(2)}) collective-permute-start(f32[18,48,128]{2,1,0:T(8,128)} %get-tuple-element.35.lists), channel_id=1, source_target_pairs={{0,16},{16,32},{32,48},{48,64},{64,80},{80,96},{96,112},{1,17},{17... | collective-permute-start | bytes 1327112 | tf_op jit(solution)/shard_map/ppermute | solution.py:621
  13.2 2.1 %collective-permute-start = (f32[8,128]{1,0:T(8,128)}, f32[8,128]{1,0:T(8,128)S(1)}, u32[]{:S(2)}, u32[]{:S(2)}) collective-permute-start(f32[8,128]{1,0:T(8,128)} %get-tuple-element.31), channel_id=1, source_target_pairs={{0,1},{1,0},{2,3},{3,2},{4,5},{5,4},{6,7},{7,6},{8,9},{9,8},{10,11... | collective-permute-start | bytes 12296 | tf_op jit(solution)/shard_map/ppermute | solution.py:612
  15.3 0.6 copy-start
  17.4 24.4 %all-to-all-start = ((f32[128,8,128]{2,1,0:T(8,128)}), f32[128,8,128]{2,1,0:T(8,128)}, u32[]{:S(2)}, u32[]{:S(2)}) async-start(f32[128,8,128]{2,1,0:T(8,128)} %join.1.token), calls=%async_computation | async-start | bytes 1048576 | tf_op jit(solution)/shard_map/all_to_all | solution.py:608
  31.5 20.9 %collective-permute-start.3 = (f32[104,8,128]{2,1,0:T(8,128)}, f32[104,8,128]{2,1,0:T(8,128)}, u32[]{:S(2)}, u32[]{:S(2)}) collective-permute-start(f32[104,8,128]{2,1,0:T(8,128)} %get-tuple-element.37), channel_id=1, source_target_pairs={{0,1},{1,0},{2,3},{3,2},{4,5},{5,4},{6,7},{7,6},{8,9},{9,8},{10,11... | collective-permute-start | bytes 1277960 | tf_op jit(solution)/shard_map/ppermute | solution.py:612
  32.7 19.7 %collective-permute-start.4 = (f32[104,8,128]{2,1,0:T(8,128)}, f32[104,8,128]{2,1,0:T(8,128)}, u32[]{:S(2)}, u32[]{:S(2)}) collective-permute-start(f32[104,8,128]{2,1,0:T(8,128)} %get-tuple-element.38), channel_id=1, source_target_pairs={{1,2},{2,1},{3,4},{4,3},{5,6},{6,5},{7,8},{8,7},{9,10},{10,9},{11,... | collective-permute-start | bytes 1277960 | tf_op jit(solution)/shard_map/ppermute | solution.py:617
  35.2 17.1 %collective-permute-start.5 = (f32[96,8,128]{2,1,0:T(8,128)}, f32[96,8,128]{2,1,0:T(8,128)}, u32[]{:S(2)}, u32[]{:S(2)}) collective-permute-start(f32[96,8,128]{2,1,0:T(8,128)} %get-tuple-element.39), channel_id=1, source_target_pairs={{0,1},{1,0},{2,3},{3,2},{4,5},{5,4},{6,7},{7,6},{8,9},{9,8},{10,11... | collective-permute-start | bytes 1179656 | tf_op jit(solution)/shard_map/ppermute | solution.py:612
  35.3 17.0 %collective-permute-start.6 = (f32[96,8,128]{2,1,0:T(8,128)}, f32[96,8,128]{2,1,0:T(8,128)}, u32[]{:S(2)}, u32[]{:S(2)}) collective-permute-start(f32[96,8,128]{2,1,0:T(8,128)} %get-tuple-element.40), channel_id=1, source_target_pairs={{1,2},{2,1},{3,4},{4,3},{5,6},{6,5},{7,8},{8,7},{9,10},{10,9},{11,... | collective-permute-start | bytes 1179656 | tf_op jit(solution)/shard_map/ppermute | solution.py:617
  43.8 21.0 %all-to-all-start.1 = ((f32[128,4,128]{2,1,0:T(4,128)}), f32[128,4,128]{2,1,0:T(4,128)}, u32[]{:S(2)}, u32[]{:S(2)}) async-start(f32[128,4,128]{2,1,0:T(4,128)} %get-tuple-element.32), calls=%async_computation.1 | async-start | bytes 524288 | tf_op jit(solution)/shard_map/all_to_all | solution.py:608
  61.2 27.2 %collective-permute-start.7 = (f32[7,64,128]{2,1,0:T(8,128)}, f32[7,64,128]{2,1,0:T(8,128)}, u32[]{:S(2)}, u32[]{:S(2)}) collective-permute-start(f32[7,64,128]{2,1,0:T(8,128)} %get-tuple-element.41), channel_id=1, source_target_pairs={{0,16},{16,0},{32,48},{48,32},{64,80},{80,64},{96,112},{112,96},{1... | collective-permute-start | bytes 688136 | tf_op jit(solution)/shard_map/ppermute | solution.py:612
  62.8 25.6 %collective-permute-start.8 = (f32[7,64,128]{2,1,0:T(8,128)}, f32[7,64,128]{2,1,0:T(8,128)}, u32[]{:S(2)}, u32[]{:S(2)}) collective-permute-start(f32[7,64,128]{2,1,0:T(8,128)} %get-tuple-element.42), channel_id=1, source_target_pairs={{16,32},{32,16},{48,64},{64,48},{80,96},{96,80},{17,33},{33,17},{4... | collective-permute-start | bytes 688136 | tf_op jit(solution)/shard_map/ppermute | solution.py:617
  98.9 16.2 %all-to-all-start.3 = ((f32[128,4,128]{2,1,0:T(4,128)}), f32[128,4,128]{2,1,0:T(4,128)}, u32[]{:S(2)}, u32[]{:S(2)}) async-start(f32[128,4,128]{2,1,0:T(4,128)} %get-tuple-element.48), calls=%async_computation.3 | async-start | bytes 524288 | tf_op jit(solution)/shard_map/all_to_all | solution.py:608
  103.9 19.2 %collective-permute-start.9 = (f32[6,64,128]{2,1,0:T(8,128)}, f32[6,64,128]{2,1,0:T(8,128)}, u32[]{:S(2)}, u32[]{:S(2)}) collective-permute-start(f32[6,64,128]{2,1,0:T(8,128)} %get-tuple-element.50), channel_id=1, source_target_pairs={{0,16},{16,0},{32,48},{48,32},{64,80},{80,64},{96,112},{112,96},{1... | collective-permute-start | bytes 589832 | tf_op jit(solution)/shard_map/ppermute | solution.py:612
  105.7 17.5 %collective-permute-start.10 = (f32[6,64,128]{2,1,0:T(8,128)}, f32[6,64,128]{2,1,0:T(8,128)}, u32[]{:S(2)}, u32[]{:S(2)}) collective-permute-start(f32[6,64,128]{2,1,0:T(8,128)} %get-tuple-element.51), channel_id=1, source_target_pairs={{16,32},{32,16},{48,64},{64,48},{80,96},{96,80},{17,33},{33,17},{4... | collective-permute-start | bytes 589832 | tf_op jit(solution)/shard_map/ppermute | solution.py:617
  118.2 14.9 %all-to-all-start.4 = ((f32[128,1,128]{2,1,0:T(1,128)}), f32[128,1,128]{2,1,0:T(1,128)}, u32[]{:S(2)}, u32[]{:S(2)}) async-start(f32[128,1,128]{2,1,0:T(1,128)} %bitcast.12), calls=%async_computation.4 | async-start | bytes 131072 | tf_op jit(solution)/shard_map/all_to_all | solution.py:608

commit v4 on v3

--- a/solution.py
+++ b/solution.py
@@ -78,14 +78,16 @@
     return (a + b) + (c + d)
 
 
-def wake_kernel(cols, chord, radius, vel, wc, ws, ww, blocks, keep, give, row, ab, v, sem):
-    hx, hy = here()
-    copies = run([(vel.at[0], v)] + [(blocks.at[2 * hx + i, 0], ab.at[i]) for i in range(2)], sem)
+def wake_kernel(cols, chord, radius, vel, wc_in, ws_in, ww_in, blocks, keep, give, row, ab, v, wc, ws, ww, sem):
+    hx, hy = here()
+    pairs = [(wc_in, wc), (ws_in, ws), (ww_in, ww), (vel.at[0], v)]
+    copies = run(pairs + [(blocks.at[2 * hx + i, 0], ab.at[i]) for i in range(2)], sem)
+    finish_all(copies[:3])
     cells = wc[...]
     place = cells >> 7
     spot = (iota((768, 256), 0) == place).astype(BF16)
     picked = jnp.zeros((128, 256), F32)
-    copies[0].wait()
+    copies[3].wait()
     for part in split2(v[...].reshape(768, 128)):
         picked = picked + lax.dot_general(part, spot, (((0,), (0,)), ((), ())), preferred_element_type=F32)
     samples = jnp.sum(jnp.where(iota((128, 256), 0) == (cells & 127), picked, 0.0), axis=0, keepdims=True) * ww[...]
@@ -104,17 +106,13 @@
     eye = iota((128, 128), 0) == iota((128, 128), 1)
     even = (hy & 1) == 0
     first, second = row[0:4, :], row[4:8, :]
-    finish_all(copies[1:])
+    finish_all(copies[4:])
     d0 = jnp.sum(jnp.where(eye, ab[0], 0.0), axis=0, keepdims=True)
     d1 = jnp.sum(jnp.where(eye, ab[1], 0.0), axis=0, keepdims=True)
     keep[...] = jnp.concatenate([jnp.where(even, first, second), jnp.where(even, crow, rrow), d0, d1, colrow], axis=0)
     give[...] = jnp.concatenate(
         [jnp.where(even, second, first), jnp.where(even, rrow, crow), jnp.zeros((3, 128), F32)], axis=0
     )
-
-
-def join_kernel(keep, got, out):
-    out[...] = jnp.broadcast_to((keep[...] + got[...])[None], out.shape)
 
 
 def trim1_kernel(recv, infl, out, state, table, grouped):
@@ -248,16 +246,17 @@
 
 
 def sweeps_kernel(
-    vel, src, pres, mdiag, pdiag, agg, near_a, far_a, near_b, far_b, xlo, xhi, token,
-    free, invd_out, invp_out, codes_out, near, far,
-    v, s, q, invd, invp, codes, ya, yb, xb, sems,
+    vel_in, src_in, pres_in, mdiag_in, pdiag_in, agg_in, near_a, far_a, near_b, far_b, xlo, xhi, token,
+    free_out, invd_out, invp_out, codes_out, near, far,
+    v, s, q, invd, invp, codes, ya, yb, xb, vel, src, pres, mdiag, pdiag, agg, free, sems,
 ):
     hx, hy = here()
     odd = hy & 1
     finish_all(
         run(
             [(near_a, ya.at[1 - odd]), (far_a, ya.at[odd]), (near_b, yb.at[1 - odd]), (far_b, yb.at[odd])]
-            + [(xlo.at[0:HALO], xb.at[0]), (xhi.at[0:HALO], xb.at[1])],
+            + [(xlo.at[0:HALO], xb.at[0]), (xhi.at[0:HALO], xb.at[1])]
+            + [(vel_in, vel), (src_in, src), (pres_in, pres), (mdiag_in, mdiag), (pdiag_in, pdiag), (agg_in, agg)],
             sems,
         )
     )
@@ -308,7 +307,12 @@
             free[c, x] = (s[c, x + 1] + q[c, x] + q[c, x + 2] + s_yz(q[c, x + 1])) * inv
         return carry
 
-    lax.fori_loop(0, CX, second, 0, unroll=2)
+    for k in range(4):
+        lax.fori_loop(4 * k, 4 * k + 4, second, 0, unroll=2)
+        part = slice(4 * k, 4 * k + 4)
+        copy = pltpu.make_async_copy(free.at[:, part], free_out.at[:, part], sems.at[3 + k])
+        copy.start()
+        copies.append(copy)
     to = 0
     for c, w in enumerate((3, 2, 2)):
         near[to : to + w] = free[c, pl.ds((1 - (hx & 1)) * (CX - w), w)]
@@ -336,8 +340,8 @@
 
 def body_kernel(
     recv, lists, ynear, yfar, xlo, xhi, unear, ufar, free_in, invd_in, invp_in, codes_in, table_in, gfold,
-    pr0, target, corr1, near, far, send,
-    b, listed, dp, corr0, acc, x3, free, invd, invp, codes, table, early_sems, sems,
+    pr0_out, target_out, corr1_out, near, far, send,
+    pr0, target, corr1, b, listed, dp, corr0, acc, x3, free, invd, invp, codes, table, early_sems, sems,
 ):
     hx, hy = here()
     early = [(lists.at[HALO, 0:16], listed.at[0:16])]
@@ -369,8 +373,10 @@
     place = cell >> 7
     cx = (place * 43691) >> 21
     cy = place - 48 * cx
-    zv = jnp.where(iota((128, EN), 0) == cz, val, 0.0)
-    zh, zl = split2(zv)
+    vh = val.astype(BF16).astype(F32)
+    at_z = iota((128, EN), 0) == cz
+    zh = jnp.where(at_z, vh, 0.0).astype(BF16)
+    zl = jnp.where(at_z, val - vh, 0.0).astype(BF16)
     for k, (sx, sy) in enumerate(body_parts()):
         lanes = slice(k * 512, (k + 1) * 512)
         x, y = cx[:, lanes], cy[:, lanes]
@@ -418,9 +424,11 @@
 
     three(24, 4, s1)
     three(22, 3, s2)
+    results = run([(pr0, pr0_out)], early_sems)
     finish_all(copies[4:])
     three(20, 2, s3)
     three(18, 1, s4)
+    results += run([(target, target_out), (corr1, corr1_out)], sems)
 
     def s5(g, carry):
         halves, picks = [], []
@@ -430,8 +438,10 @@
             full = target[x + 2] + corr1[x] + corr1[x + 2] + s_yz(v)
             res = full[8:56] - v[8:56] / invp[x + 2, MID, :]
             code = codes[x, MID, :]
-            hi, lo = split2(jnp.concatenate([jnp.where(code == float(n + 1), res, 0.0) for n in range(7)], axis=0))
-            halves += [hi, lo]
+            high = res.astype(BF16).astype(F32)
+            for half in (high, res - high):
+                picked = [jnp.where(code == float(n + 1), half, 0.0) for n in range(7)]
+                halves.append(jnp.concatenate(picked, axis=0).astype(BF16))
             picks += [(iota((256, 128), 1) == x).astype(BF16)]
         part = mm(jnp.concatenate(halves, axis=1), jnp.concatenate(picks, axis=0))
         acc[...] = jnp.where(g == 0, part, acc[...] + part)
@@ -461,16 +471,17 @@
         at = jnp.where((at >= 0) & (at < CX), at, -1)
         wants.append((lane == at).astype(F32))
     send[...] = jnp.broadcast_to(nt(jnp.concatenate(wants, axis=1), spread, HIGH)[:, None, :], send.shape)
-
-
-def coarse_kernel(cols, recv, blocks, table, out, ab, diag, sem):
-    hx, hy = here()
-    copy = pltpu.make_async_copy(blocks.at[pl.ds(2 * hx, 2)], ab, sem)
-    copy.start()
+    finish_all(results)
+
+
+def coarse_kernel(cols, recv_in, blocks, table_in, out, ab, diag, recv, table, sem):
+    hx, hy = here()
+    copies = run([(recv_in, recv), (table_in, table), (blocks.at[pl.ds(2 * hx, 2)], ab)], sem)
     c0, c1 = cols[1, 2 * hx], cols[1, 2 * hx + 1]
     half = (0, 1, c0 & 1, c1 & 1)
     m = hx * HY + hy
     diag[...] = jnp.ones((8, 128), F32)
+    finish_all(copies[:2])
     diag[0:1, :] = table[1, pl.ds(m, 1), :]
     diag[1:2, :] = table[2, pl.ds(m, 1), :]
     for i, c in enumerate((c0, c1)):
@@ -494,7 +505,7 @@
     res = jnp.concatenate(rows + [jnp.zeros((4, 128), F32)], axis=0)
     first = 0.8 * res / diag[...]
     seconds = []
-    copy.wait()
+    copies[2].wait()
     parts = jnp.concatenate(split3(first), axis=0)
 
     def product(block, row):
@@ -523,8 +534,8 @@
 
 def last_kernel(
     recv, corr1_in, codes_in, xnear, xfar, target_in, invp_in, pr0_in, free_in, pres_in, glift,
-    vel_out, pres_out,
-    win, c2, s1, s2, corr1, codes, target, invp, pr0, free, pres, xb, sems,
+    vel_hbm, pres_hbm,
+    vel_out, pres_out, win, c2, s1, s2, corr1, codes, target, invp, pr0, free, pres, xb, sems,
 ):
     hx, hy = here()
     mid = slice(1, CX + 1)
@@ -586,7 +597,15 @@
         pres_out[x] = pres[x] + 0.7 * v[8:56]
         return carry
 
-    lax.fori_loop(0, CX, finish, 0, unroll=2)
+    results = []
+    for k in range(4):
+        lax.fori_loop(4 * k, 4 * k + 4, finish, 0, unroll=2)
+        part = slice(4 * k, 4 * k + 4)
+        for n, (src, dst) in enumerate(((vel_out.at[:, part], vel_hbm.at[:, part]), (pres_out.at[part], pres_hbm.at[part]))):
+            copy = pltpu.make_async_copy(src, dst, sems.at[2 * k + n])
+            copy.start()
+            results.append(copy)
+    finish_all(results)
 
 
 def tables():
@@ -651,11 +670,12 @@
     x1lo, x1hi = shift(xt, 1), shift(xh, -1)
 
     keep, give = call(
-        wake_kernel, "wake", (shp(8, 128),) * 2, [SM, SM, SM, AN, VM, VM, VM, AN],
-        [pltpu.VMEM((8, 128), F32), pltpu.VMEM((2, 128, 128), F32), pltpu.VMEM((CX, CY, CZ), F32), sems(3)],
+        wake_kernel, "wake", (shp(8, 128),) * 2, [SM, SM, SM] + [AN] * 5,
+        [pltpu.VMEM((8, 128), F32), pltpu.VMEM((2, 128, 128), F32), pltpu.VMEM((CX, CY, CZ), F32)]
+        + [pltpu.VMEM((1, 256), I32)] * 2 + [pltpu.VMEM((1, 256), F32), sems(6)],
         (cols, chord, radius, velocity, wake_cells[None], wake_sections[None], wake_weights[None]) + (coarse_blocks,),
     )
-    payload = call(join_kernel, "join", shp(128, 8, 128), [VM, VM], [], (keep, pair(give)))
+    payload = jnp.broadcast_to((keep + pair(give))[None], (128, 8, 128))
     recv1 = to_all(payload)
     out1, state, table = call(
         trim1_kernel, "trim1", (shp(128, ROWS[0], 128), shp(3, 8, 128), shp(3, 128, 128)), [VM, VM],
@@ -667,17 +687,20 @@
         packy_kernel, "packy", (shp(96, 8, CZ),) * 2 + (shp(104, 8, CZ),) * 2, [AN] * 10,
         [pltpu.VMEM((2, 2, CX, 8, CZ), F32), pltpu.VMEM((2, CX, 8, CZ), I32), sems(36)],
         (velocity, mom_source, pressure, mom_diag, press_diag, agglomeration, xt, x1lo, x1hi, payload),
+        (VM, VM, VM, VM),
     )
     ya_near, yb_near = pair(ya_near), pair(yb_near)
     ya_far, yb_far = across(ya_far), across(yb_far)
     free, invd, invp, codes, fxt, fxh = call(
         sweeps_kernel, "sweeps",
         (shp(3, CX, YE, CZ), shp(24, YE, CZ), shp(20, YE, CZ), shp(CX, YE, CZ)) + (shp(7, YE, CZ),) * 2,
-        [VM] * 6 + [AN] * 7,
+        [AN] * 13,
         [block(4, CX + 4), block(3, CX + 2), block(3, CX + 2), block(24), block(20), block(CX)]
-        + [pltpu.VMEM((2, 96, 8, CZ), F32), pltpu.VMEM((2, 104, 8, CZ), F32), pltpu.VMEM((2, HALO, CY, CZ), F32), sems(6)],
+        + [pltpu.VMEM((2, 96, 8, CZ), F32), pltpu.VMEM((2, 104, 8, CZ), F32), pltpu.VMEM((2, HALO, CY, CZ), F32)]
+        + [pltpu.VMEM((3, CX, CY, CZ), F32)] * 2 + [pltpu.VMEM((CX, CY, CZ), F32)] * 3
+        + [pltpu.VMEM((CX, CY, CZ), I32), block(3, CX), sems(12)],
         (velocity, mom_source, pressure, mom_diag, press_diag, agglomeration, ya_near, ya_far, yb_near, yb_far, x1lo, x1hi, state),
-        (VM, AN, AN, AN, VM, VM),
+        (AN, AN, AN, AN, VM, VM),
     )
     x3near, x3far = pair(fxt, "hullx"), across(fxh, "hullx")
 
@@ -691,24 +714,28 @@
         body_kernel, "body",
         (shp(22, YE, CZ), shp(20, YE, CZ), shp(18, YE, CZ), shp(6, YE, CZ), shp(6, YE, CZ), shp(128, ROWS[2], 128)),
         [VM] + [AN] * 12 + [VM],
-        [block(24), pltpu.VMEM((144, 128), F32), block(24), block(20), pltpu.VMEM((7 * CY, 128), F32)]
+        [block(22), block(20), block(18), block(24), pltpu.VMEM((144, 128), F32), block(24), block(20), pltpu.VMEM((7 * CY, 128), F32)]
         + [block(2, 7), block(3, CX), block(24), block(20), block(CX), pltpu.VMEM((3, 128, 128), F32), sems(15), sems(7)],
         (recv3, xt, yb_near, yb_far, x1lo, x1hi, x3near, x3far, free, invd, invp, codes, table, gfold),
+        (AN, AN, AN, VM, VM, VM),
     )
     recv4 = to_all(out4)
     cxnear, cxfar = pair(ct, "hullx"), across(ch, "hullx")
     out5 = call(
-        coarse_kernel, "coarse", shp(128, 128), [SM, VM, AN, VM],
-        [pltpu.VMEM((2, 2, 128, 128), F32), pltpu.VMEM((8, 128), F32), pltpu.SemaphoreType.DMA],
-        (cols, recv4) + (coarse_blocks,) + (table,),
+        coarse_kernel, "coarse", shp(128, 128), [SM, AN, AN, AN],
+        [pltpu.VMEM((2, 2, 128, 128), F32), pltpu.VMEM((8, 128), F32), pltpu.VMEM((128, 4, 128), F32)]
+        + [pltpu.VMEM((3, 128, 128), F32), sems(3)],
+        (cols, recv4, coarse_blocks, table),
     )
     recv5 = to_all(out5[:, None, :])[:, 0, :]
     vel_new, pres_new = call(
         last_kernel, "last", (shp(3, CX, CY, CZ), shp(CX, CY, CZ)),
         [VM] + [AN] * 9 + [VM],
-        [pltpu.VMEM((128, 128), F32), block(22), block(20), block(18), block(CX + 2), block(CX), block(20), block(20)]
+        [pltpu.VMEM((3, CX, CY, CZ), F32), pltpu.VMEM((CX, CY, CZ), F32)]
+        + [pltpu.VMEM((128, 128), F32), block(22), block(20), block(18), block(CX + 2), block(CX), block(20), block(20)]
         + [pltpu.VMEM((CX, CY, CZ), F32), pltpu.VMEM((2, CX, CY, CZ), F32), pltpu.VMEM((CX, CY, CZ), F32), block(2, 6), sems(9)],
         (recv5, corr1, codes, cxnear, cxfar, target, invp, pr0, free, pressure, glift.astype(BF16)),
+        (AN, AN),
     )
     section_force = force.reshape(8)
     return vel_new, pres_new, section_force

time: 142 us -> 145 us (1.021)
  starting transfers between devices: 50.9 us -> 56 us
  Pallas kernels: 43.9 us -> 41.1 us
    all_to_all x4, starting transfers between devices: 29.5 us -> 34.5 us  [to_all(): return lax.all_to_all(x, BOTH, 0, 0, tiled=True)]
    pallas_call x10 -> x9, Pallas kernels: 43.9 us -> 41.1 us  [call(): pl.pallas_call(kernel, out_shape=outs, in_specs=ins, out_specs=out_specs,...]
  transfers between devices with their start and end apart: 15 -> 15, of which waited for: 4 -> 5; matrix products, arithmetic and copies ran while one was open for 0% -> 1% of each run, Pallas kernels for 17% -> 15%
where the time goes in v4:
time: 145 us; the launch traced here: 144 us
  starting transfers between devices  56 us (39%)
  Pallas kernels  41.1 us (28%)
  waiting for transfers between devices  22 us (15%)
  blocking collectives  21.8 us (15%)
  between operations  1.47 us (1%)
    pallas_call x9, Pallas kernels, call(): pl.pallas_call(kernel, out_shape=outs, in_specs=ins, out_specs=out_specs,...  41.1 us
    all_to_all x4, starting transfers between devices, to_all(): return lax.all_to_all(x, BOTH, 0, 0, tiled=True)  34.5 us
    all_to_all x1, blocking collectives, to_all(): return lax.all_to_all(x, BOTH, 0, 0, tiled=True)  21.8 us
    all_to_all x4, waiting for transfers between devices, to_all(): return lax.all_to_all(x, BOTH, 0, 0, tiled=True)  20.9 us
    ppermute x4, starting transfers between devices, across(): lax.ppermute(x, axis, [(i, j) for k in range(1, n - 1, 2) for i, j in ((k...  8.84 us
    ppermute x2, starting transfers between devices, shift(): lax.ppermute(x, 'hullx', [(i, i + by) for i in range(HX) if 0 <= i + by <...  7.08 us
    ppermute x5, starting transfers between devices, pair(): lax.ppermute(x, axis, [(i, i ^ 1) for i in range(HX if axis == 'hullx' el...  5.58 us
  transfers between devices with their start and end apart: 15, of which 5 were waited for; matrix products, arithmetic and copies ran while one was open for 1% of the time, Pallas kernels for 15%

profile of v4, /device:TPU:1, one launch (start us, length us, event | category | flops | bytes accessed | tf_op | source)
XLA Modules:
  0.0 143.9 jit_solution(7109110869231172302)
XLA Ops:
  0.6 2.3 %packx.1 = (f32[18,48,128]{2,1,0:T(8,128)}, f32[18,48,128]{2,1,0:T(8,128)}) custom-call(f32[3,16,48,128]{3,2,1,0:T(8,128)} %vel_in.1, f32[3,16,48,128]{3,2,1,0:T(8,128)} %src_in.1, f32[16,48,128]{2,1,0:T(8,128)} %pres_in.3, f32[16,48,128]{2,1,0:T(8,128)} %mdiag_in.1, f32[16,48,128]{2,1,0:T(8,128)} %pdiag_in.1, s32[4,128]{1,0:T(4,128)} %bitcast.15, ...), custom_call_target="tpu_custom_call" | custom-call | tf_op jit(solution)/shard_map/packx/pallas_call | solution.py:660
  2.9 1.3 collective-permute-start.2
  4.2 5.8 %collective-permute-start.1 = (f32[18,48,128]{2,1,0:T(8,128)}, f32[18,48,128]{2,1,0:T(8,128)}, u32[]{:S(2)}, u32[]{:S(2)}) collective-permute-start(f32[18,48,128]{2,1,0:T(8,128)} %get-tuple-element.35.lists), channel_id=1, source_target_pairs={{0,16},{16,32},{32,48},{48,64},{64,80},{80,96},{96,112},{1,17},{17... | collective-permute-start | bytes 1327112 | tf_op jit(solution)/shard_map/ppermute | solution.py:640
  10.0 3.1 %wake.1 = (f32[8,128]{1,0:T(8,128)}, f32[8,128]{1,0:T(8,128)}) custom-call(s32[2,16]{1,0:T(2,128)} %bitcast.13, f32[8]{0:T(128)} %chord.1, f32[8]{0:T(128)} %radius.1, f32[3,16,48,128]{3,2,1,0:T(8,128)} %vel_in.1, s32[1,256]{1,0:T(1,128)} %bitcast.18, s32[1,256]{1,0:T(1,128)} %bitcast.19, f32[1,256]{1,0:T(1,128)} %bitcast.20, f32[16,2,128,128]{3,2,1,0:T(8,128)} %blocks.3), custom_call_target="tpu_custom_call" | custom-call | tf_op jit(solution)/shard_map/wake/pallas_call | solution.py:660
  13.1 1.0 collective-permute-start
  14.2 1.0 collective-permute-done
  15.2 0.7 add.3
  15.9 0.8 broadcast_in_dim.21.token
  16.7 11.0 %all-to-all-start = ((f32[128,8,128]{2,1,0:T(8,128)}), f32[128,8,128]{2,1,0:T(8,128)}, u32[]{:S(2)}, u32[]{:S(2)}) async-start(f32[128,8,128]{2,1,0:T(8,128)} %broadcast_in_dim.21.token), calls=%async_computation | async-start | bytes 1048576 | tf_op jit(solution)/shard_map/all_to_all | solution.py:627
  27.7 0.1 collective-permute-done.1.xlo
  27.9 3.0 %packy.1 = (f32[96,8,128]{2,1,0:T(8,128)}, f32[96,8,128]{2,1,0:T(8,128)}, f32[104,8,128]{2,1,0:T(8,128)}, f32[104,8,128]{2,1,0:T(8,128)}) custom-call(f32[3,16,48,128]{3,2,1,0:T(8,128)} %vel_in.1, f32[3,16,48,128]{3,2,1,0:T(8,128)} %src_in.1, f32[16,48,128]{2,1,0:T(8,128)} %pres_in.3, f32[16,48,128]{2,1,0:T(8,128)} %mdiag_in.1, f32[16,48,128]{2,1,0:T(8,128)} %pdiag_in.1, ...), custom_call_target="tpu_custom_call" | custom-call | tf_op jit(solution)/shard_map/packy/pallas_call | solution.py:660
  30.9 1.1 collective-permute-start.3
  32.0 2.6 %collective-permute-start.4 = (f32[104,8,128]{2,1,0:T(8,128)}, f32[104,8,128]{2,1,0:T(8,128)}, u32[]{:S(2)}, u32[]{:S(2)}) collective-permute-start(f32[104,8,128]{2,1,0:T(8,128)} %get-tuple-element.38), channel_id=1, source_target_pairs={{1,2},{2,1},{3,4},{4,3},{5,6},{6,5},{7,8},{8,7},{9,10},{10,9},{11,... | collective-permute-start | bytes 1277960 | tf_op jit(solution)/shard_map/ppermute | solution.py:636
  34.6 0.1 collective-permute-start.5
  34.7 3.6 %collective-permute-start.6 = (f32[96,8,128]{2,1,0:T(8,128)}, f32[96,8,128]{2,1,0:T(8,128)}, u32[]{:S(2)}, u32[]{:S(2)}) collective-permute-start(f32[96,8,128]{2,1,0:T(8,128)} %get-tuple-element.40), channel_id=1, source_target_pairs={{1,2},{2,1},{3,4},{4,3},{5,6},{6,5},{7,8},{8,7},{9,10},{10,9},{11,... | collective-permute-start | bytes 1179656 | tf_op jit(solution)/shard_map/ppermute | solution.py:636
  38.3 2.9 %all-to-all-done.recv = f32[128,8,128]{2,1,0:T(8,128)} async-done(((f32[128,8,128]{2,1,0:T(8,128)}), f32[128,8,128]{2,1,0:T(8,128)}, u32[]{:S(2)}, u32[]{:S(2)}) %all-to-all-start) | async-done | bytes 524320 | tf_op jit(solution)/shard_map/all_to_all | solution.py:627
  41.1 2.0 %trim1.1 = (f32[128,4,128]{2,1,0:T(4,128)}, f32[3,8,128]{2,1,0:T(8,128)}, f32[3,128,128]{2,1,0:T(8,128)}) custom-call(f32[128,8,128]{2,1,0:T(8,128)} %all-to-all-done.recv, f32[8,1024]{1,0:T(8,128)} %infl.3), custom_call_target="tpu_custom_call" | custom-call | tf_op jit(solution)/shard_map/trim1/pallas_call | solution.py:660
  43.2 13.6 %all-to-all-start.1 = ((f32[128,4,128]{2,1,0:T(4,128)}), f32[128,4,128]{2,1,0:T(4,128)}, u32[]{:S(2)}, u32[]{:S(2)}) async-start(f32[128,4,128]{2,1,0:T(4,128)} %get-tuple-element.32), calls=%async_computation.1 | async-start | bytes 524288 | tf_op jit(solution)/shard_map/all_to_all | solution.py:627
  56.8 8.3 %sweeps.1 = (f32[3,16,64,128]{3,2,1,0:T(8,128)}, f32[24,64,128]{2,1,0:T(8,128)}, f32[20,64,128]{2,1,0:T(8,128)}, f32[16,64,128]{2,1,0:T(8,128)}, f32[7,64,128]{2,1,0:T(8,128)}, /*index=5*/f32[7,64,128]{2,1,0:T(8,128)}) custom-call(f32[3,16,48,128]{3,2,1,0:T(8,128)} %vel_in.1, f32[3,16,48,128]{3,2,1,0:T(8,128)} %src_in.1, f32[16,48,128]{2,1,0:T(8,128)} %pres_in.3, ...), custom_call_target="tpu_custom_call" | custom-call | tf_op jit(solution)/shard_map/sweeps/pallas_call | solution.py:660
  65.0 1.6 %collective-permute-start.7 = (f32[7,64,128]{2,1,0:T(8,128)}, f32[7,64,128]{2,1,0:T(8,128)}, u32[]{:S(2)}, u32[]{:S(2)}) collective-permute-start(f32[7,64,128]{2,1,0:T(8,128)} %get-tuple-element.41), channel_id=1, source_target_pairs={{0,16},{16,0},{32,48},{48,32},{64,80},{80,64},{96,112},{112,96},{1... | collective-permute-start | bytes 688136 | tf_op jit(solution)/shard_map/ppermute | solution.py:631
  66.6 1.3 collective-permute-start.8
  68.6 1.8 %trim2.1 = (f32[128,1,128]{2,1,0:T(1,128)}, f32[1,8]{1,0:T(1,128)}) custom-call(f32[1]{0:T(128)S(6)} %copy.24.res, f32[128,4,128]{2,1,0:T(4,128)} %all-to-all-done.1.recv, f32[3,8,128]{2,1,0:T(8,128)} %get-tuple-element.33.state.token, f32[8,1024]{1,0:T(8,128)} %infl.3), custom_call_target="tpu_custom_call" | custom-call | tf_op jit(solution)/shard_map/trim2/pallas_call | solution.py:660
  70.5 21.8 %all_to_all.25.recv = f32[128,1,128]{2,1,0:T(1,128)} all-to-all(f32[128,1,128]{2,1,0:T(1,128)} %get-tuple-element.34), channel_id=1, replica_groups=mesh['hullx'=8,'hully'=16] {'hullx','hully'}, dimensions={0} | all-to-all | bytes 131072 | tf_op jit(solution)/shard_map/all_to_all | solution.py:627
  92.2 10.3 %body.1 = (f32[22,64,128]{2,1,0:T(8,128)}, f32[20,64,128]{2,1,0:T(8,128)}, f32[18,64,128]{2,1,0:T(8,128)}, f32[6,64,128]{2,1,0:T(8,128)}, f32[6,64,128]{2,1,0:T(8,128)}, /*index=5*/f32[128,4,128]{2,1,0:T(4,128)}) custom-call(f32[128,1,128]{2,1,0:T(1,128)} %all_to_all.25.recv, f32[18,48,128]{2,1,0:T(8,128)} %get-tuple-element.35.lists, ...), custom_call_target="tpu_custom_call" | custom-call | tf_op jit(solution)/shard_map/body/pallas_call | solution.py:660
  102.5 5.0 %all-to-all-start.3 = ((f32[128,4,128]{2,1,0:T(4,128)}), f32[128,4,128]{2,1,0:T(4,128)}, u32[]{:S(2)}, u32[]{:S(2)}) async-start(f32[128,4,128]{2,1,0:T(4,128)} %get-tuple-element.48), calls=%async_computation.3 | async-start | bytes 524288 | tf_op jit(solution)/shard_map/all_to_all | solution.py:627
  107.5 1.7 %collective-permute-start.9 = (f32[6,64,128]{2,1,0:T(8,128)}, f32[6,64,128]{2,1,0:T(8,128)}, u32[]{:S(2)}, u32[]{:S(2)}) collective-permute-start(f32[6,64,128]{2,1,0:T(8,128)} %get-tuple-element.50), channel_id=1, source_target_pairs={{0,16},{16,0},{32,48},{48,32},{64,80},{80,64},{96,112},{112,96},{1... | collective-permute-start | bytes 589832 | tf_op jit(solution)/shard_map/ppermute | solution.py:631
  109.2 1.3 collective-permute-start.10
  110.6 8.1 %all-to-all-done.3.recv_in = f32[128,4,128]{2,1,0:T(4,128)} async-done(((f32[128,4,128]{2,1,0:T(4,128)}), f32[128,4,128]{2,1,0:T(4,128)}, u32[]{:S(2)}, u32[]{:S(2)}) %all-to-all-start.3) | async-done | bytes 262176 | tf_op jit(solution)/shard_map/all_to_all | solution.py:627
  118.7 3.0 %coarse.1 = f32[128,128]{1,0:T(8,128)} custom-call(s32[2,16]{1,0:T(2,128)} %bitcast.14, f32[128,4,128]{2,1,0:T(4,128)} %all-to-all-done.3.recv_in, f32[16,2,128,128]{3,2,1,0:T(8,128)} %blocks.3, f32[3,128,128]{2,1,0:T(8,128)} %get-tuple-element.47.table_in), custom_call_target="tpu_custom_call" | custom-call | tf_op jit(solution)/shard_map/coarse/pallas_call | solution.py:660
  121.8 5.0 %all-to-all-start.4 = ((f32[128,1,128]{2,1,0:T(1,128)}), f32[128,1,128]{2,1,0:T(1,128)}, u32[]{:S(2)}, u32[]{:S(2)}) async-start(f32[128,1,128]{2,1,0:T(1,128)} %bitcast.12), calls=%async_computation.4 | async-start | bytes 131072 | tf_op jit(solution)/shard_map/all_to_all | solution.py:627
  126.8 9.9 %all-to-all-done.4 = f32[128,1,128]{2,1,0:T(1,128)} async-done(((f32[128,1,128]{2,1,0:T(1,128)}), f32[128,1,128]{2,1,0:T(1,128)}, u32[]{:S(2)}, u32[]{:S(2)}) %all-to-all-start.4) | async-done | bytes 65568 | tf_op jit(solution)/shard_map/all_to_all | solution.py:627
  136.6 7.3 %last.1 = (f32[3,16,48,128]{3,2,1,0:T(8,128)}, f32[16,48,128]{2,1,0:T(8,128)}) custom-call(f32[128,128]{1,0:T(8,128)} %bitcast.9.recv, f32[18,64,128]{2,1,0:T(8,128)} %get-tuple-element.49.corr1_in, f32[16,64,128]{2,1,0:T(8,128)} %get-tuple-element.46.codes_in, f32[6,64,128]{2,1,0:T(8,128)} %collective-permute-done.9.xnear, ...), custom_call_target="tpu_custom_call" | custom-call | tf_op jit(solution)/shard_map/last/pallas_call | solution.py:660
  (10 shorter events, 0.0 us)
Async XLA Ops:
  2.9 24.8 %collective-permute-start.2 = (f32[18,48,128]{2,1,0:T(8,128)}, f32[18,48,128]{2,1,0:T(8,128)}, u32[]{:S(2)}, u32[]{:S(2)}) collective-permute-start(f32[18,48,128]{2,1,0:T(8,128)} %get-tuple-element.36), channel_id=1, source_target_pairs={{16,0},{32,16},{48,32},{64,48},{80,64},{96,80},{112,96},{17,1},{33... | collective-permute-start | bytes 1327112 | tf_op jit(solution)/shard_map/ppermute | solution.py:640
  4.2 23.6 %collective-permute-start.1 = (f32[18,48,128]{2,1,0:T(8,128)}, f32[18,48,128]{2,1,0:T(8,128)}, u32[]{:S(2)}, u32[]{:S(2)}) collective-permute-start(f32[18,48,128]{2,1,0:T(8,128)} %get-tuple-element.35.lists), channel_id=1, source_target_pairs={{0,16},{16,32},{32,48},{48,64},{64,80},{80,96},{96,112},{1,17},{17... | collective-permute-start | bytes 1327112 | tf_op jit(solution)/shard_map/ppermute | solution.py:640
  13.1 2.1 %collective-permute-start = (f32[8,128]{1,0:T(8,128)}, f32[8,128]{1,0:T(8,128)S(1)}, u32[]{:S(2)}, u32[]{:S(2)}) collective-permute-start(f32[8,128]{1,0:T(8,128)} %get-tuple-element.31), channel_id=1, source_target_pairs={{0,1},{1,0},{2,3},{3,2},{4,5},{5,4},{6,7},{7,6},{8,9},{9,8},{10,11... | collective-permute-start | bytes 12296 | tf_op jit(solution)/shard_map/ppermute | solution.py:631
  16.7 24.4 %all-to-all-start = ((f32[128,8,128]{2,1,0:T(8,128)}), f32[128,8,128]{2,1,0:T(8,128)}, u32[]{:S(2)}, u32[]{:S(2)}) async-start(f32[128,8,128]{2,1,0:T(8,128)} %broadcast_in_dim.21.token), calls=%async_computation | async-start | bytes 1048576 | tf_op jit(solution)/shard_map/all_to_all | solution.py:627
  30.9 25.9 %collective-permute-start.3 = (f32[104,8,128]{2,1,0:T(8,128)}, f32[104,8,128]{2,1,0:T(8,128)}, u32[]{:S(2)}, u32[]{:S(2)}) collective-permute-start(f32[104,8,128]{2,1,0:T(8,128)} %get-tuple-element.37), channel_id=1, source_target_pairs={{0,1},{1,0},{2,3},{3,2},{4,5},{5,4},{6,7},{7,6},{8,9},{9,8},{10,11... | collective-permute-start | bytes 1277960 | tf_op jit(solution)/shard_map/ppermute | solution.py:631
  32.0 24.8 %collective-permute-start.4 = (f32[104,8,128]{2,1,0:T(8,128)}, f32[104,8,128]{2,1,0:T(8,128)}, u32[]{:S(2)}, u32[]{:S(2)}) collective-permute-start(f32[104,8,128]{2,1,0:T(8,128)} %get-tuple-element.38), channel_id=1, source_target_pairs={{1,2},{2,1},{3,4},{4,3},{5,6},{6,5},{7,8},{8,7},{9,10},{10,9},{11,... | collective-permute-start | bytes 1277960 | tf_op jit(solution)/shard_map/ppermute | solution.py:636
  34.6 22.1 %collective-permute-start.5 = (f32[96,8,128]{2,1,0:T(8,128)}, f32[96,8,128]{2,1,0:T(8,128)}, u32[]{:S(2)}, u32[]{:S(2)}) collective-permute-start(f32[96,8,128]{2,1,0:T(8,128)} %get-tuple-element.39), channel_id=1, source_target_pairs={{0,1},{1,0},{2,3},{3,2},{4,5},{5,4},{6,7},{7,6},{8,9},{9,8},{10,11... | collective-permute-start | bytes 1179656 | tf_op jit(solution)/shard_map/ppermute | solution.py:631
  34.7 22.1 %collective-permute-start.6 = (f32[96,8,128]{2,1,0:T(8,128)}, f32[96,8,128]{2,1,0:T(8,128)}, u32[]{:S(2)}, u32[]{:S(2)}) collective-permute-start(f32[96,8,128]{2,1,0:T(8,128)} %get-tuple-element.40), channel_id=1, source_target_pairs={{1,2},{2,1},{3,4},{4,3},{5,6},{6,5},{7,8},{8,7},{9,10},{10,9},{11,... | collective-permute-start | bytes 1179656 | tf_op jit(solution)/shard_map/ppermute | solution.py:636
  43.2 25.5 %all-to-all-start.1 = ((f32[128,4,128]{2,1,0:T(4,128)}), f32[128,4,128]{2,1,0:T(4,128)}, u32[]{:S(2)}, u32[]{:S(2)}) async-start(f32[128,4,128]{2,1,0:T(4,128)} %get-tuple-element.32), calls=%async_computation.1 | async-start | bytes 524288 | tf_op jit(solution)/shard_map/all_to_all | solution.py:627
  65.0 27.2 %collective-permute-start.7 = (f32[7,64,128]{2,1,0:T(8,128)}, f32[7,64,128]{2,1,0:T(8,128)}, u32[]{:S(2)}, u32[]{:S(2)}) collective-permute-start(f32[7,64,128]{2,1,0:T(8,128)} %get-tuple-element.41), channel_id=1, source_target_pairs={{0,16},{16,0},{32,48},{48,32},{64,80},{80,64},{96,112},{112,96},{1... | collective-permute-start | bytes 688136 | tf_op jit(solution)/shard_map/ppermute | solution.py:631
  66.6 25.6 %collective-permute-start.8 = (f32[7,64,128]{2,1,0:T(8,128)}, f32[7,64,128]{2,1,0:T(8,128)}, u32[]{:S(2)}, u32[]{:S(2)}) collective-permute-start(f32[7,64,128]{2,1,0:T(8,128)} %get-tuple-element.42), channel_id=1, source_target_pairs={{16,32},{32,16},{48,64},{64,48},{80,96},{96,80},{17,33},{33,17},{4... | collective-permute-start | bytes 688136 | tf_op jit(solution)/shard_map/ppermute | solution.py:636
  102.5 16.2 %all-to-all-start.3 = ((f32[128,4,128]{2,1,0:T(4,128)}), f32[128,4,128]{2,1,0:T(4,128)}, u32[]{:S(2)}, u32[]{:S(2)}) async-start(f32[128,4,128]{2,1,0:T(4,128)} %get-tuple-element.48), calls=%async_computation.3 | async-start | bytes 524288 | tf_op jit(solution)/shard_map/all_to_all | solution.py:627
  107.5 19.2 %collective-permute-start.9 = (f32[6,64,128]{2,1,0:T(8,128)}, f32[6,64,128]{2,1,0:T(8,128)}, u32[]{:S(2)}, u32[]{:S(2)}) collective-permute-start(f32[6,64,128]{2,1,0:T(8,128)} %get-tuple-element.50), channel_id=1, source_target_pairs={{0,16},{16,0},{32,48},{48,32},{64,80},{80,64},{96,112},{112,96},{1... | collective-permute-start | bytes 589832 | tf_op jit(solution)/shard_map/ppermute | solution.py:631
  109.2 17.5 %collective-permute-start.10 = (f32[6,64,128]{2,1,0:T(8,128)}, f32[6,64,128]{2,1,0:T(8,128)}, u32[]{:S(2)}, u32[]{:S(2)}) collective-permute-start(f32[6,64,128]{2,1,0:T(8,128)} %get-tuple-element.51), channel_id=1, source_target_pairs={{16,32},{32,16},{48,64},{64,48},{80,96},{96,80},{17,33},{33,17},{4... | collective-permute-start | bytes 589832 | tf_op jit(solution)/shard_map/ppermute | solution.py:636
  121.8 14.9 %all-to-all-start.4 = ((f32[128,1,128]{2,1,0:T(1,128)}), f32[128,1,128]{2,1,0:T(1,128)}, u32[]{:S(2)}, u32[]{:S(2)}) async-start(f32[128,1,128]{2,1,0:T(1,128)} %bitcast.12), calls=%async_computation.4 | async-start | bytes 131072 | tf_op jit(solution)/shard_map/all_to_all | solution.py:627

commit v5 on v4

--- a/solution.py
+++ b/solution.py
@@ -115,6 +115,10 @@
     )
 
 
+def join_kernel(keep, got, out):
+    out[...] = jnp.broadcast_to((keep[...] + got[...])[None], out.shape)
+
+
 def trim1_kernel(recv, infl, out, state, table, grouped):
     hx, hy = here()
     by_core = recv[...].reshape(HX, HY // 2, 2, 8, 128)
@@ -284,7 +288,7 @@
         codes[x] = widen(ylo[48 + x], (agg[x] - base + 4).astype(F32), yhi[48 + x])
         return carry
 
-    lax.fori_loop(0, CX, grow, 0, unroll=2)
+    lax.fori_loop(0, CX, grow, 0, unroll=4)
 
     copies = run([(invd, invd_out), (invp, invp_out), (codes, codes_out)], sems)
 
@@ -299,7 +303,7 @@
             q[c, i] = (sc + v[c, i] + v[c, i + 2] + s_yz(v[c, i + 1])) * inv
         return carry
 
-    lax.fori_loop(0, CX + 2, first, 0, unroll=2)
+    lax.fori_loop(0, CX + 2, first, 0, unroll=3)
 
     def second(x, carry):
         inv = invd[x + 4]
@@ -308,7 +312,7 @@
         return carry
 
     for k in range(4):
-        lax.fori_loop(4 * k, 4 * k + 4, second, 0, unroll=2)
+        lax.fori_loop(4 * k, 4 * k + 4, second, 0, unroll=4)
         part = slice(4 * k, 4 * k + 4)
         copy = pltpu.make_async_copy(free.at[:, part], free_out.at[:, part], sems.at[3 + k])
         copy.start()
@@ -333,7 +337,7 @@
         fn(j + w, 1, j)
         return carry
 
-    lax.fori_loop(0, CX, own, 0, unroll=4)
+    lax.fori_loop(0, CX, own, 0, unroll=8)
     for i in range(n - CX - w):
         fn(CX + w + i, 2, i)
 
@@ -599,7 +603,7 @@
 
     results = []
     for k in range(4):
-        lax.fori_loop(4 * k, 4 * k + 4, finish, 0, unroll=2)
+        lax.fori_loop(4 * k, 4 * k + 4, finish, 0, unroll=4)
         part = slice(4 * k, 4 * k + 4)
         for n, (src, dst) in enumerate(((vel_out.at[:, part], vel_hbm.at[:, part]), (pres_out.at[part], pres_hbm.at[part]))):
             copy = pltpu.make_async_copy(src, dst, sems.at[2 * k + n])
@@ -675,7 +679,7 @@
         + [pltpu.VMEM((1, 256), I32)] * 2 + [pltpu.VMEM((1, 256), F32), sems(6)],
         (cols, chord, radius, velocity, wake_cells[None], wake_sections[None], wake_weights[None]) + (coarse_blocks,),
     )
-    payload = jnp.broadcast_to((keep + pair(give))[None], (128, 8, 128))
+    payload = call(join_kernel, "join", shp(128, 8, 128), [VM, VM], [], (keep, pair(give)))
     recv1 = to_all(payload)
     out1, state, table = call(
         trim1_kernel, "trim1", (shp(128, ROWS[0], 128), shp(3, 8, 128), shp(3, 128, 128)), [VM, VM],
@@ -687,7 +691,6 @@
         packy_kernel, "packy", (shp(96, 8, CZ),) * 2 + (shp(104, 8, CZ),) * 2, [AN] * 10,
         [pltpu.VMEM((2, 2, CX, 8, CZ), F32), pltpu.VMEM((2, CX, 8, CZ), I32), sems(36)],
         (velocity, mom_source, pressure, mom_diag, press_diag, agglomeration, xt, x1lo, x1hi, payload),
-        (VM, VM, VM, VM),
     )
     ya_near, yb_near = pair(ya_near), pair(yb_near)
     ya_far, yb_far = across(ya_far), across(yb_far)

time: 145 us -> 140 us (0.966)
  starting transfers between devices: 56 us -> 52.4 us
    all_to_all x4, starting transfers between devices: 34.5 us -> 31 us  [to_all(): return lax.all_to_all(x, BOTH, 0, 0, tiled=True)]
    pallas_call x9 -> x10, Pallas kernels: 41.1 us -> 40.5 us  [call(): pl.pallas_call(kernel, out_shape=outs, in_specs=ins, out_specs=out_specs,...]
  transfers between devices with their start and end apart: 15 -> 15, of which waited for: 5 -> 4; matrix products, arithmetic and copies ran while one was open for 1% -> 0% of each run, Pallas kernels for 15% -> 16%
where the time goes in v5:
time: 140 us; the launch traced here: 139 us
  starting transfers between devices  52.4 us (37%)
  Pallas kernels  40.5 us (29%)
  waiting for transfers between devices  22.1 us (16%)
  blocking collectives  21.8 us (16%)
  between operations  1.47 us (1%)
    pallas_call x10, Pallas kernels, call(): pl.pallas_call(kernel, out_shape=outs, in_specs=ins, out_specs=out_specs,...  40.5 us
    all_to_all x4, starting transfers between devices, to_all(): return lax.all_to_all(x, BOTH, 0, 0, tiled=True)  31 us
    all_to_all x1, blocking collectives, to_all(): return lax.all_to_all(x, BOTH, 0, 0, tiled=True)  21.8 us
    all_to_all x4, waiting for transfers between devices, to_all(): return lax.all_to_all(x, BOTH, 0, 0, tiled=True)  21 us
    ppermute x4, starting transfers between devices, across(): lax.ppermute(x, axis, [(i, j) for k in range(1, n - 1, 2) for i, j in ((k...  8.68 us
    ppermute x2, starting transfers between devices, shift(): lax.ppermute(x, 'hullx', [(i, i + by) for i in range(HX) if 0 <= i + by <...  7.08 us
    ppermute x5, starting transfers between devices, pair(): lax.ppermute(x, axis, [(i, i ^ 1) for i in range(HX if axis == 'hullx' el...  5.66 us
  transfers between devices with their start and end apart: 15, of which 4 were waited for; matrix products, arithmetic and copies ran while one was open for 0% of the time, Pallas kernels for 16%

profile of v5, /device:TPU:1, one launch (start us, length us, event | category | flops | bytes accessed | tf_op | source)
XLA Modules:
  0.0 138.8 jit_solution(6200162952300617406)
XLA Ops:
  0.6 2.3 %packx.1 = (f32[18,48,128]{2,1,0:T(8,128)}, f32[18,48,128]{2,1,0:T(8,128)}) custom-call(f32[3,16,48,128]{3,2,1,0:T(8,128)} %vel_in.1, f32[3,16,48,128]{3,2,1,0:T(8,128)} %src_in.1, f32[16,48,128]{2,1,0:T(8,128)} %pres_in.3, f32[16,48,128]{2,1,0:T(8,128)} %mdiag_in.1, f32[16,48,128]{2,1,0:T(8,128)} %pdiag_in.1, s32[4,128]{1,0:T(4,128)} %bitcast.15, ...), custom_call_target="tpu_custom_call" | custom-call | tf_op jit(solution)/shard_map/packx/pallas_call | solution.py:664
  2.9 1.3 collective-permute-start.2
  4.2 5.8 %collective-permute-start.1 = (f32[18,48,128]{2,1,0:T(8,128)}, f32[18,48,128]{2,1,0:T(8,128)}, u32[]{:S(2)}, u32[]{:S(2)}) collective-permute-start(f32[18,48,128]{2,1,0:T(8,128)} %get-tuple-element.35.lists), channel_id=1, source_target_pairs={{0,16},{16,32},{32,48},{48,64},{64,80},{80,96},{96,112},{1,17},{17... | collective-permute-start | bytes 1327112 | tf_op jit(solution)/shard_map/ppermute | solution.py:644
  10.0 3.1 %wake.1 = (f32[8,128]{1,0:T(8,128)}, f32[8,128]{1,0:T(8,128)}) custom-call(s32[2,16]{1,0:T(2,128)} %bitcast.13, f32[8]{0:T(128)} %chord.1, f32[8]{0:T(128)} %radius.1, f32[3,16,48,128]{3,2,1,0:T(8,128)} %vel_in.1, s32[1,256]{1,0:T(1,128)} %bitcast.18, s32[1,256]{1,0:T(1,128)} %bitcast.19, f32[1,256]{1,0:T(1,128)} %bitcast.20, f32[16,2,128,128]{3,2,1,0:T(8,128)} %blocks.3), custom_call_target="tpu_custom_call" | custom-call | tf_op jit(solution)/shard_map/wake/pallas_call | solution.py:664
  13.1 1.0 collective-permute-start
  14.2 1.0 collective-permute-done.got
  15.2 0.6 copy-done
  15.8 1.5 %join.1.token = f32[128,8,128]{2,1,0:T(8,128)} custom-call(f32[8,128]{1,0:T(8,128)} %get-tuple-element.30.keep, f32[8,128]{1,0:T(8,128)} %copy-done), custom_call_target="tpu_custom_call" | custom-call | tf_op jit(solution)/shard_map/join/pallas_call | solution.py:664
  17.3 11.0 %all-to-all-start = ((f32[128,8,128]{2,1,0:T(8,128)}), f32[128,8,128]{2,1,0:T(8,128)}, u32[]{:S(2)}, u32[]{:S(2)}) async-start(f32[128,8,128]{2,1,0:T(8,128)} %join.1.token), calls=%async_computation | async-start | bytes 1048576 | tf_op jit(solution)/shard_map/all_to_all | solution.py:631
  28.3 0.0 collective-permute-done.1.xlo
  28.4 3.0 %packy.1 = (f32[96,8,128]{2,1,0:T(8,128)}, f32[96,8,128]{2,1,0:T(8,128)}, f32[104,8,128]{2,1,0:T(8,128)}, f32[104,8,128]{2,1,0:T(8,128)}) custom-call(f32[3,16,48,128]{3,2,1,0:T(8,128)} %vel_in.1, f32[3,16,48,128]{3,2,1,0:T(8,128)} %src_in.1, f32[16,48,128]{2,1,0:T(8,128)} %pres_in.3, f32[16,48,128]{2,1,0:T(8,128)} %mdiag_in.1, f32[16,48,128]{2,1,0:T(8,128)} %pdiag_in.1, ...), custom_call_target="tpu_custom_call" | custom-call | tf_op jit(solution)/shard_map/packy/pallas_call | solution.py:664
  31.4 1.2 collective-permute-start.3
  32.6 2.5 %collective-permute-start.4 = (f32[104,8,128]{2,1,0:T(8,128)}, f32[104,8,128]{2,1,0:T(8,128)}, u32[]{:S(2)}, u32[]{:S(2)}) collective-permute-start(f32[104,8,128]{2,1,0:T(8,128)} %get-tuple-element.38), channel_id=1, source_target_pairs={{1,2},{2,1},{3,4},{4,3},{5,6},{6,5},{7,8},{8,7},{9,10},{10,9},{11,... | collective-permute-start | bytes 1277960 | tf_op jit(solution)/shard_map/ppermute | solution.py:640
  35.2 0.1 collective-permute-start.5
  35.3 3.5 %collective-permute-start.6 = (f32[96,8,128]{2,1,0:T(8,128)}, f32[96,8,128]{2,1,0:T(8,128)}, u32[]{:S(2)}, u32[]{:S(2)}) collective-permute-start(f32[96,8,128]{2,1,0:T(8,128)} %get-tuple-element.40), channel_id=1, source_target_pairs={{1,2},{2,1},{3,4},{4,3},{5,6},{6,5},{7,8},{8,7},{9,10},{10,9},{11,... | collective-permute-start | bytes 1179656 | tf_op jit(solution)/shard_map/ppermute | solution.py:640
  38.7 3.0 %all-to-all-done.recv = f32[128,8,128]{2,1,0:T(8,128)} async-done(((f32[128,8,128]{2,1,0:T(8,128)}), f32[128,8,128]{2,1,0:T(8,128)}, u32[]{:S(2)}, u32[]{:S(2)}) %all-to-all-start) | async-done | bytes 524320 | tf_op jit(solution)/shard_map/all_to_all | solution.py:631
  41.7 2.0 %trim1.1 = (f32[128,4,128]{2,1,0:T(4,128)}, f32[3,8,128]{2,1,0:T(8,128)}, f32[3,128,128]{2,1,0:T(8,128)}) custom-call(f32[128,8,128]{2,1,0:T(8,128)} %all-to-all-done.recv, f32[8,1024]{1,0:T(8,128)} %infl.3), custom_call_target="tpu_custom_call" | custom-call | tf_op jit(solution)/shard_map/trim1/pallas_call | solution.py:664
  43.7 10.0 %all-to-all-start.1 = ((f32[128,4,128]{2,1,0:T(4,128)}), f32[128,4,128]{2,1,0:T(4,128)}, u32[]{:S(2)}, u32[]{:S(2)}) async-start(f32[128,4,128]{2,1,0:T(4,128)} %get-tuple-element.32), calls=%async_computation.1 | async-start | bytes 524288 | tf_op jit(solution)/shard_map/all_to_all | solution.py:631
  53.8 7.5 %sweeps.1 = (f32[3,16,64,128]{3,2,1,0:T(8,128)}, f32[24,64,128]{2,1,0:T(8,128)}, f32[20,64,128]{2,1,0:T(8,128)}, f32[16,64,128]{2,1,0:T(8,128)}, f32[7,64,128]{2,1,0:T(8,128)}, /*index=5*/f32[7,64,128]{2,1,0:T(8,128)}) custom-call(f32[3,16,48,128]{3,2,1,0:T(8,128)} %vel_in.1, f32[3,16,48,128]{3,2,1,0:T(8,128)} %src_in.1, f32[16,48,128]{2,1,0:T(8,128)} %pres_in.3, ...), custom_call_target="tpu_custom_call" | custom-call | tf_op jit(solution)/shard_map/sweeps/pallas_call | solution.py:664
  61.3 1.6 %collective-permute-start.7 = (f32[7,64,128]{2,1,0:T(8,128)}, f32[7,64,128]{2,1,0:T(8,128)}, u32[]{:S(2)}, u32[]{:S(2)}) collective-permute-start(f32[7,64,128]{2,1,0:T(8,128)} %get-tuple-element.41), channel_id=1, source_target_pairs={{0,16},{16,0},{32,48},{48,32},{64,80},{80,64},{96,112},{112,96},{1... | collective-permute-start | bytes 688136 | tf_op jit(solution)/shard_map/ppermute | solution.py:635
  62.9 1.3 collective-permute-start.8
  64.9 1.8 %trim2.1 = (f32[128,1,128]{2,1,0:T(1,128)}, f32[1,8]{1,0:T(1,128)}) custom-call(f32[1]{0:T(128)S(6)} %copy.24.res, f32[128,4,128]{2,1,0:T(4,128)} %all-to-all-done.1.recv, f32[3,8,128]{2,1,0:T(8,128)} %get-tuple-element.33.state.token, f32[8,1024]{1,0:T(8,128)} %infl.3), custom_call_target="tpu_custom_call" | custom-call | tf_op jit(solution)/shard_map/trim2/pallas_call | solution.py:664
  66.7 21.8 %all_to_all.25.recv = f32[128,1,128]{2,1,0:T(1,128)} all-to-all(f32[128,1,128]{2,1,0:T(1,128)} %get-tuple-element.34), channel_id=1, replica_groups=mesh['hullx'=8,'hully'=16] {'hullx','hully'}, dimensions={0} | all-to-all | bytes 131072 | tf_op jit(solution)/shard_map/all_to_all | solution.py:631
  88.5 9.9 %body.1 = (f32[22,64,128]{2,1,0:T(8,128)}, f32[20,64,128]{2,1,0:T(8,128)}, f32[18,64,128]{2,1,0:T(8,128)}, f32[6,64,128]{2,1,0:T(8,128)}, f32[6,64,128]{2,1,0:T(8,128)}, /*index=5*/f32[128,4,128]{2,1,0:T(4,128)}) custom-call(f32[128,1,128]{2,1,0:T(1,128)} %all_to_all.25.recv, f32[18,48,128]{2,1,0:T(8,128)} %get-tuple-element.35.lists, ...), custom_call_target="tpu_custom_call" | custom-call | tf_op jit(solution)/shard_map/body/pallas_call | solution.py:664
  98.4 5.0 %all-to-all-start.3 = ((f32[128,4,128]{2,1,0:T(4,128)}), f32[128,4,128]{2,1,0:T(4,128)}, u32[]{:S(2)}, u32[]{:S(2)}) async-start(f32[128,4,128]{2,1,0:T(4,128)} %get-tuple-element.48), calls=%async_computation.3 | async-start | bytes 524288 | tf_op jit(solution)/shard_map/all_to_all | solution.py:631
  103.4 1.7 %collective-permute-start.9 = (f32[6,64,128]{2,1,0:T(8,128)}, f32[6,64,128]{2,1,0:T(8,128)}, u32[]{:S(2)}, u32[]{:S(2)}) collective-permute-start(f32[6,64,128]{2,1,0:T(8,128)} %get-tuple-element.50), channel_id=1, source_target_pairs={{0,16},{16,0},{32,48},{48,32},{64,80},{80,64},{96,112},{112,96},{1... | collective-permute-start | bytes 589832 | tf_op jit(solution)/shard_map/ppermute | solution.py:635
  105.1 1.3 collective-permute-start.10
  106.5 8.1 %all-to-all-done.3.recv_in = f32[128,4,128]{2,1,0:T(4,128)} async-done(((f32[128,4,128]{2,1,0:T(4,128)}), f32[128,4,128]{2,1,0:T(4,128)}, u32[]{:S(2)}, u32[]{:S(2)}) %all-to-all-start.3) | async-done | bytes 262176 | tf_op jit(solution)/shard_map/all_to_all | solution.py:631
  114.6 3.0 %coarse.1 = f32[128,128]{1,0:T(8,128)} custom-call(s32[2,16]{1,0:T(2,128)} %bitcast.14, f32[128,4,128]{2,1,0:T(4,128)} %all-to-all-done.3.recv_in, f32[16,2,128,128]{3,2,1,0:T(8,128)} %blocks.3, f32[3,128,128]{2,1,0:T(8,128)} %get-tuple-element.47.table_in), custom_call_target="tpu_custom_call" | custom-call | tf_op jit(solution)/shard_map/coarse/pallas_call | solution.py:664
  117.6 5.0 %all-to-all-start.4 = ((f32[128,1,128]{2,1,0:T(1,128)}), f32[128,1,128]{2,1,0:T(1,128)}, u32[]{:S(2)}, u32[]{:S(2)}) async-start(f32[128,1,128]{2,1,0:T(1,128)} %bitcast.12), calls=%async_computation.4 | async-start | bytes 131072 | tf_op jit(solution)/shard_map/all_to_all | solution.py:631
  122.6 9.9 %all-to-all-done.4 = f32[128,1,128]{2,1,0:T(1,128)} async-done(((f32[128,1,128]{2,1,0:T(1,128)}), f32[128,1,128]{2,1,0:T(1,128)}, u32[]{:S(2)}, u32[]{:S(2)}) %all-to-all-start.4) | async-done | bytes 65568 | tf_op jit(solution)/shard_map/all_to_all | solution.py:631
  132.5 6.3 %last.1 = (f32[3,16,48,128]{3,2,1,0:T(8,128)}, f32[16,48,128]{2,1,0:T(8,128)}) custom-call(f32[128,128]{1,0:T(8,128)} %bitcast.9.recv, f32[18,64,128]{2,1,0:T(8,128)} %get-tuple-element.49.corr1_in, f32[16,64,128]{2,1,0:T(8,128)} %get-tuple-element.46.codes_in, f32[6,64,128]{2,1,0:T(8,128)} %collective-permute-done.9.xnear, ...), custom_call_target="tpu_custom_call" | custom-call | tf_op jit(solution)/shard_map/last/pallas_call | solution.py:664
  (11 shorter events, 0.0 us)
Async XLA Ops:
  2.9 25.4 %collective-permute-start.2 = (f32[18,48,128]{2,1,0:T(8,128)}, f32[18,48,128]{2,1,0:T(8,128)}, u32[]{:S(2)}, u32[]{:S(2)}) collective-permute-start(f32[18,48,128]{2,1,0:T(8,128)} %get-tuple-element.36), channel_id=1, source_target_pairs={{16,0},{32,16},{48,32},{64,48},{80,64},{96,80},{112,96},{17,1},{33... | collective-permute-start | bytes 1327112 | tf_op jit(solution)/shard_map/ppermute | solution.py:644
  4.2 24.1 %collective-permute-start.1 = (f32[18,48,128]{2,1,0:T(8,128)}, f32[18,48,128]{2,1,0:T(8,128)}, u32[]{:S(2)}, u32[]{:S(2)}) collective-permute-start(f32[18,48,128]{2,1,0:T(8,128)} %get-tuple-element.35.lists), channel_id=1, source_target_pairs={{0,16},{16,32},{32,48},{48,64},{64,80},{80,96},{96,112},{1,17},{17... | collective-permute-start | bytes 1327112 | tf_op jit(solution)/shard_map/ppermute | solution.py:644
  13.1 2.1 %collective-permute-start = (f32[8,128]{1,0:T(8,128)}, f32[8,128]{1,0:T(8,128)S(1)}, u32[]{:S(2)}, u32[]{:S(2)}) collective-permute-start(f32[8,128]{1,0:T(8,128)} %get-tuple-element.31), channel_id=1, source_target_pairs={{0,1},{1,0},{2,3},{3,2},{4,5},{5,4},{6,7},{7,6},{8,9},{9,8},{10,11... | collective-permute-start | bytes 12296 | tf_op jit(solution)/shard_map/ppermute | solution.py:635
  15.2 0.6 copy-start
  17.3 24.4 %all-to-all-start = ((f32[128,8,128]{2,1,0:T(8,128)}), f32[128,8,128]{2,1,0:T(8,128)}, u32[]{:S(2)}, u32[]{:S(2)}) async-start(f32[128,8,128]{2,1,0:T(8,128)} %join.1.token), calls=%async_computation | async-start | bytes 1048576 | tf_op jit(solution)/shard_map/all_to_all | solution.py:631
  31.4 22.4 %collective-permute-start.3 = (f32[104,8,128]{2,1,0:T(8,128)}, f32[104,8,128]{2,1,0:T(8,128)}, u32[]{:S(2)}, u32[]{:S(2)}) collective-permute-start(f32[104,8,128]{2,1,0:T(8,128)} %get-tuple-element.37), channel_id=1, source_target_pairs={{0,1},{1,0},{2,3},{3,2},{4,5},{5,4},{6,7},{7,6},{8,9},{9,8},{10,11... | collective-permute-start | bytes 1277960 | tf_op jit(solution)/shard_map/ppermute | solution.py:635
  32.6 21.2 %collective-permute-start.4 = (f32[104,8,128]{2,1,0:T(8,128)}, f32[104,8,128]{2,1,0:T(8,128)}, u32[]{:S(2)}, u32[]{:S(2)}) collective-permute-start(f32[104,8,128]{2,1,0:T(8,128)} %get-tuple-element.38), channel_id=1, source_target_pairs={{1,2},{2,1},{3,4},{4,3},{5,6},{6,5},{7,8},{8,7},{9,10},{10,9},{11,... | collective-permute-start | bytes 1277960 | tf_op jit(solution)/shard_map/ppermute | solution.py:640
  35.2 18.6 %collective-permute-start.5 = (f32[96,8,128]{2,1,0:T(8,128)}, f32[96,8,128]{2,1,0:T(8,128)}, u32[]{:S(2)}, u32[]{:S(2)}) collective-permute-start(f32[96,8,128]{2,1,0:T(8,128)} %get-tuple-element.39), channel_id=1, source_target_pairs={{0,1},{1,0},{2,3},{3,2},{4,5},{5,4},{6,7},{7,6},{8,9},{9,8},{10,11... | collective-permute-start | bytes 1179656 | tf_op jit(solution)/shard_map/ppermute | solution.py:635
  35.3 18.5 %collective-permute-start.6 = (f32[96,8,128]{2,1,0:T(8,128)}, f32[96,8,128]{2,1,0:T(8,128)}, u32[]{:S(2)}, u32[]{:S(2)}) collective-permute-start(f32[96,8,128]{2,1,0:T(8,128)} %get-tuple-element.40), channel_id=1, source_target_pairs={{1,2},{2,1},{3,4},{4,3},{5,6},{6,5},{7,8},{8,7},{9,10},{10,9},{11,... | collective-permute-start | bytes 1179656 | tf_op jit(solution)/shard_map/ppermute | solution.py:640
  43.7 21.2 %all-to-all-start.1 = ((f32[128,4,128]{2,1,0:T(4,128)}), f32[128,4,128]{2,1,0:T(4,128)}, u32[]{:S(2)}, u32[]{:S(2)}) async-start(f32[128,4,128]{2,1,0:T(4,128)} %get-tuple-element.32), calls=%async_computation.1 | async-start | bytes 524288 | tf_op jit(solution)/shard_map/all_to_all | solution.py:631
  61.3 27.2 %collective-permute-start.7 = (f32[7,64,128]{2,1,0:T(8,128)}, f32[7,64,128]{2,1,0:T(8,128)}, u32[]{:S(2)}, u32[]{:S(2)}) collective-permute-start(f32[7,64,128]{2,1,0:T(8,128)} %get-tuple-element.41), channel_id=1, source_target_pairs={{0,16},{16,0},{32,48},{48,32},{64,80},{80,64},{96,112},{112,96},{1... | collective-permute-start | bytes 688136 | tf_op jit(solution)/shard_map/ppermute | solution.py:635
  62.9 25.6 %collective-permute-start.8 = (f32[7,64,128]{2,1,0:T(8,128)}, f32[7,64,128]{2,1,0:T(8,128)}, u32[]{:S(2)}, u32[]{:S(2)}) collective-permute-start(f32[7,64,128]{2,1,0:T(8,128)} %get-tuple-element.42), channel_id=1, source_target_pairs={{16,32},{32,16},{48,64},{64,48},{80,96},{96,80},{17,33},{33,17},{4... | collective-permute-start | bytes 688136 | tf_op jit(solution)/shard_map/ppermute | solution.py:640
  98.4 16.2 %all-to-all-start.3 = ((f32[128,4,128]{2,1,0:T(4,128)}), f32[128,4,128]{2,1,0:T(4,128)}, u32[]{:S(2)}, u32[]{:S(2)}) async-start(f32[128,4,128]{2,1,0:T(4,128)} %get-tuple-element.48), calls=%async_computation.3 | async-start | bytes 524288 | tf_op jit(solution)/shard_map/all_to_all | solution.py:631
  103.4 19.2 %collective-permute-start.9 = (f32[6,64,128]{2,1,0:T(8,128)}, f32[6,64,128]{2,1,0:T(8,128)}, u32[]{:S(2)}, u32[]{:S(2)}) collective-permute-start(f32[6,64,128]{2,1,0:T(8,128)} %get-tuple-element.50), channel_id=1, source_target_pairs={{0,16},{16,0},{32,48},{48,32},{64,80},{80,64},{96,112},{112,96},{1... | collective-permute-start | bytes 589832 | tf_op jit(solution)/shard_map/ppermute | solution.py:635
  105.1 17.5 %collective-permute-start.10 = (f32[6,64,128]{2,1,0:T(8,128)}, f32[6,64,128]{2,1,0:T(8,128)}, u32[]{:S(2)}, u32[]{:S(2)}) collective-permute-start(f32[6,64,128]{2,1,0:T(8,128)} %get-tuple-element.51), channel_id=1, source_target_pairs={{16,32},{32,16},{48,64},{64,48},{80,96},{96,80},{17,33},{33,17},{4... | collective-permute-start | bytes 589832 | tf_op jit(solution)/shard_map/ppermute | solution.py:640
  117.6 14.9 %all-to-all-start.4 = ((f32[128,1,128]{2,1,0:T(1,128)}), f32[128,1,128]{2,1,0:T(1,128)}, u32[]{:S(2)}, u32[]{:S(2)}) async-start(f32[128,1,128]{2,1,0:T(1,128)} %bitcast.12), calls=%async_computation.4 | async-start | bytes 131072 | tf_op jit(solution)/shard_map/all_to_all | solution.py:631

commit v6 on v5

--- a/solution.py
+++ b/solution.py
@@ -288,7 +288,7 @@
         codes[x] = widen(ylo[48 + x], (agg[x] - base + 4).astype(F32), yhi[48 + x])
         return carry
 
-    lax.fori_loop(0, CX, grow, 0, unroll=4)
+    lax.fori_loop(0, CX, grow, 0, unroll=8)
 
     copies = run([(invd, invd_out), (invp, invp_out), (codes, codes_out)], sems)
 
@@ -303,7 +303,7 @@
             q[c, i] = (sc + v[c, i] + v[c, i + 2] + s_yz(v[c, i + 1])) * inv
         return carry
 
-    lax.fori_loop(0, CX + 2, first, 0, unroll=3)
+    lax.fori_loop(0, CX + 2, first, 0, unroll=6)
 
     def second(x, carry):
         inv = invd[x + 4]
@@ -337,7 +337,7 @@
         fn(j + w, 1, j)
         return carry
 
-    lax.fori_loop(0, CX, own, 0, unroll=8)
+    lax.fori_loop(0, CX, own, 0, unroll=16)
     for i in range(n - CX - w):
         fn(CX + w + i, 2, i)
 
@@ -452,7 +452,7 @@
         return carry
 
     acc[...] = jnp.zeros(acc.shape, F32)
-    lax.fori_loop(0, CX // 4, s5, 0)
+    lax.fori_loop(0, CX // 4, s5, 0, unroll=4)
     for last, out in ((1 - (hx & 1), near), (hx & 1, far)):
         out[0:3] = corr1[pl.ds(1 + last * (CX - 3), 3)]
         out[3:6] = codes[pl.ds(last * (CX - 3), 3)]

time: 140 us -> 138 us (0.986)
  Pallas kernels: 40.5 us -> 38.4 us
    pallas_call x10, Pallas kernels: 40.5 us -> 38.4 us  [call(): pl.pallas_call(kernel, out_shape=outs, in_specs=ins, out_specs=out_specs,...]
  transfers between devices with their start and end apart: 15 -> 15, of which waited for: 4 -> 5; matrix products, arithmetic and copies ran while one was open for 0% -> 0% of each run, Pallas kernels for 16% -> 16%
where the time goes in v6:
time: 138 us; the launch traced here: 137 us
  starting transfers between devices  52.6 us (38%)
  Pallas kernels  38.4 us (28%)
  waiting for transfers between devices  22.1 us (16%)
  blocking collectives  21.7 us (16%)
  between operations  1.63 us (1%)
    pallas_call x10, Pallas kernels, call(): pl.pallas_call(kernel, out_shape=outs, in_specs=ins, out_specs=out_specs,...  38.4 us
    all_to_all x4, starting transfers between devices, to_all(): return lax.all_to_all(x, BOTH, 0, 0, tiled=True)  31.2 us
    all_to_all x1, blocking collectives, to_all(): return lax.all_to_all(x, BOTH, 0, 0, tiled=True)  21.7 us
    all_to_all x4, waiting for transfers between devices, to_all(): return lax.all_to_all(x, BOTH, 0, 0, tiled=True)  21.1 us
    ppermute x4, starting transfers between devices, across(): lax.ppermute(x, axis, [(i, j) for k in range(1, n - 1, 2) for i, j in ((k...  8.68 us
    ppermute x2, starting transfers between devices, shift(): lax.ppermute(x, 'hullx', [(i, i + by) for i in range(HX) if 0 <= i + by <...  7.08 us
    ppermute x5, starting transfers between devices, pair(): lax.ppermute(x, axis, [(i, i ^ 1) for i in range(HX if axis == 'hullx' el...  5.66 us
  transfers between devices with their start and end apart: 15, of which 5 were waited for; matrix products, arithmetic and copies ran while one was open for 0% of the time, Pallas kernels for 16%

profile of v6, /device:TPU:1, one launch (start us, length us, event | category | flops | bytes accessed | tf_op | source)
XLA Modules:
  0.0 137.1 jit_solution(18214661597925095470)
XLA Ops:
  0.6 2.3 %packx.1 = (f32[18,48,128]{2,1,0:T(8,128)}, f32[18,48,128]{2,1,0:T(8,128)}) custom-call(f32[3,16,48,128]{3,2,1,0:T(8,128)} %vel_in.1, f32[3,16,48,128]{3,2,1,0:T(8,128)} %src_in.1, f32[16,48,128]{2,1,0:T(8,128)} %pres_in.3, f32[16,48,128]{2,1,0:T(8,128)} %mdiag_in.1, f32[16,48,128]{2,1,0:T(8,128)} %pdiag_in.1, s32[4,128]{1,0:T(4,128)} %bitcast.15, ...), custom_call_target="tpu_custom_call" | custom-call | tf_op jit(solution)/shard_map/packx/pallas_call | solution.py:664
  2.9 1.3 collective-permute-start.2
  4.2 5.8 %collective-permute-start.1 = (f32[18,48,128]{2,1,0:T(8,128)}, f32[18,48,128]{2,1,0:T(8,128)}, u32[]{:S(2)}, u32[]{:S(2)}) collective-permute-start(f32[18,48,128]{2,1,0:T(8,128)} %get-tuple-element.35.lists), channel_id=1, source_target_pairs={{0,16},{16,32},{32,48},{48,64},{64,80},{80,96},{96,112},{1,17},{17... | collective-permute-start | bytes 1327112 | tf_op jit(solution)/shard_map/ppermute | solution.py:644
  10.0 3.1 %wake.1 = (f32[8,128]{1,0:T(8,128)}, f32[8,128]{1,0:T(8,128)}) custom-call(s32[2,16]{1,0:T(2,128)} %bitcast.13, f32[8]{0:T(128)} %chord.1, f32[8]{0:T(128)} %radius.1, f32[3,16,48,128]{3,2,1,0:T(8,128)} %vel_in.1, s32[1,256]{1,0:T(1,128)} %bitcast.18, s32[1,256]{1,0:T(1,128)} %bitcast.19, f32[1,256]{1,0:T(1,128)} %bitcast.20, f32[16,2,128,128]{3,2,1,0:T(8,128)} %blocks.3), custom_call_target="tpu_custom_call" | custom-call | tf_op jit(solution)/shard_map/wake/pallas_call | solution.py:664
  13.1 1.0 collective-permute-start
  14.2 1.0 collective-permute-done.got
  15.2 0.6 copy-done
  15.8 1.5 %join.1.token = f32[128,8,128]{2,1,0:T(8,128)} custom-call(f32[8,128]{1,0:T(8,128)} %get-tuple-element.30.keep, f32[8,128]{1,0:T(8,128)} %copy-done), custom_call_target="tpu_custom_call" | custom-call | tf_op jit(solution)/shard_map/join/pallas_call | solution.py:664
  17.3 11.0 %all-to-all-start = ((f32[128,8,128]{2,1,0:T(8,128)}), f32[128,8,128]{2,1,0:T(8,128)}, u32[]{:S(2)}, u32[]{:S(2)}) async-start(f32[128,8,128]{2,1,0:T(8,128)} %join.1.token), calls=%async_computation | async-start | bytes 1048576 | tf_op jit(solution)/shard_map/all_to_all | solution.py:631
  28.4 3.0 %packy.1 = (f32[96,8,128]{2,1,0:T(8,128)}, f32[96,8,128]{2,1,0:T(8,128)}, f32[104,8,128]{2,1,0:T(8,128)}, f32[104,8,128]{2,1,0:T(8,128)}) custom-call(f32[3,16,48,128]{3,2,1,0:T(8,128)} %vel_in.1, f32[3,16,48,128]{3,2,1,0:T(8,128)} %src_in.1, f32[16,48,128]{2,1,0:T(8,128)} %pres_in.3, f32[16,48,128]{2,1,0:T(8,128)} %mdiag_in.1, f32[16,48,128]{2,1,0:T(8,128)} %pdiag_in.1, ...), custom_call_target="tpu_custom_call" | custom-call | tf_op jit(solution)/shard_map/packy/pallas_call | solution.py:664
  31.4 1.2 collective-permute-start.3
  32.6 2.5 %collective-permute-start.4 = (f32[104,8,128]{2,1,0:T(8,128)}, f32[104,8,128]{2,1,0:T(8,128)}, u32[]{:S(2)}, u32[]{:S(2)}) collective-permute-start(f32[104,8,128]{2,1,0:T(8,128)} %get-tuple-element.38), channel_id=1, source_target_pairs={{1,2},{2,1},{3,4},{4,3},{5,6},{6,5},{7,8},{8,7},{9,10},{10,9},{11,... | collective-permute-start | bytes 1277960 | tf_op jit(solution)/shard_map/ppermute | solution.py:640
  35.2 0.1 collective-permute-start.5
  35.3 3.5 %collective-permute-start.6 = (f32[96,8,128]{2,1,0:T(8,128)}, f32[96,8,128]{2,1,0:T(8,128)}, u32[]{:S(2)}, u32[]{:S(2)}) collective-permute-start(f32[96,8,128]{2,1,0:T(8,128)} %get-tuple-element.40), channel_id=1, source_target_pairs={{1,2},{2,1},{3,4},{4,3},{5,6},{6,5},{7,8},{8,7},{9,10},{10,9},{11,... | collective-permute-start | bytes 1179656 | tf_op jit(solution)/shard_map/ppermute | solution.py:640
  38.7 3.0 %all-to-all-done.recv = f32[128,8,128]{2,1,0:T(8,128)} async-done(((f32[128,8,128]{2,1,0:T(8,128)}), f32[128,8,128]{2,1,0:T(8,128)}, u32[]{:S(2)}, u32[]{:S(2)}) %all-to-all-start) | async-done | bytes 524320 | tf_op jit(solution)/shard_map/all_to_all | solution.py:631
  41.7 2.0 %trim1.1 = (f32[128,4,128]{2,1,0:T(4,128)}, f32[3,8,128]{2,1,0:T(8,128)}, f32[3,128,128]{2,1,0:T(8,128)}) custom-call(f32[128,8,128]{2,1,0:T(8,128)} %all-to-all-done.recv, f32[8,1024]{1,0:T(8,128)} %infl.3), custom_call_target="tpu_custom_call" | custom-call | tf_op jit(solution)/shard_map/trim1/pallas_call | solution.py:664
  43.7 10.0 %all-to-all-start.1 = ((f32[128,4,128]{2,1,0:T(4,128)}), f32[128,4,128]{2,1,0:T(4,128)}, u32[]{:S(2)}, u32[]{:S(2)}) async-start(f32[128,4,128]{2,1,0:T(4,128)} %get-tuple-element.32), calls=%async_computation.1 | async-start | bytes 524288 | tf_op jit(solution)/shard_map/all_to_all | solution.py:631
  53.8 7.3 %sweeps.1 = (f32[3,16,64,128]{3,2,1,0:T(8,128)}, f32[24,64,128]{2,1,0:T(8,128)}, f32[20,64,128]{2,1,0:T(8,128)}, f32[16,64,128]{2,1,0:T(8,128)}, f32[7,64,128]{2,1,0:T(8,128)}, /*index=5*/f32[7,64,128]{2,1,0:T(8,128)}) custom-call(f32[3,16,48,128]{3,2,1,0:T(8,128)} %vel_in.1, f32[3,16,48,128]{3,2,1,0:T(8,128)} %src_in.1, f32[16,48,128]{2,1,0:T(8,128)} %pres_in.3, ...), custom_call_target="tpu_custom_call" | custom-call | tf_op jit(solution)/shard_map/sweeps/pallas_call | solution.py:664
  61.1 1.6 %collective-permute-start.7 = (f32[7,64,128]{2,1,0:T(8,128)}, f32[7,64,128]{2,1,0:T(8,128)}, u32[]{:S(2)}, u32[]{:S(2)}) collective-permute-start(f32[7,64,128]{2,1,0:T(8,128)} %get-tuple-element.41), channel_id=1, source_target_pairs={{0,16},{16,0},{32,48},{48,32},{64,80},{80,64},{96,112},{112,96},{1... | collective-permute-start | bytes 688136 | tf_op jit(solution)/shard_map/ppermute | solution.py:635
  62.7 1.3 collective-permute-start.8
  64.7 0.1 all-to-all-done.1.recv
  64.8 1.8 %trim2.1 = (f32[128,1,128]{2,1,0:T(1,128)}, f32[1,8]{1,0:T(1,128)}) custom-call(f32[1]{0:T(128)S(6)} %copy.24.res, f32[128,4,128]{2,1,0:T(4,128)} %all-to-all-done.1.recv, f32[3,8,128]{2,1,0:T(8,128)} %get-tuple-element.33.state.token, f32[8,1024]{1,0:T(8,128)} %infl.3), custom_call_target="tpu_custom_call" | custom-call | tf_op jit(solution)/shard_map/trim2/pallas_call | solution.py:664
  66.6 21.7 %all_to_all.25.recv = f32[128,1,128]{2,1,0:T(1,128)} all-to-all(f32[128,1,128]{2,1,0:T(1,128)} %get-tuple-element.34), channel_id=1, replica_groups=mesh['hullx'=8,'hully'=16] {'hullx','hully'}, dimensions={0} | all-to-all | bytes 131072 | tf_op jit(solution)/shard_map/all_to_all | solution.py:631
  88.3 9.1 %body.1 = (f32[22,64,128]{2,1,0:T(8,128)}, f32[20,64,128]{2,1,0:T(8,128)}, f32[18,64,128]{2,1,0:T(8,128)}, f32[6,64,128]{2,1,0:T(8,128)}, f32[6,64,128]{2,1,0:T(8,128)}, /*index=5*/f32[128,4,128]{2,1,0:T(4,128)}) custom-call(f32[128,1,128]{2,1,0:T(1,128)} %all_to_all.25.recv, f32[18,48,128]{2,1,0:T(8,128)} %get-tuple-element.35.lists, ...), custom_call_target="tpu_custom_call" | custom-call | tf_op jit(solution)/shard_map/body/pallas_call | solution.py:664
  97.4 5.2 %all-to-all-start.3 = ((f32[128,4,128]{2,1,0:T(4,128)}), f32[128,4,128]{2,1,0:T(4,128)}, u32[]{:S(2)}, u32[]{:S(2)}) async-start(f32[128,4,128]{2,1,0:T(4,128)} %get-tuple-element.48), calls=%async_computation.3 | async-start | bytes 524288 | tf_op jit(solution)/shard_map/all_to_all | solution.py:631
  102.6 1.7 %collective-permute-start.9 = (f32[6,64,128]{2,1,0:T(8,128)}, f32[6,64,128]{2,1,0:T(8,128)}, u32[]{:S(2)}, u32[]{:S(2)}) collective-permute-start(f32[6,64,128]{2,1,0:T(8,128)} %get-tuple-element.50), channel_id=1, source_target_pairs={{0,16},{16,0},{32,48},{48,32},{64,80},{80,64},{96,112},{112,96},{1... | collective-permute-start | bytes 589832 | tf_op jit(solution)/shard_map/ppermute | solution.py:635
  104.3 1.3 collective-permute-start.10
  105.6 8.1 %all-to-all-done.3.recv_in = f32[128,4,128]{2,1,0:T(4,128)} async-done(((f32[128,4,128]{2,1,0:T(4,128)}), f32[128,4,128]{2,1,0:T(4,128)}, u32[]{:S(2)}, u32[]{:S(2)}) %all-to-all-start.3) | async-done | bytes 262176 | tf_op jit(solution)/shard_map/all_to_all | solution.py:631
  113.8 3.0 %coarse.1 = f32[128,128]{1,0:T(8,128)} custom-call(s32[2,16]{1,0:T(2,128)} %bitcast.14, f32[128,4,128]{2,1,0:T(4,128)} %all-to-all-done.3.recv_in, f32[16,2,128,128]{3,2,1,0:T(8,128)} %blocks.3, f32[3,128,128]{2,1,0:T(8,128)} %get-tuple-element.47.table_in), custom_call_target="tpu_custom_call" | custom-call | tf_op jit(solution)/shard_map/coarse/pallas_call | solution.py:664
  116.8 5.0 %all-to-all-start.4 = ((f32[128,1,128]{2,1,0:T(1,128)}), f32[128,1,128]{2,1,0:T(1,128)}, u32[]{:S(2)}, u32[]{:S(2)}) async-start(f32[128,1,128]{2,1,0:T(1,128)} %bitcast.12), calls=%async_computation.4 | async-start | bytes 131072 | tf_op jit(solution)/shard_map/all_to_all | solution.py:631
  121.8 9.9 %all-to-all-done.4 = f32[128,1,128]{2,1,0:T(1,128)} async-done(((f32[128,1,128]{2,1,0:T(1,128)}), f32[128,1,128]{2,1,0:T(1,128)}, u32[]{:S(2)}, u32[]{:S(2)}) %all-to-all-start.4) | async-done | bytes 65568 | tf_op jit(solution)/shard_map/all_to_all | solution.py:631
  131.7 5.2 %last.1 = (f32[3,16,48,128]{3,2,1,0:T(8,128)}, f32[16,48,128]{2,1,0:T(8,128)}) custom-call(f32[128,128]{1,0:T(8,128)} %bitcast.9.recv, f32[18,64,128]{2,1,0:T(8,128)} %get-tuple-element.49.corr1_in, f32[16,64,128]{2,1,0:T(8,128)} %get-tuple-element.46.codes_in, f32[6,64,128]{2,1,0:T(8,128)} %collective-permute-done.9.xnear, ...), custom_call_target="tpu_custom_call" | custom-call | tf_op jit(solution)/shard_map/last/pallas_call | solution.py:664
  (11 shorter events, 0.0 us)
Async XLA Ops:
  2.9 25.4 %collective-permute-start.2 = (f32[18,48,128]{2,1,0:T(8,128)}, f32[18,48,128]{2,1,0:T(8,128)}, u32[]{:S(2)}, u32[]{:S(2)}) collective-permute-start(f32[18,48,128]{2,1,0:T(8,128)} %get-tuple-element.36), channel_id=1, source_target_pairs={{16,0},{32,16},{48,32},{64,48},{80,64},{96,80},{112,96},{17,1},{33... | collective-permute-start | bytes 1327112 | tf_op jit(solution)/shard_map/ppermute | solution.py:644
  4.2 24.1 %collective-permute-start.1 = (f32[18,48,128]{2,1,0:T(8,128)}, f32[18,48,128]{2,1,0:T(8,128)}, u32[]{:S(2)}, u32[]{:S(2)}) collective-permute-start(f32[18,48,128]{2,1,0:T(8,128)} %get-tuple-element.35.lists), channel_id=1, source_target_pairs={{0,16},{16,32},{32,48},{48,64},{64,80},{80,96},{96,112},{1,17},{17... | collective-permute-start | bytes 1327112 | tf_op jit(solution)/shard_map/ppermute | solution.py:644
  13.1 2.1 %collective-permute-start = (f32[8,128]{1,0:T(8,128)}, f32[8,128]{1,0:T(8,128)S(1)}, u32[]{:S(2)}, u32[]{:S(2)}) collective-permute-start(f32[8,128]{1,0:T(8,128)} %get-tuple-element.31), channel_id=1, source_target_pairs={{0,1},{1,0},{2,3},{3,2},{4,5},{5,4},{6,7},{7,6},{8,9},{9,8},{10,11... | collective-permute-start | bytes 12296 | tf_op jit(solution)/shard_map/ppermute | solution.py:635
  15.2 0.6 copy-start
  17.3 24.4 %all-to-all-start = ((f32[128,8,128]{2,1,0:T(8,128)}), f32[128,8,128]{2,1,0:T(8,128)}, u32[]{:S(2)}, u32[]{:S(2)}) async-start(f32[128,8,128]{2,1,0:T(8,128)} %join.1.token), calls=%async_computation | async-start | bytes 1048576 | tf_op jit(solution)/shard_map/all_to_all | solution.py:631
  31.4 22.4 %collective-permute-start.3 = (f32[104,8,128]{2,1,0:T(8,128)}, f32[104,8,128]{2,1,0:T(8,128)}, u32[]{:S(2)}, u32[]{:S(2)}) collective-permute-start(f32[104,8,128]{2,1,0:T(8,128)} %get-tuple-element.37), channel_id=1, source_target_pairs={{0,1},{1,0},{2,3},{3,2},{4,5},{5,4},{6,7},{7,6},{8,9},{9,8},{10,11... | collective-permute-start | bytes 1277960 | tf_op jit(solution)/shard_map/ppermute | solution.py:635
  32.6 21.2 %collective-permute-start.4 = (f32[104,8,128]{2,1,0:T(8,128)}, f32[104,8,128]{2,1,0:T(8,128)}, u32[]{:S(2)}, u32[]{:S(2)}) collective-permute-start(f32[104,8,128]{2,1,0:T(8,128)} %get-tuple-element.38), channel_id=1, source_target_pairs={{1,2},{2,1},{3,4},{4,3},{5,6},{6,5},{7,8},{8,7},{9,10},{10,9},{11,... | collective-permute-start | bytes 1277960 | tf_op jit(solution)/shard_map/ppermute | solution.py:640
  35.2 18.6 %collective-permute-start.5 = (f32[96,8,128]{2,1,0:T(8,128)}, f32[96,8,128]{2,1,0:T(8,128)}, u32[]{:S(2)}, u32[]{:S(2)}) collective-permute-start(f32[96,8,128]{2,1,0:T(8,128)} %get-tuple-element.39), channel_id=1, source_target_pairs={{0,1},{1,0},{2,3},{3,2},{4,5},{5,4},{6,7},{7,6},{8,9},{9,8},{10,11... | collective-permute-start | bytes 1179656 | tf_op jit(solution)/shard_map/ppermute | solution.py:635
  35.3 18.5 %collective-permute-start.6 = (f32[96,8,128]{2,1,0:T(8,128)}, f32[96,8,128]{2,1,0:T(8,128)}, u32[]{:S(2)}, u32[]{:S(2)}) collective-permute-start(f32[96,8,128]{2,1,0:T(8,128)} %get-tuple-element.40), channel_id=1, source_target_pairs={{1,2},{2,1},{3,4},{4,3},{5,6},{6,5},{7,8},{8,7},{9,10},{10,9},{11,... | collective-permute-start | bytes 1179656 | tf_op jit(solution)/shard_map/ppermute | solution.py:640
  43.7 21.0 %all-to-all-start.1 = ((f32[128,4,128]{2,1,0:T(4,128)}), f32[128,4,128]{2,1,0:T(4,128)}, u32[]{:S(2)}, u32[]{:S(2)}) async-start(f32[128,4,128]{2,1,0:T(4,128)} %get-tuple-element.32), calls=%async_computation.1 | async-start | bytes 524288 | tf_op jit(solution)/shard_map/all_to_all | solution.py:631
  61.1 27.2 %collective-permute-start.7 = (f32[7,64,128]{2,1,0:T(8,128)}, f32[7,64,128]{2,1,0:T(8,128)}, u32[]{:S(2)}, u32[]{:S(2)}) collective-permute-start(f32[7,64,128]{2,1,0:T(8,128)} %get-tuple-element.41), channel_id=1, source_target_pairs={{0,16},{16,0},{32,48},{48,32},{64,80},{80,64},{96,112},{112,96},{1... | collective-permute-start | bytes 688136 | tf_op jit(solution)/shard_map/ppermute | solution.py:635
  62.7 25.6 %collective-permute-start.8 = (f32[7,64,128]{2,1,0:T(8,128)}, f32[7,64,128]{2,1,0:T(8,128)}, u32[]{:S(2)}, u32[]{:S(2)}) collective-permute-start(f32[7,64,128]{2,1,0:T(8,128)} %get-tuple-element.42), channel_id=1, source_target_pairs={{16,32},{32,16},{48,64},{64,48},{80,96},{96,80},{17,33},{33,17},{4... | collective-permute-start | bytes 688136 | tf_op jit(solution)/shard_map/ppermute | solution.py:640
  97.4 16.4 %all-to-all-start.3 = ((f32[128,4,128]{2,1,0:T(4,128)}), f32[128,4,128]{2,1,0:T(4,128)}, u32[]{:S(2)}, u32[]{:S(2)}) async-start(f32[128,4,128]{2,1,0:T(4,128)} %get-tuple-element.48), calls=%async_computation.3 | async-start | bytes 524288 | tf_op jit(solution)/shard_map/all_to_all | solution.py:631
  102.6 19.2 %collective-permute-start.9 = (f32[6,64,128]{2,1,0:T(8,128)}, f32[6,64,128]{2,1,0:T(8,128)}, u32[]{:S(2)}, u32[]{:S(2)}) collective-permute-start(f32[6,64,128]{2,1,0:T(8,128)} %get-tuple-element.50), channel_id=1, source_target_pairs={{0,16},{16,0},{32,48},{48,32},{64,80},{80,64},{96,112},{112,96},{1... | collective-permute-start | bytes 589832 | tf_op jit(solution)/shard_map/ppermute | solution.py:635
  104.3 17.5 %collective-permute-start.10 = (f32[6,64,128]{2,1,0:T(8,128)}, f32[6,64,128]{2,1,0:T(8,128)}, u32[]{:S(2)}, u32[]{:S(2)}) collective-permute-start(f32[6,64,128]{2,1,0:T(8,128)} %get-tuple-element.51), channel_id=1, source_target_pairs={{16,32},{32,16},{48,64},{64,48},{80,96},{96,80},{17,33},{33,17},{4... | collective-permute-start | bytes 589832 | tf_op jit(solution)/shard_map/ppermute | solution.py:640
  116.8 14.9 %all-to-all-start.4 = ((f32[128,1,128]{2,1,0:T(1,128)}), f32[128,1,128]{2,1,0:T(1,128)}, u32[]{:S(2)}, u32[]{:S(2)}) async-start(f32[128,1,128]{2,1,0:T(1,128)} %bitcast.12), calls=%async_computation.4 | async-start | bytes 131072 | tf_op jit(solution)/shard_map/all_to_all | solution.py:631
